TPU v7x, 512 devices: a whole 4x4x16 slice. The times are simulated.
512 devices in a mesh: row: 16 (over y_hi, x, core), col: 32 (over z, y_lo).
Axes of the slice: x: 4, y: 4 (y_hi: 2, y_lo: 2; y = y_hi * 2 + y_lo), z: 16, core: 2. Of those that a mesh axis runs over, the one named last changes fastest.
Arguments:
- section_a: bfloat16 [256, 1024, 256], P('row', 'col'), may hold values from -16 to 16
- section_b: bfloat16 [256, 1024, 256], P('row', 'col'), may hold values from -16 to 16
- ln_gain: float32 [256], replicated, may hold values from 0.5 to 1.5
- ln_shift: float32 [256], replicated, may hold values from -3 to 3
- w_qkv: bfloat16 [256, 768], replicated, may hold values from -0.375 to 0.375
- b_qkv: float32 [768], replicated, may hold values from -3 to 3
- rel_table: float32 [8, 225], replicated, may hold values from -4 to 4
- w_out: bfloat16 [256, 256], replicated, may hold values from -0.375 to 0.375
- b_out: float32 [256], replicated, may hold values from -3 to 3
- w_hid: bfloat16 [289, 256], replicated, may hold values from -0.375 to 0.375
- b_hid: float32 [256], replicated, may hold values from -3 to 3
- w_flow: bfloat16 [256, 2], replicated, may hold values from -0.375 to 0.375
- b_flow: float32 [2], replicated, may hold values from -3 to 3
Outputs:
- flow: float32 [2, 256, 1024], P(None, 'row', 'col')
All inputs are finite; a program needn't handle non-finite values.
Results may differ from a plain program's by a relative error of at most 0.04.
Values may be sent and summed in bfloat16 or wider, within the bound.
No kernel may reach another device: no remote copies, remote signals or barrier semaphores. Data moves between devices by JAX's collectives and lax.ppermute only.
A program may use at most 64 MiB of HBM per device.

v0:
```python
import jax
import jax.numpy as jnp
import numpy as np
from jax import lax
from jax.sharding import PartitionSpec as P

C = 256
HEADS = 8
HEAD = 32
WIN = 8
SHIFT = 4
RADIUS = 8
OFFS = 289


def shifted(array, axis, by):
    peers = lax.axis_size(axis)
    return lax.ppermute(array, axis, [(i, (i + by) % peers) for i in range(peers)])


def with_halo(cells, sides, width):
    for axis, dim in sides:
        count = lax.axis_size(axis)
        ends = count - 1
        head = lax.slice_in_dim(cells, 0, width, axis=dim)
        tail = lax.slice_in_dim(cells, cells.shape[dim] - width, cells.shape[dim], axis=dim)
        cells = jnp.concatenate(
            [
                lax.ppermute(tail, axis, [(i, (i + 1) % count) for i in range(ends)]),
                cells,
                lax.ppermute(head, axis, [((i + 1) % count, i) for i in range(ends)]),
            ],
            axis=dim,
        )
    return cells


def relative_index():
    places = np.arange(WIN)
    grid_rows, grid_cols = np.meshgrid(places, places, indexing="ij")
    flat_rows = grid_rows.reshape(-1)
    flat_cols = grid_cols.reshape(-1)
    rel_rows = flat_rows[:, None] - flat_rows[None, :] + WIN - 1
    rel_cols = flat_cols[:, None] - flat_cols[None, :] + WIN - 1
    return rel_rows * (2 * WIN - 1) + rel_cols


def layer_norm(features, ln_gain, ln_shift):
    values = features.astype(jnp.float32)
    average = jnp.mean(values, axis=-1, keepdims=True)
    centred = values - average
    variance = jnp.mean(centred * centred, axis=-1, keepdims=True)
    return (centred * lax.rsqrt(variance + 1e-05) * ln_gain + ln_shift).astype(jnp.bfloat16)


def labels_of(row_places, col_places, total_rows, total_cols):
    row_label = (row_places >= total_rows - WIN).astype(jnp.int32) + (
        row_places >= total_rows - SHIFT
    ).astype(jnp.int32)
    col_label = (col_places >= total_cols - WIN).astype(jnp.int32) + (
        col_places >= total_cols - SHIFT
    ).astype(jnp.int32)
    return row_label[:, None] * 3 + col_label[None, :]


def attend(rolled, labels, w_qkv, b_qkv, position_bias, w_out, b_out):
    height, width = (rolled.shape[0], rolled.shape[1])
    high, wide = (height // WIN, width // WIN)
    windows = rolled.reshape(high, WIN, wide, WIN, C).transpose(0, 2, 1, 3, 4).reshape(-1, C)
    win_labels = (
        labels.reshape(high, WIN, wide, WIN).transpose(0, 2, 1, 3).reshape(high * wide, WIN * WIN)
    )
    qkv = (jnp.dot(windows, w_qkv, preferred_element_type=jnp.float32) + b_qkv).astype(jnp.bfloat16)
    qkv = qkv.reshape(high * wide, WIN * WIN, 3, HEADS, HEAD)
    masking = jnp.where(win_labels[:, :, None] == win_labels[:, None, :], 0.0, -100.0).astype(
        jnp.float32
    )
    scores = jnp.einsum(
        "gqhd,gkhd->ghqk", qkv[:, :, 0], qkv[:, :, 1], preferred_element_type=jnp.float32
    ) * HEAD ** (-0.5)
    scores = scores + position_bias[None] + masking[:, None]
    weights = jax.nn.softmax(scores, axis=-1).astype(jnp.bfloat16)
    mixed = jnp.einsum(
        "ghqk,gkhd->gqhd", weights, qkv[:, :, 2], preferred_element_type=jnp.float32
    ).astype(jnp.bfloat16)
    mixed = mixed.reshape(-1, C)
    attended = (jnp.dot(mixed, w_out, preferred_element_type=jnp.float32) + b_out).astype(
        jnp.bfloat16
    )
    return (
        attended.reshape(high, wide, WIN, WIN, C).transpose(0, 2, 1, 3, 4).reshape(height, width, C)
    )


def flow_head(corr, w_hid, b_hid, w_flow, b_flow):
    probability = jax.nn.softmax(corr, axis=-1)
    offsets = jnp.arange(OFFS, dtype=jnp.int32)
    disp_rows = (offsets // (2 * RADIUS + 1) - RADIUS).astype(jnp.float32)
    disp_cols = (offsets % (2 * RADIUS + 1) - RADIUS).astype(jnp.float32)
    expected = jnp.stack(
        [jnp.sum(probability * disp_rows, axis=-1), jnp.sum(probability * disp_cols, axis=-1)],
        axis=-1,
    )
    scaled = (probability * OFFS).astype(jnp.bfloat16)
    lead = scaled.shape[:-1]
    hidden = jax.nn.gelu(
        jnp.dot(scaled.reshape(-1, OFFS), w_hid, preferred_element_type=jnp.float32) + b_hid
    ).astype(jnp.bfloat16)
    regressed = jnp.dot(hidden, w_flow, preferred_element_type=jnp.float32) + b_flow
    return expected + regressed.reshape(lead + (2,))


def correlate(feature_a, padded):
    height, width = (feature_a.shape[0], feature_a.shape[1])
    reach_span = 2 * RADIUS + 1

    def one_row_offset(row_off):
        reach = lax.dynamic_slice_in_dim(padded, row_off, height, 0)
        parts = [
            jnp.einsum(
                "yxc,yxc->yx",
                feature_a,
                reach[:, col_off : col_off + width],
                preferred_element_type=jnp.float32,
            )
            for col_off in range(reach_span)
        ]
        return jnp.stack(parts, axis=-1)

    volume = lax.map(one_row_offset, jnp.arange(reach_span, dtype=jnp.int32))
    return jnp.transpose(volume, (1, 2, 0, 3)).reshape(height, width, OFFS) * C ** (-0.5)


def unroll_both(out_a, out_b):
    strips = shifted((out_a[:, -SHIFT:], out_b[:, -SHIFT:]), "col", 1)
    wider_a = jnp.concatenate([strips[0], out_a[:, :-SHIFT]], axis=1)
    wider_b = jnp.concatenate([strips[1], out_b[:, :-SHIFT]], axis=1)
    strips = shifted((wider_a[-SHIFT:], wider_b[-SHIFT:]), "row", 1)
    back_a = jnp.concatenate([strips[0], wider_a[:-SHIFT]], axis=0)
    back_b = jnp.concatenate([strips[1], wider_b[:-SHIFT]], axis=0)
    return (back_a, back_b)


def add_features(section, attended):
    return (section.astype(jnp.float32) + attended.astype(jnp.float32)).astype(jnp.bfloat16)


def shards(
    section_a,
    section_b,
    ln_gain,
    ln_shift,
    w_qkv,
    b_qkv,
    rel_table,
    w_out,
    b_out,
    w_hid,
    b_hid,
    w_flow,
    b_flow,
):
    tile_rows, tile_cols = (section_a.shape[0], section_a.shape[1])
    total_rows = tile_rows * lax.axis_size("row")
    total_cols = tile_cols * lax.axis_size("col")
    row_start = lax.axis_index("row") * tile_rows
    col_start = lax.axis_index("col") * tile_cols
    normed_a = layer_norm(section_a, ln_gain, ln_shift)
    normed_b = layer_norm(section_b, ln_gain, ln_shift)
    strips = shifted((normed_a[:SHIFT], normed_b[:SHIFT]), "row", -1)
    taller_a = jnp.concatenate([normed_a[SHIFT:], strips[0]], axis=0)
    taller_b = jnp.concatenate([normed_b[SHIFT:], strips[1]], axis=0)
    strips = shifted((taller_a[:, :SHIFT], taller_b[:, :SHIFT]), "col", -1)
    rolled_a = jnp.concatenate([taller_a[:, SHIFT:], strips[0]], axis=1)
    rolled_b = jnp.concatenate([taller_b[:, SHIFT:], strips[1]], axis=1)
    row_places = row_start + jnp.arange(tile_rows, dtype=jnp.int32)
    col_places = col_start + jnp.arange(tile_cols, dtype=jnp.int32)
    labels = labels_of(row_places, col_places, total_rows, total_cols)
    position_bias = rel_table[:, relative_index()]
    out_a = attend(rolled_a, labels, w_qkv, b_qkv, position_bias, w_out, b_out)
    out_b = attend(rolled_b, labels, w_qkv, b_qkv, position_bias, w_out, b_out)
    back_a, back_b = unroll_both(out_a, out_b)
    feature_a = add_features(section_a, back_a)
    feature_b = add_features(section_b, back_b)
    padded = with_halo(feature_b, (("row", 0), ("col", 1)), RADIUS)
    corr = correlate(feature_a, padded)
    flows = flow_head(corr, w_hid, b_hid, w_flow, b_flow)
    return jnp.transpose(flows, (2, 0, 1))


def solution(mesh):
    placed = (
        P("row", "col", None),
        P("row", "col", None),
        P(),
        P(),
        P(),
        P(),
        P(),
        P(),
        P(),
        P(),
        P(),
        P(),
        P(),
    )
    return jax.shard_map(
        shards, mesh=mesh, in_specs=placed, out_specs=P(None, "row", "col"), check_vma=False
    )
```

profile of v0, /device:TPU:7, one launch (start us, length us, event | category | flops | bytes accessed | tf_op | source)
XLA Modules:
  0.0 200.9 jit_solution(7782055570027161816)
XLA Ops:
  6.1 2.6 %collective-permute-start.8 = (bf16[4,32,256]{2,1,0:T(8,128)(2,1)S(1)}, bf16[4,32,256]{2,1,0:T(8,128)(2,1)S(1)}, u32[]{:S(2)}, u32[]{:S(2)}) collective-permute-start(bf16[4,32,256]{2,1,0:T(8,128)(2,1)S(1)} %slice.169), channel_id=1, source_target_pairs={{0,480},{32,0},{64,32},{96,64},{128,96},{160,128},{192,160},{224,1... | collective-permute-start | bytes 196616 | tf_op jit(solution)/shard_map/ppermute | solution.py:18
  8.8 2.2 %collective-permute-start = (bf16[4,32,256]{2,1,0:T(8,128)(2,1)S(1)}, bf16[4,32,256]{2,1,0:T(8,128)(2,1)S(1)}, u32[]{:S(2)}, u32[]{:S(2)}) collective-permute-start(bf16[4,32,256]{2,1,0:T(8,128)(2,1)S(1)} %slice.158), channel_id=1, source_target_pairs={{0,480},{32,0},{64,32},{96,64},{128,96},{160,128},{192,160},{224,1... | collective-permute-start | bytes 196616 | tf_op jit(solution)/shard_map/ppermute | solution.py:18
  12.1 10.8 %gather_fusion = f32[4096,8]{1,0:T(8,128)S(1)} fusion(f32[8,225]{0,1:T(8,128)S(1)} %copy.49, s32[4096]{0:T(1024)S(1)} %broadcast_clamp_fusion), kind=kCustom, calls=%fused_computation | custom fusion | bytes 278528 | tf_op jit(solution)/shard_map/gather | solution.py:179
  24.8 12.1 %collective-permute-start.9 = (bf16[16,4,256]{2,1,0:T(4,128)(2,1)S(1)}, bf16[16,4,256]{2,1,0:T(4,128)(2,1)S(1)}, u32[]{:S(2)}, u32[]{:S(2)}) collective-permute-start(bf16[16,4,256]{2,1,0:T(4,128)(2,1)S(1)} %pad_maximum_fusion.10), channel_id=1, source_target_pairs={{0,31},{1,0},{2,1},{3,2},{4,3},{5,4},{6,5},{7,6},{8,7},{9,8},{10,9... | collective-permute-start | bytes 98312 | tf_op jit(solution)/shard_map/ppermute | solution.py:18
  37.0 2.1 %collective-permute-start.1 = (bf16[16,4,256]{2,1,0:T(4,128)(2,1)S(1)}, bf16[16,4,256]{2,1,0:T(4,128)(2,1)S(1)}, u32[]{:S(2)}, u32[]{:S(2)}) collective-permute-start(bf16[16,4,256]{2,1,0:T(4,128)(2,1)S(1)} %pad_maximum_fusion.11), channel_id=1, source_target_pairs={{0,31},{1,0},{2,1},{3,2},{4,3},{5,4},{6,5},{7,6},{8,7},{9,8},{10,9... | collective-permute-start | bytes 98312 | tf_op jit(solution)/shard_map/ppermute | solution.py:18
  43.8 3.4 %fusion.96 = (f32[8,8,64]{2,1,0:T(8,128)S(1)}, f32[8,8,64,64]{2,3,1,0:T(8,128)}) fusion(f32[8,64,64]{1,2,0:T(8,128)} %compare_select_fusion, f32[8,64,64]{1,2,0:T(8,128)} %bitcast.202, bf16[8,64,1,8,32]{1,0,4,3,2:T(8,128)(2,1)S(1)} %get-tuple-element.67, bf16[8,64,1,8,32]{1,0,4,3,2:T(8,128)(2,1)S(1)} %get-tuple-element.66), kind=kOutput, calls=%fused_computation.190 | convolution fusion | flops 18088000 | bytes 1851392 | tf_op jit(solution)/shard_map/sub | solution.py:82
  47.2 2.0 %fusion.23 = bf16[8,64,8,32]{1,3,2,0:T(8,128)(2,1)S(1)} fusion(f32[8,8,64,64]{2,3,1,0:T(8,128)} %get-tuple-element.75, f32[8,8,64]{2,1,0:T(8,128)S(1)} %get-tuple-element.74, bf16[8,64,1,8,32]{1,0,4,3,2:T(8,128)(2,1)S(1)} %get-tuple-element.65), kind=kOutput, calls=%fused_computation.73 | convolution fusion | flops 17432576 | bytes 1589248 | tf_op jit(solution)/shard_map/ghqk,gkhd->gqhd/dot_general | solution.py:83
  50.3 3.2 %collective-permute-start.2 = (bf16[16,4,256]{2,1,0:T(4,128)(2,1)S(1)}, bf16[16,4,256]{2,1,0:T(4,128)(2,1)S(1)}, u32[]{:S(2)}, u32[]{:S(2)}) collective-permute-start(bf16[16,4,256]{2,1,0:T(4,128)(2,1)S(1)} %slice.164), channel_id=1, source_target_pairs={{0,1},{1,2},{2,3},{3,4},{4,5},{5,6},{6,7},{7,8},{8,9},{9,10},{10,1... | collective-permute-start | bytes 98312 | tf_op jit(solution)/shard_map/ppermute | solution.py:18
  53.5 2.4 %fusion.97 = (f32[8,8,64]{2,1,0:T(8,128)S(1)}, f32[8,8,64,64]{2,3,1,0:T(8,128)}) fusion(f32[8,64,64]{1,2,0:T(8,128)S(1)} %copy-done.8, f32[8,64,64]{1,2,0:T(8,128)S(1)} %bitcast.203, bf16[8,64,1,8,32]{1,0,4,3,2:T(8,128)(2,1)S(1)} %copy-done.6, bf16[8,64,1,8,32]{1,0,4,3,2:T(8,128)(2,1)S(1)} %copy-done.5), kind=kOutput, calls=%fused_computation.191 | convolution fusion | flops 18088000 | bytes 1851392 | tf_op jit(solution)/shard_map/sub | solution.py:82
  58.7 8.6 %collective-permute-start.3 = (bf16[4,32,256]{2,1,0:T(8,128)(2,1)S(1)}, bf16[4,32,256]{2,1,0:T(8,128)(2,1)S(1)}, u32[]{:S(2)}, u32[]{:S(2)}) collective-permute-start(bf16[4,32,256]{2,1,0:T(8,128)(2,1)S(1)} %pad_maximum_fusion.9), channel_id=1, source_target_pairs={{0,32},{32,64},{64,96},{96,128},{128,160},{160,192},{192,224},{224... | collective-permute-start | bytes 196616 | tf_op jit(solution)/shard_map/ppermute | solution.py:18
  71.8 6.4 %collective-permute-start.4 = (bf16[8,32,256]{2,1,0:T(8,128)(2,1)}, bf16[8,32,256]{2,1,0:T(8,128)(2,1)}, u32[]{:S(2)}, u32[]{:S(2)}) collective-permute-start(bf16[8,32,256]{2,1,0:T(8,128)(2,1)} %get-tuple-element.70), channel_id=1, source_target_pairs={{0,32},{32,64},{64,96},{96,128},{128,160},{160,192},{192,224},{224... | collective-permute-start | bytes 393224 | tf_op jit(solution)/shard_map/ppermute | solution.py:29
  81.5 7.3 %collective-permute-start.11 = (bf16[4,32,256]{2,1,0:T(8,128)(2,1)S(1)}, bf16[4,32,256]{2,1,0:T(8,128)(2,1)S(1)}, u32[]{:S(2)}, u32[]{:S(2)}) collective-permute-start(bf16[4,32,256]{2,1,0:T(8,128)(2,1)S(1)} %pad_maximum_fusion.8), channel_id=1, source_target_pairs={{0,32},{32,64},{64,96},{96,128},{128,160},{160,192},{192,224},{224... | collective-permute-start | bytes 196616 | tf_op jit(solution)/shard_map/ppermute | solution.py:18
  93.9 2.7 %collective-permute-done.7 = bf16[32,8,256]{2,1,0:T(8,128)(2,1)S(1)} collective-permute-done((bf16[32,8,256]{2,1,0:T(8,128)(2,1)S(1)}, bf16[32,8,256]{2,1,0:T(8,128)(2,1)S(1)}, u32[]{:S(2)}, u32[]{:S(2)}) %collective-permute-start.7) | collective-permute-done | bytes 131104 | tf_op jit(solution)/shard_map/ppermute | solution.py:31
  97.7 94.8 %while.10 = (s32[]{:T(128)}, f32[17,16,32,17]{2,1,3,0:T(8,128)S(1)}, s32[17]{0:T(128)S(1)}, bf16[32,48,256]{2,1,0:T(8,128)(2,1)S(1)}, bf16[16,32,256]{2,1,0:T(8,...) while((s32[]{:T(128)}, ...), condition=%wide.region_9.10_spmd, body=%wide.region_8.9_spmd.sunk | while | flops 6807061 | bytes 5304843 | solution.py:130
  100.2 2.8 %fusion.109 = (f32[16,32]{1,0:T(8,128)S(1)}, f32[16,32]{1,0:T(8,128)S(1)}, f32[16,32]{1,0:T(8,128)S(1)}, f32[16,32]{1,0:T(8,128)S(1)}, f32[16,32]{1,0:T(8,128)S(...) fusion(bf16[16,32,256]{2,1,0:T(8,128)(2,1)} %get-tuple-element., ...), kind=kLoop, calls=%fused_computation.34.clone.1 | loop fusion | flops 6807040 | bytes 4753476 | tf_op jit(solution)/shard_map/while/body/eval_jaxpr/yxc,yxc->yx/dot_general | solution.py:120
  105.8 2.8 %fusion.109 = (f32[16,32]{1,0:T(8,128)S(1)}, f32[16,32]{1,0:T(8,128)S(1)}, f32[16,32]{1,0:T(8,128)S(1)}, f32[16,32]{1,0:T(8,128)S(1)}, f32[16,32]{1,0:T(8,128)S(...) fusion(bf16[16,32,256]{2,1,0:T(8,128)(2,1)} %get-tuple-element., ...), kind=kLoop, calls=%fused_computation.34.clone.1 | loop fusion | flops 6807040 | bytes 4753476 | tf_op jit(solution)/shard_map/while/body/eval_jaxpr/yxc,yxc->yx/dot_general | solution.py:120
  111.4 2.8 %fusion.109 = (f32[16,32]{1,0:T(8,128)S(1)}, f32[16,32]{1,0:T(8,128)S(1)}, f32[16,32]{1,0:T(8,128)S(1)}, f32[16,32]{1,0:T(8,128)S(1)}, f32[16,32]{1,0:T(8,128)S(...) fusion(bf16[16,32,256]{2,1,0:T(8,128)(2,1)} %get-tuple-element., ...), kind=kLoop, calls=%fused_computation.34.clone.1 | loop fusion | flops 6807040 | bytes 4753476 | tf_op jit(solution)/shard_map/while/body/eval_jaxpr/yxc,yxc->yx/dot_general | solution.py:120
  117.0 2.8 %fusion.109 = (f32[16,32]{1,0:T(8,128)S(1)}, f32[16,32]{1,0:T(8,128)S(1)}, f32[16,32]{1,0:T(8,128)S(1)}, f32[16,32]{1,0:T(8,128)S(1)}, f32[16,32]{1,0:T(8,128)S(...) fusion(bf16[16,32,256]{2,1,0:T(8,128)(2,1)} %get-tuple-element., ...), kind=kLoop, calls=%fused_computation.34.clone.1 | loop fusion | flops 6807040 | bytes 4753476 | tf_op jit(solution)/shard_map/while/body/eval_jaxpr/yxc,yxc->yx/dot_general | solution.py:120
  122.5 2.8 %fusion.109 = (f32[16,32]{1,0:T(8,128)S(1)}, f32[16,32]{1,0:T(8,128)S(1)}, f32[16,32]{1,0:T(8,128)S(1)}, f32[16,32]{1,0:T(8,128)S(1)}, f32[16,32]{1,0:T(8,128)S(...) fusion(bf16[16,32,256]{2,1,0:T(8,128)(2,1)} %get-tuple-element., ...), kind=kLoop, calls=%fused_computation.34.clone.1 | loop fusion | flops 6807040 | bytes 4753476 | tf_op jit(solution)/shard_map/while/body/eval_jaxpr/yxc,yxc->yx/dot_general | solution.py:120
  128.1 2.8 %fusion.109 = (f32[16,32]{1,0:T(8,128)S(1)}, f32[16,32]{1,0:T(8,128)S(1)}, f32[16,32]{1,0:T(8,128)S(1)}, f32[16,32]{1,0:T(8,128)S(1)}, f32[16,32]{1,0:T(8,128)S(...) fusion(bf16[16,32,256]{2,1,0:T(8,128)(2,1)} %get-tuple-element., ...), kind=kLoop, calls=%fused_computation.34.clone.1 | loop fusion | flops 6807040 | bytes 4753476 | tf_op jit(solution)/shard_map/while/body/eval_jaxpr/yxc,yxc->yx/dot_general | solution.py:120
  133.7 2.8 %fusion.109 = (f32[16,32]{1,0:T(8,128)S(1)}, f32[16,32]{1,0:T(8,128)S(1)}, f32[16,32]{1,0:T(8,128)S(1)}, f32[16,32]{1,0:T(8,128)S(1)}, f32[16,32]{1,0:T(8,128)S(...) fusion(bf16[16,32,256]{2,1,0:T(8,128)(2,1)} %get-tuple-element., ...), kind=kLoop, calls=%fused_computation.34.clone.1 | loop fusion | flops 6807040 | bytes 4753476 | tf_op jit(solution)/shard_map/while/body/eval_jaxpr/yxc,yxc->yx/dot_general | solution.py:120
  139.3 2.8 %fusion.109 = (f32[16,32]{1,0:T(8,128)S(1)}, f32[16,32]{1,0:T(8,128)S(1)}, f32[16,32]{1,0:T(8,128)S(1)}, f32[16,32]{1,0:T(8,128)S(1)}, f32[16,32]{1,0:T(8,128)S(...) fusion(bf16[16,32,256]{2,1,0:T(8,128)(2,1)} %get-tuple-element., ...), kind=kLoop, calls=%fused_computation.34.clone.1 | loop fusion | flops 6807040 | bytes 4753476 | tf_op jit(solution)/shard_map/while/body/eval_jaxpr/yxc,yxc->yx/dot_general | solution.py:120
  144.8 2.8 %fusion.109 = (f32[16,32]{1,0:T(8,128)S(1)}, f32[16,32]{1,0:T(8,128)S(1)}, f32[16,32]{1,0:T(8,128)S(1)}, f32[16,32]{1,0:T(8,128)S(1)}, f32[16,32]{1,0:T(8,128)S(...) fusion(bf16[16,32,256]{2,1,0:T(8,128)(2,1)} %get-tuple-element., ...), kind=kLoop, calls=%fused_computation.34.clone.1 | loop fusion | flops 6807040 | bytes 4753476 | tf_op jit(solution)/shard_map/while/body/eval_jaxpr/yxc,yxc->yx/dot_general | solution.py:120
  150.4 2.8 %fusion.109 = (f32[16,32]{1,0:T(8,128)S(1)}, f32[16,32]{1,0:T(8,128)S(1)}, f32[16,32]{1,0:T(8,128)S(1)}, f32[16,32]{1,0:T(8,128)S(1)}, f32[16,32]{1,0:T(8,128)S(...) fusion(bf16[16,32,256]{2,1,0:T(8,128)(2,1)} %get-tuple-element., ...), kind=kLoop, calls=%fused_computation.34.clone.1 | loop fusion | flops 6807040 | bytes 4753476 | tf_op jit(solution)/shard_map/while/body/eval_jaxpr/yxc,yxc->yx/dot_general | solution.py:120
  156.0 2.8 %fusion.109 = (f32[16,32]{1,0:T(8,128)S(1)}, f32[16,32]{1,0:T(8,128)S(1)}, f32[16,32]{1,0:T(8,128)S(1)}, f32[16,32]{1,0:T(8,128)S(1)}, f32[16,32]{1,0:T(8,128)S(...) fusion(bf16[16,32,256]{2,1,0:T(8,128)(2,1)} %get-tuple-element., ...), kind=kLoop, calls=%fused_computation.34.clone.1 | loop fusion | flops 6807040 | bytes 4753476 | tf_op jit(solution)/shard_map/while/body/eval_jaxpr/yxc,yxc->yx/dot_general | solution.py:120
  161.6 2.8 %fusion.109 = (f32[16,32]{1,0:T(8,128)S(1)}, f32[16,32]{1,0:T(8,128)S(1)}, f32[16,32]{1,0:T(8,128)S(1)}, f32[16,32]{1,0:T(8,128)S(1)}, f32[16,32]{1,0:T(8,128)S(...) fusion(bf16[16,32,256]{2,1,0:T(8,128)(2,1)} %get-tuple-element., ...), kind=kLoop, calls=%fused_computation.34.clone.1 | loop fusion | flops 6807040 | bytes 4753476 | tf_op jit(solution)/shard_map/while/body/eval_jaxpr/yxc,yxc->yx/dot_general | solution.py:120
  167.1 2.8 %fusion.109 = (f32[16,32]{1,0:T(8,128)S(1)}, f32[16,32]{1,0:T(8,128)S(1)}, f32[16,32]{1,0:T(8,128)S(1)}, f32[16,32]{1,0:T(8,128)S(1)}, f32[16,32]{1,0:T(8,128)S(...) fusion(bf16[16,32,256]{2,1,0:T(8,128)(2,1)} %get-tuple-element., ...), kind=kLoop, calls=%fused_computation.34.clone.1 | loop fusion | flops 6807040 | bytes 4753476 | tf_op jit(solution)/shard_map/while/body/eval_jaxpr/yxc,yxc->yx/dot_general | solution.py:120
  172.7 2.8 %fusion.109 = (f32[16,32]{1,0:T(8,128)S(1)}, f32[16,32]{1,0:T(8,128)S(1)}, f32[16,32]{1,0:T(8,128)S(1)}, f32[16,32]{1,0:T(8,128)S(1)}, f32[16,32]{1,0:T(8,128)S(...) fusion(bf16[16,32,256]{2,1,0:T(8,128)(2,1)} %get-tuple-element., ...), kind=kLoop, calls=%fused_computation.34.clone.1 | loop fusion | flops 6807040 | bytes 4753476 | tf_op jit(solution)/shard_map/while/body/eval_jaxpr/yxc,yxc->yx/dot_general | solution.py:120
  178.3 2.8 %fusion.109 = (f32[16,32]{1,0:T(8,128)S(1)}, f32[16,32]{1,0:T(8,128)S(1)}, f32[16,32]{1,0:T(8,128)S(1)}, f32[16,32]{1,0:T(8,128)S(1)}, f32[16,32]{1,0:T(8,128)S(...) fusion(bf16[16,32,256]{2,1,0:T(8,128)(2,1)} %get-tuple-element., ...), kind=kLoop, calls=%fused_computation.34.clone.1 | loop fusion | flops 6807040 | bytes 4753476 | tf_op jit(solution)/shard_map/while/body/eval_jaxpr/yxc,yxc->yx/dot_general | solution.py:120
  183.9 2.8 %fusion.109 = (f32[16,32]{1,0:T(8,128)S(1)}, f32[16,32]{1,0:T(8,128)S(1)}, f32[16,32]{1,0:T(8,128)S(1)}, f32[16,32]{1,0:T(8,128)S(1)}, f32[16,32]{1,0:T(8,128)S(...) fusion(bf16[16,32,256]{2,1,0:T(8,128)(2,1)} %get-tuple-element., ...), kind=kLoop, calls=%fused_computation.34.clone.1 | loop fusion | flops 6807040 | bytes 4753476 | tf_op jit(solution)/shard_map/while/body/eval_jaxpr/yxc,yxc->yx/dot_general | solution.py:120
  189.4 2.8 %fusion.109 = (f32[16,32]{1,0:T(8,128)S(1)}, f32[16,32]{1,0:T(8,128)S(1)}, f32[16,32]{1,0:T(8,128)S(1)}, f32[16,32]{1,0:T(8,128)S(1)}, f32[16,32]{1,0:T(8,128)S(...) fusion(bf16[16,32,256]{2,1,0:T(8,128)(2,1)} %get-tuple-element., ...), kind=kLoop, calls=%fused_computation.34.clone.1 | loop fusion | flops 6807040 | bytes 4753476 | tf_op jit(solution)/shard_map/while/body/eval_jaxpr/yxc,yxc->yx/dot_general | solution.py:120
  195.1 2.4 %mul.141 = f32[512,289]{0,1:T(8,128)S(1)} reshape(f32[16,32,17,17]{1,0,3,2:T(8,128)} %multiply_bitcast_fusion) | data formatting | bytes 1183744 | tf_op jit(solution)/shard_map/mul | solution.py:131
  (444 shorter events, 49.4 us)
Async XLA Ops:
  0.0 39.3 %copy-start = (bf16[256,768]{1,0:T(8,128)(2,1)S(1)}, bf16[256,768]{1,0:T(8,128)(2,1)}, u32[]{:S(2)}) copy-start(bf16[256,768]{1,0:T(8,128)(2,1)} %param.21) | copy-start | bytes 1179652
  0.0 12.0 %copy-start.12 = (s32[4096]{0:T(1024)S(1)}, s32[4096]{0:T(1024)}, u32[]{:S(2)}) copy-start(s32[4096]{0:T(1024)} %constant.105) | copy-start | bytes 49156
  0.0 12.0 %copy-start.13 = (f32[8,225]{1,0:T(8,128)S(1)}, f32[8,225]{1,0:T(8,128)}, u32[]{:S(2)}) copy-start(f32[8,225]{1,0:T(8,128)} %param.23) | copy-start | bytes 21604
  6.1 18.7 %collective-permute-start.8 = (bf16[4,32,256]{2,1,0:T(8,128)(2,1)S(1)}, bf16[4,32,256]{2,1,0:T(8,128)(2,1)S(1)}, u32[]{:S(2)}, u32[]{:S(2)}) collective-permute-start(bf16[4,32,256]{2,1,0:T(8,128)(2,1)S(1)} %slice.169), channel_id=1, source_target_pairs={{0,480},{32,0},{64,32},{96,64},{128,96},{160,128},{192,160},{224,1... | collective-permute-start | bytes 196616 | tf_op jit(solution)/shard_map/ppermute | solution.py:18
  8.8 28.2 %collective-permute-start = (bf16[4,32,256]{2,1,0:T(8,128)(2,1)S(1)}, bf16[4,32,256]{2,1,0:T(8,128)(2,1)S(1)}, u32[]{:S(2)}, u32[]{:S(2)}) collective-permute-start(bf16[4,32,256]{2,1,0:T(8,128)(2,1)S(1)} %slice.158), channel_id=1, source_target_pairs={{0,480},{32,0},{64,32},{96,64},{128,96},{160,128},{192,160},{224,1... | collective-permute-start | bytes 196616 | tf_op jit(solution)/shard_map/ppermute | solution.py:18
  22.9 16.4 %copy-start.15 = (f32[768]{0:T(1024)S(1)}, f32[768]{0:T(1024)}, u32[]{:S(2)}) copy-start(f32[768]{0:T(1024)} %param.22) | copy-start | bytes 9220
  24.8 14.4 %collective-permute-start.9 = (bf16[16,4,256]{2,1,0:T(4,128)(2,1)S(1)}, bf16[16,4,256]{2,1,0:T(4,128)(2,1)S(1)}, u32[]{:S(2)}, u32[]{:S(2)}) collective-permute-start(bf16[16,4,256]{2,1,0:T(4,128)(2,1)S(1)} %pad_maximum_fusion.10), channel_id=1, source_target_pairs={{0,31},{1,0},{2,1},{3,2},{4,3},{5,4},{6,5},{7,6},{8,7},{9,8},{10,9... | collective-permute-start | bytes 98312 | tf_op jit(solution)/shard_map/ppermute | solution.py:18
  37.0 5.0 %collective-permute-start.1 = (bf16[16,4,256]{2,1,0:T(4,128)(2,1)S(1)}, bf16[16,4,256]{2,1,0:T(4,128)(2,1)S(1)}, u32[]{:S(2)}, u32[]{:S(2)}) collective-permute-start(bf16[16,4,256]{2,1,0:T(4,128)(2,1)S(1)} %pad_maximum_fusion.11), channel_id=1, source_target_pairs={{0,31},{1,0},{2,1},{3,2},{4,3},{5,4},{6,5},{7,6},{8,7},{9,8},{10,9... | collective-permute-start | bytes 98312 | tf_op jit(solution)/shard_map/ppermute | solution.py:18
  47.2 2.7 %copy-start.14 = (bf16[256,256]{1,0:T(8,128)(2,1)S(1)}, bf16[256,256]{1,0:T(8,128)(2,1)}, u32[]{:S(2)}) copy-start(bf16[256,256]{1,0:T(8,128)(2,1)} %param.24) | copy-start | bytes 393220
  47.2 2.8 %copy-start.16 = (f32[256]{0:T(256)S(1)}, f32[256]{0:T(256)}, u32[]{:S(2)}) copy-start(f32[256]{0:T(256)} %param.25) | copy-start | bytes 3076
  49.2 4.3 %copy-start.5 = (bf16[8,64,1,8,32]{1,0,4,3,2:T(8,128)(2,1)S(1)}, bf16[8,64,1,8,32]{1,0,4,3,2:T(8,128)(2,1)}, u32[]{:S(2)}) copy-start(bf16[8,64,1,8,32]{1,0,4,3,2:T(8,128)(2,1)} %get-tuple-element.63) | copy-start | bytes 786436
  49.2 4.3 %copy-start.6 = (bf16[8,64,1,8,32]{1,0,4,3,2:T(8,128)(2,1)S(1)}, bf16[8,64,1,8,32]{1,0,4,3,2:T(8,128)(2,1)}, u32[]{:S(2)}) copy-start(bf16[8,64,1,8,32]{1,0,4,3,2:T(8,128)(2,1)} %get-tuple-element.64) | copy-start | bytes 786436
  49.2 4.3 %copy-start.7 = (f32[64,64,8]{0,1,2:T(8,128)S(1)}, f32[64,64,8]{0,1,2:T(8,128)}, u32[]{:S(2)}) copy-start(f32[64,64,8]{0,1,2:T(8,128)} %copy.50) | copy-start | bytes 393220
  49.2 4.3 %copy-start.8 = (f32[8,64,64]{1,2,0:T(8,128)S(1)}, f32[8,64,64]{1,2,0:T(8,128)}, u32[]{:S(2)}) copy-start(f32[8,64,64]{1,2,0:T(8,128)} %compare_select_fusion) | copy-start | bytes 393220
  50.3 8.3 %collective-permute-start.2 = (bf16[16,4,256]{2,1,0:T(4,128)(2,1)S(1)}, bf16[16,4,256]{2,1,0:T(4,128)(2,1)S(1)}, u32[]{:S(2)}, u32[]{:S(2)}) collective-permute-start(bf16[16,4,256]{2,1,0:T(4,128)(2,1)S(1)} %slice.164), channel_id=1, source_target_pairs={{0,1},{1,2},{2,3},{3,4},{4,5},{5,6},{6,7},{7,8},{8,9},{9,10},{10,1... | collective-permute-start | bytes 98312 | tf_op jit(solution)/shard_map/ppermute | solution.py:18
  53.5 2.4 %copy-start.4 = (bf16[8,64,1,8,32]{1,0,4,3,2:T(8,128)(2,1)S(1)}, bf16[8,64,1,8,32]{1,0,4,3,2:T(8,128)(2,1)}, u32[]{:S(2)}) copy-start(bf16[8,64,1,8,32]{1,0,4,3,2:T(8,128)(2,1)} %get-tuple-element.62) | copy-start | bytes 786436
  57.9 12.2 %copy-start.2 = (bf16[16,32,256]{2,1,0:T(8,128)(2,1)S(1)}, bf16[16,32,256]{2,1,0:T(8,128)(2,1)}, u32[]{:S(2)}) copy-start(bf16[16,32,256]{2,1,0:T(8,128)(2,1)} %param.18) | copy-start | bytes 786436
  58.6 8.9 %copy-start.9 = (bf16[16,4,256]{2,1,0:T(4,128)(2,1)}, bf16[16,4,256]{2,1,0:T(4,128)(2,1)S(1)}, u32[]{:S(2)}) copy-start(bf16[16,4,256]{2,1,0:T(4,128)(2,1)S(1)} %collective-permute-done.2) | copy-start | bytes 98308
  58.6 33.7 %copy-start.3 = (bf16[16,32,256]{2,1,0:T(8,128)(2,1)S(1)}, bf16[16,32,256]{2,1,0:T(8,128)(2,1)}, u32[]{:S(2)}) copy-start(bf16[16,32,256]{2,1,0:T(8,128)(2,1)} %param.17) | copy-start | bytes 786436
  58.7 11.4 %collective-permute-start.3 = (bf16[4,32,256]{2,1,0:T(8,128)(2,1)S(1)}, bf16[4,32,256]{2,1,0:T(8,128)(2,1)S(1)}, u32[]{:S(2)}, u32[]{:S(2)}) collective-permute-start(bf16[4,32,256]{2,1,0:T(8,128)(2,1)S(1)} %pad_maximum_fusion.9), channel_id=1, source_target_pairs={{0,32},{32,64},{64,96},{96,128},{128,160},{160,192},{192,224},{224... | collective-permute-start | bytes 196616 | tf_op jit(solution)/shard_map/ppermute | solution.py:18
  68.2 12.5 %collective-permute-start.10 = (bf16[16,4,256]{2,1,0:T(4,128)(2,1)}, bf16[16,4,256]{2,1,0:T(4,128)(2,1)}, u32[]{:S(2)}, u32[]{:S(2)}) collective-permute-start(bf16[16,4,256]{2,1,0:T(4,128)(2,1)} %slice.175), channel_id=1, source_target_pairs={{0,1},{1,2},{2,3},{3,4},{4,5},{5,6},{6,7},{7,8},{8,9},{9,10},{10,1... | collective-permute-start | bytes 98312 | tf_op jit(solution)/shard_map/ppermute | solution.py:18
  71.0 22.9 %copy-start.1 = (bf16[16,32,256]{2,1,0:T(8,128)(2,1)}, bf16[16,32,256]{2,1,0:T(8,128)(2,1)S(1)}, u32[]{:S(2)}) copy-start(bf16[16,32,256]{2,1,0:T(8,128)(2,1)S(1)} %fusion.45) | copy-start | bytes 786436
  71.8 17.0 %collective-permute-start.4 = (bf16[8,32,256]{2,1,0:T(8,128)(2,1)}, bf16[8,32,256]{2,1,0:T(8,128)(2,1)}, u32[]{:S(2)}, u32[]{:S(2)}) collective-permute-start(bf16[8,32,256]{2,1,0:T(8,128)(2,1)} %get-tuple-element.70), channel_id=1, source_target_pairs={{0,32},{32,64},{64,96},{96,128},{128,160},{160,192},{192,224},{224... | collective-permute-start | bytes 393224 | tf_op jit(solution)/shard_map/ppermute | solution.py:29
  78.2 10.6 %collective-permute-start.5 = (bf16[8,32,256]{2,1,0:T(8,128)(2,1)}, bf16[8,32,256]{2,1,0:T(8,128)(2,1)}, u32[]{:S(2)}, u32[]{:S(2)}) collective-permute-start(bf16[8,32,256]{2,1,0:T(8,128)(2,1)} %get-tuple-element.71), channel_id=1, source_target_pairs={{32,0},{64,32},{96,64},{128,96},{160,128},{192,160},{224,192},{256... | collective-permute-start | bytes 393224 | tf_op jit(solution)/shard_map/ppermute | solution.py:31
  81.5 10.9 %collective-permute-start.11 = (bf16[4,32,256]{2,1,0:T(8,128)(2,1)S(1)}, bf16[4,32,256]{2,1,0:T(8,128)(2,1)S(1)}, u32[]{:S(2)}, u32[]{:S(2)}) collective-permute-start(bf16[4,32,256]{2,1,0:T(8,128)(2,1)S(1)} %pad_maximum_fusion.8), channel_id=1, source_target_pairs={{0,32},{32,64},{64,96},{96,128},{128,160},{160,192},{192,224},{224... | collective-permute-start | bytes 196616 | tf_op jit(solution)/shard_map/ppermute | solution.py:18
  89.6 4.4 %collective-permute-start.6 = (bf16[32,8,256]{2,1,0:T(8,128)(2,1)S(1)}, bf16[32,8,256]{2,1,0:T(8,128)(2,1)S(1)}, u32[]{:S(2)}, u32[]{:S(2)}) collective-permute-start(bf16[32,8,256]{2,1,0:T(8,128)(2,1)S(1)} %get-tuple-element.68), channel_id=1, source_target_pairs={{0,1},{1,2},{2,3},{3,4},{4,5},{5,6},{6,7},{7,8},{8,9},{9,10},{10,1... | collective-permute-start | bytes 393224 | tf_op jit(solution)/shard_map/ppermute | solution.py:29
  90.9 5.7 %collective-permute-start.7 = (bf16[32,8,256]{2,1,0:T(8,128)(2,1)S(1)}, bf16[32,8,256]{2,1,0:T(8,128)(2,1)S(1)}, u32[]{:S(2)}, u32[]{:S(2)}) collective-permute-start(bf16[32,8,256]{2,1,0:T(8,128)(2,1)S(1)} %get-tuple-element.69), channel_id=1, source_target_pairs={{1,0},{2,1},{3,2},{4,3},{5,4},{6,5},{7,6},{8,7},{9,8},{10,9},{11,1... | collective-permute-start | bytes 393224 | tf_op jit(solution)/shard_map/ppermute | solution.py:31
  194.4 3.1 %copy-start.17 = (bf16[256,2]{0,1:T(2,128)(2,1)S(1)}, bf16[256,2]{0,1:T(2,128)(2,1)}, u32[]{:S(2)}) copy-start(bf16[256,2]{0,1:T(2,128)(2,1)} %param.28) | copy-start | bytes 3076
  194.4 3.1 %copy-start.18 = (f32[256]{0:T(256)S(1)}, f32[256]{0:T(256)}, u32[]{:S(2)}) copy-start(f32[256]{0:T(256)} %param.27) | copy-start | bytes 3076
  194.4 3.1 %copy-start.19 = (f32[2]{0:T(128)S(1)}, f32[2]{0:T(128)}, u32[]{:S(2)}) copy-start(f32[2]{0:T(128)} %param.29) | copy-start | bytes 28
  197.5 1.7 copy-start.10
  197.5 1.6 copy-start.11
where the time goes:
time: 203 us; the launch traced here: 201 us
  other arithmetic  65.2 us (32%)
  starting transfers between devices  51 us (25%)
  loops' own time  34.5 us (17%)
  local copies, waits for them, and re-layouts  34.1 us (17%)
  matrix products  12.6 us (6%)
  waiting for transfers between devices  2.68 us (1%)
    dot_general x17, other arithmetic, one_row_offset(): jnp.einsum('yxc,yxc->yx', feature_a, reach[:, col_off:col_off + width], p...  48.2 us
    ppermute x8, starting transfers between devices, shifted(): lax.ppermute(array, axis, [(i, (i + by) % peers) for i in range(peers)])  39.9 us
    another operation x1, loops' own time, correlate(): volume = lax.map(one_row_offset, jnp.arange(reach_span, dtype=jnp.int32))  34.5 us
    gather x2, local copies, waits for them, and re-layouts, shards(): position_bias = rel_table[:, relative_index()]  12.7 us
    dynamic_slice x17, local copies, waits for them, and re-layouts, correlate(): volume = lax.map(one_row_offset, jnp.arange(reach_span, dtype=jnp.int32))  11 us
    ppermute x2, starting transfers between devices, with_halo(): lax.ppermute(tail, axis, [(i, (i + 1) % count) for i in range(ends)])  7.71 us
    sub x2, matrix products, attend(): weights = jax.nn.softmax(scores, axis=-1).astype(jnp.bfloat16)  5.82 us
  transfers between devices with their start and end apart: 12, of which 1 were waited for; matrix products, arithmetic and copies ran while one was open for 14% of the time, Pallas kernels for 0%

commit v1 on v0

v1 whole, which is shorter than its diff:
```python
import jax
import jax.numpy as jnp
import numpy as np
from jax import lax
from jax.experimental import pallas as pl
from jax.experimental.pallas import tpu as pltpu
from jax.sharding import PartitionSpec as P

C = 256
HEADS = 8
HEAD = 32
WIN = 8
SHIFT = 4
RADIUS = 8
SPAN = 2 * RADIUS + 1
OFFS = SPAN * SPAN
ROWS = 16
COLS = 32
HALO_A = 4
HALO_B = 12
HIGH_A, WIDE_A = 3, 5
HIGH_B, WIDE_B = 5, 7
CELLS = WIN * WIN
COUNT_A = HIGH_A * WIDE_A
COUNT_B = HIGH_B * WIDE_B
BLOCK = HIGH_B * CELLS
BLOCKS = (COUNT_A + COUNT_B) // HIGH_B
KEYS = 64
REACH = 18 * KEYS
LOG2E = 1.4426950408889634
NT = (((1,), (1,)), ((), ()))


def ring(array, axis, by):
    peers = lax.axis_size(axis)
    return lax.ppermute(array, axis, [(i, (i + by) % peers) for i in range(peers)])


def dot(left, right):
    return jnp.dot(left, right, preferred_element_type=jnp.float32)


def body(
    marks,
    xb,
    xa,
    gain,
    shift,
    w_qkv,
    b_qkv,
    bias,
    w_out,
    b_out,
    w_even,
    w_odd,
    w_off,
    b_hid,
    w_flow,
    b_flow,
    mirror,
    unmirror,
    out,
    q_s,
    k_s,
    v_s,
    mix_s,
    fb,
    fa,
    e_s,
):
    def project(x, row):
        x = x.astype(jnp.float32)
        centred = x - jnp.mean(x, axis=-1, keepdims=True)
        variance = jnp.mean(centred * centred, axis=-1, keepdims=True)
        normed = centred * lax.rsqrt(variance + 1e-05) * gain[...] + shift[...]
        qkv = dot(normed.astype(jnp.bfloat16), w_qkv[...]) + b_qkv[...]
        rows = pl.ds(row, BLOCK)
        q_s[rows] = (qkv[:, :C] * (HEAD**-0.5 * LOG2E)).astype(jnp.bfloat16)
        k_s[rows] = qkv[:, C : 2 * C].astype(jnp.bfloat16)
        v_s[rows] = qkv[:, 2 * C :].astype(jnp.bfloat16)

    @pl.loop(0, WIDE_B)
    def _(j):
        row = pl.multiple_of(j * BLOCK, BLOCK)
        project(xb[pl.ds(row, BLOCK)], row)

    @pl.loop(0, BLOCKS - WIDE_B)
    def _(j):
        row = pl.multiple_of(j * BLOCK, BLOCK)
        project(xa[pl.ds(row, BLOCK)], pl.multiple_of(row + WIDE_B * BLOCK, BLOCK))

    lanes = lax.broadcasted_iota(jnp.int32, (1, C), 1) // HEAD
    picks = [(lanes == h).astype(jnp.float32).astype(jnp.bfloat16) for h in range(HEADS)]
    ones = jnp.concatenate(
        [jnp.broadcast_to(p, (CELLS, C)) for p in picks], axis=0
    )
    half = lax.broadcasted_iota(jnp.int32, (CELLS, 128), 1) < CELLS

    def attend(window):
        rows = pl.ds(pl.multiple_of(window * CELLS, CELLS), CELLS)
        q, k, v = q_s[rows], k_s[rows], v_s[rows]
        keys = jnp.concatenate([k * p for p in picks], axis=0)
        values = jnp.concatenate([v * p for p in picks], axis=0)
        scores = lax.dot_general(q, keys, NT, preferred_element_type=jnp.float32)
        scores = scores + bias[marks[window]]
        weights = []
        for pair in range(HEADS // 2):
            s = scores[:, 128 * pair : 128 * (pair + 1)]
            low = jnp.max(jnp.where(half, s, -jnp.inf), axis=-1, keepdims=True)
            top = jnp.max(jnp.where(half, -jnp.inf, s), axis=-1, keepdims=True)
            weights.append(jnp.exp2(s - jnp.where(half, low, top)).astype(jnp.bfloat16))
        weights = jnp.concatenate(weights, axis=1)
        mix_s[rows] = (dot(weights, values) / dot(weights, ones)).astype(jnp.bfloat16)

    @pl.loop(0, BLOCKS)
    def _(block):
        for i in range(HIGH_B):
            attend(block * HIGH_B + i)

    row_start = marks[64] * ROWS
    col_start = marks[65] * COLS
    total_rows = marks[66] * ROWS
    total_cols = marks[67] * COLS

    def features(x, mixed):
        attended = (dot(mixed, w_out[...]) + b_out[...]).astype(jnp.bfloat16)
        return x.astype(jnp.float32) + attended.astype(jnp.float32)

    col_places = col_start - HALO_B + lax.broadcasted_iota(jnp.int32, (KEYS, 1), 0)
    col_inside = (col_places >= 0) & (col_places < total_cols)
    blank = jnp.zeros((KEYS - WIDE_B * WIN, C), jnp.float32)

    @pl.loop(0, HIGH_B)
    def _(i):
        starts = [
            pl.multiple_of(j * BLOCK + i * CELLS, CELLS) for j in range(WIDE_B)
        ]
        x = jnp.concatenate([xb[pl.ds(s, CELLS)] for s in starts], axis=0)
        mixed = jnp.concatenate([mix_s[pl.ds(s, CELLS)] for s in starts], axis=0)
        f = features(x, mixed)
        for r in range(WIN):
            row = jnp.concatenate(
                [f[CELLS * j + WIN * r : CELLS * j + WIN * (r + 1)] for j in range(WIDE_B)]
                + [blank],
                axis=0,
            )
            place = row_start - HALO_B + i * WIN + r
            inside = col_inside & (place >= 0) & (place < total_rows)
            fb[i * WIN + r] = jnp.where(inside, row, 0.0).astype(jnp.bfloat16)

    @pl.loop(0, HIGH_A)
    def _(i):
        starts = [
            pl.multiple_of(j * HIGH_A * CELLS + i * CELLS, CELLS) for j in range(WIDE_A)
        ]
        x = jnp.concatenate([xa[pl.ds(s, CELLS)] for s in starts], axis=0)
        mixed = jnp.concatenate(
            [mix_s[pl.ds(pl.multiple_of(s + WIDE_B * BLOCK, CELLS), CELLS)] for s in starts],
            axis=0,
        )
        f = features(x, mixed)
        f = dot(mirror[...], f.astype(jnp.bfloat16)).astype(jnp.bfloat16)
        fa[pl.ds(i * WIN, WIN)] = f.reshape(WIN, COLS, C)

    lane = lax.broadcasted_iota(jnp.int32, (COLS, 128), 1)
    near = lane % KEYS < SPAN
    first = near & (lane < KEYS)
    second = near & (lane >= KEYS)

    @pl.loop(0, ROWS // 4)
    def _(t):
        queries = fa[pl.ds(HALO_A + 4 * t, 4)].reshape(4 * COLS, C)
        keys = fb[pl.ds(HALO_B - RADIUS + 4 * t, 20)].reshape(20 * KEYS, C)
        gram = lax.dot_general(queries, keys, NT, preferred_element_type=jnp.float32)
        for r in range(4):
            tiles = []
            for n in range(9):
                at = 128 * (n + r // 2)
                tile = gram[COLS * r : COLS * (r + 1), at : at + 128]
                tile = pltpu.roll(tile, 128 - HALO_A - COLS + 1, 1, stride=1, stride_axis=0)
                keep = near
                if r % 2 == 0 and n == 8:
                    keep = first
                if r % 2 == 1 and n == 0:
                    keep = second
                tiles.append(jnp.where(keep, tile * (C**-0.5 * LOG2E), -1e30))
            most = tiles[0]
            for tile in tiles[1:]:
                most = jnp.maximum(most, tile)
            most = jnp.max(most, axis=-1, keepdims=True)
            rows = pl.ds(pl.multiple_of((2 * t + r // 2) * COLS, COLS), COLS)
            for n in range(9):
                e_s[r % 2, rows, 128 * n : 128 * (n + 1)] = jnp.exp2(tiles[n] - most).astype(
                    jnp.bfloat16
                )

    for par, w_hid in enumerate((w_even, w_odd)):
        e = e_s[par]
        sums = dot(e, w_off[par])
        scale = 1.0 / sums[:, 2:3]
        hidden = jax.nn.gelu(dot(e, w_hid[...]) * (scale * OFFS) + b_hid[...])
        flow = sums * scale + dot(hidden.astype(jnp.bfloat16), w_flow[...]) + b_flow[...]
        flow = jnp.dot(
            unmirror[...],
            flow,
            precision=lax.Precision.HIGHEST,
            preferred_element_type=jnp.float32,
        ).T
        for t in range(ROWS // 2):
            out[:, 2 * t + par, :] = flow[0:2, COLS * t : COLS * (t + 1)]


def skewed(w_hid):
    w = w_hid.reshape(SPAN, SPAN, C)
    w = jnp.pad(w, ((0, 0), (0, KEYS - SPAN), (0, 0)))
    even = jnp.pad(w, ((0, 1), (0, 0), (0, 0))).reshape(REACH, C)
    odd = jnp.pad(w, ((1, 0), (0, 0), (0, 0))).reshape(REACH, C)
    return even, odd


def offsets():
    table = np.zeros((2, 18, KEYS, 128), np.float32)
    for par in range(2):
        for dr in range(SPAN):
            for dc in range(SPAN):
                table[par, dr + par, dc, :3] = (dr - RADIUS, dc - RADIUS, 1.0)
    return jnp.asarray(table.reshape(2, REACH, 128), jnp.bfloat16)


def mirrors():
    turn = np.zeros((WIN, COLS, WIDE_A, WIN, WIN), np.float32)
    for r in range(WIN):
        for c in range(COLS):
            place = HALO_A + COLS - 1 - c
            turn[r, c, place // WIN, r, place % WIN] = 1.0
    turn = jnp.asarray(turn.reshape(WIN * COLS, WIDE_A * CELLS), jnp.bfloat16)
    back = np.kron(np.eye(ROWS // 2, dtype=np.float32), np.eye(COLS, dtype=np.float32)[::-1])
    return turn, jnp.asarray(back)


def position_bias(rel_table):
    places = np.arange(CELLS)
    rows, cols = places // WIN, places % WIN
    index = (rows[:, None] - rows[None, :] + WIN - 1) * (2 * WIN - 1) + (
        cols[:, None] - cols[None, :] + WIN - 1
    )
    pick = np.zeros(((2 * WIN - 1) ** 2, CELLS * CELLS), np.float32)
    pick[index.reshape(-1), np.arange(CELLS * CELLS)] = 1.0
    pick = jnp.asarray(pick, jnp.bfloat16)
    high = rel_table.astype(jnp.bfloat16)
    rest = rel_table - high.astype(jnp.float32)
    mid = rest.astype(jnp.bfloat16)
    low = (rest - mid.astype(jnp.float32)).astype(jnp.bfloat16)
    table = jnp.sum(
        dot(jnp.concatenate([high, mid, low], axis=0), pick).reshape(3, HEADS, CELLS, CELLS),
        axis=0,
    )
    split_r = (rows[:, None] < SHIFT) != (rows[None, :] < SHIFT)
    split_c = (cols[:, None] < SHIFT) != (cols[None, :] < SHIFT)
    masks = np.stack([split_r & False, split_r, split_c, split_r | split_c])
    masks = jnp.asarray(np.where(masks, -100.0, 0.0), jnp.float32)
    full = (table.transpose(1, 0, 2)[None] + masks[:, :, None, :]) * LOG2E
    return full.reshape(4, CELLS, HEADS * CELLS)


def window_marks(row, col, rows, cols):
    def marks(high, wide, inset):
        i = jnp.arange(high, dtype=jnp.int32)[None, :]
        j = jnp.arange(wide, dtype=jnp.int32)[:, None]
        on_row = ((row == 0) & (i == inset)) | ((row == rows - 1) & (i == high - 1 - inset))
        on_col = ((col == 0) & (j == inset)) | ((col == cols - 1) & (j == wide - 1 - inset))
        return (on_row.astype(jnp.int32) + 2 * on_col.astype(jnp.int32)).reshape(-1)

    return jnp.concatenate(
        [
            marks(HIGH_B, WIDE_B, 1),
            marks(HIGH_A, WIDE_A, 0),
            jnp.zeros((14,), jnp.int32),
            jnp.stack([row, col, jnp.int32(rows), jnp.int32(cols)]),
        ]
    )


def split_cols(cells, wide):
    return cells.reshape(cells.shape[0], wide, WIN, C).transpose(1, 0, 2, 3)


def shards(
    section_a,
    section_b,
    ln_gain,
    ln_shift,
    w_qkv,
    b_qkv,
    rel_table,
    w_out,
    b_out,
    w_hid,
    b_hid,
    w_flow,
    b_flow,
):
    rows, cols = lax.axis_size("row"), lax.axis_size("col")
    row, col = lax.axis_index("row"), lax.axis_index("col")

    left = jnp.concatenate([section_b[:, :HALO_B], section_a[:, :HALO_A]], axis=1)
    right = jnp.concatenate([section_b[:, -HALO_B:], section_a[:, -HALO_A:]], axis=1)
    after = ring(left, "col", -1)
    before = ring(right, "col", 1)
    wide_b = jnp.concatenate([before[:, :HALO_B], section_b, after[:, :HALO_B]], axis=1)
    wide_a = jnp.concatenate([before[:, HALO_B:], section_a, after[:, HALO_B:]], axis=1)
    wide_b = split_cols(wide_b, WIDE_B)
    wide_a = split_cols(wide_a, WIDE_A)

    def pack(b_part, a_part):
        return jnp.concatenate([b_part.reshape(-1, C), a_part.reshape(-1, C)], axis=0)

    def unpack(flat):
        cut = WIDE_B * HALO_B * WIN
        return (
            flat[:cut].reshape(WIDE_B, HALO_B, WIN, C),
            flat[cut:].reshape(WIDE_A, HALO_A, WIN, C),
        )

    below_b, below_a = unpack(ring(pack(wide_b[:, :HALO_B], wide_a[:, :HALO_A]), "row", -1))
    above_b, above_a = unpack(ring(pack(wide_b[:, -HALO_B:], wide_a[:, -HALO_A:]), "row", 1))
    xb = jnp.concatenate([above_b, wide_b, below_b], axis=1).reshape(-1, C)
    xa = jnp.concatenate([above_a, wide_a, below_a], axis=1).reshape(-1, C)

    w_even, w_odd = skewed(w_hid)
    flow_pad = jnp.pad(w_flow, ((0, 0), (0, 126)))
    b_flow_pad = jnp.pad(b_flow, (0, 126))
    total = (COUNT_A + COUNT_B) * CELLS
    whole = pl.BlockSpec(memory_space=pltpu.VMEM)
    call = pl.pallas_call(
        body,
        out_shape=jax.ShapeDtypeStruct((2, ROWS, COLS), jnp.float32),
        in_specs=[pl.BlockSpec(memory_space=pltpu.SMEM)] + [whole] * 17,
        out_specs=whole,
        scratch_shapes=[
            pltpu.VMEM((total, C), jnp.bfloat16),
            pltpu.VMEM((total, C), jnp.bfloat16),
            pltpu.VMEM((total, C), jnp.bfloat16),
            pltpu.VMEM((total, C), jnp.bfloat16),
            pltpu.VMEM((HIGH_B * WIN, KEYS, C), jnp.bfloat16),
            pltpu.VMEM((HIGH_A * WIN, COLS, C), jnp.bfloat16),
            pltpu.VMEM((2, ROWS // 2 * COLS, REACH), jnp.bfloat16),
        ],
        compiler_params=pltpu.CompilerParams(vmem_limit_bytes=40 * 1024 * 1024),
    )
    return call(
        window_marks(row, col, rows, cols),
        xb,
        xa,
        ln_gain[None],
        ln_shift[None],
        w_qkv,
        b_qkv[None],
        position_bias(rel_table),
        w_out,
        b_out[None],
        w_even,
        w_odd,
        offsets(),
        b_hid[None],
        flow_pad,
        b_flow_pad[None],
        *mirrors(),
    )


def solution(mesh):
    placed = (P("row", "col", None),) * 2 + (P(),) * 11
    return jax.shard_map(
        shards, mesh=mesh, in_specs=placed, out_specs=P(None, "row", "col"), check_vma=False
    )
```

time: 203 us -> 77.3 us (0.38)
  other arithmetic: 65.2 us -> 2.4 us
  loops' own time: 34.5 us -> 0 us
  Pallas kernels: 0 us -> 31 us
  starting transfers between devices: 51 us -> 22.4 us
  local copies, waits for them, and re-layouts: 34.1 us -> 7.52 us
  matrix products: 12.6 us -> 1.99 us
  waiting for transfers between devices: 2.68 us -> 11.1 us
    dot_general x17 -> x0, other arithmetic: 48.2 us -> none  [one_row_offset(): jnp.einsum('yxc,yxc->yx', feature_a, reach[:, col_off:col_off + width], p...]
    another operation x1 -> x0, loops' own time: 34.5 us -> none  [correlate(): volume = lax.map(one_row_offset, jnp.arange(reach_span, dtype=jnp.int32))]
    pallas_call x0 -> x1, Pallas kernels: none -> 31 us  [shards(): call(window_marks(row, col, rows, cols), xb, xa, ln_gain[None], ln_shift[...]
    ppermute x12 -> x4, starting transfers between devices: 51 us -> 22.4 us  [ring(): lax.ppermute(array, axis, [(i, (i + by) % peers) for i in range(peers)])]
    gather x2 -> x0, local copies, waits for them, and re-layouts: 12.7 us -> none  [shards(): position_bias = rel_table[:, relative_index()]]
    dynamic_slice x17 -> x0, local copies, waits for them, and re-layouts: 11 us -> none  [correlate(): volume = lax.map(one_row_offset, jnp.arange(reach_span, dtype=jnp.int32))]
    ppermute x12 -> x4, waiting for transfers between devices: 2.68 us -> 11.1 us  [ring(): lax.ppermute(array, axis, [(i, (i + by) % peers) for i in range(peers)])]
    reduce_sum x6 -> x1, other arithmetic: 6.2 us -> 0.08 us  [position_bias(): jnp.sum(dot(jnp.concatenate([high, mid, low], axis=0), pick).reshape(3, H...]
  transfers between devices with their start and end apart: 12 -> 4, of which waited for: 1 -> 2; matrix products, arithmetic and copies ran while one was open for 14% -> 8% of each run, Pallas kernels for 0% -> 0%
where the time goes in v1:
time: 77.3 us; the launch traced here: 76.9 us
  Pallas kernels  31 us (40%)
  starting transfers between devices  22.4 us (29%)
  waiting for transfers between devices  11.1 us (14%)
  local copies, waits for them, and re-layouts  7.52 us (10%)
  other arithmetic  2.4 us (3%)
  matrix products  1.99 us (3%)
    pallas_call x1, Pallas kernels, shards(): call(window_marks(row, col, rows, cols), xb, xa, ln_gain[None], ln_shift[...  31 us
    ppermute x4, starting transfers between devices, ring(): lax.ppermute(array, axis, [(i, (i + by) % peers) for i in range(peers)])  22.4 us
    ppermute x4, waiting for transfers between devices, ring(): lax.ppermute(array, axis, [(i, (i + by) % peers) for i in range(peers)])  11.1 us
    unnamed x35, local copies, waits for them, and re-layouts  2.56 us
    dot_general x1, matrix products, dot(): return jnp.dot(left, right, preferred_element_type=jnp.float32)  1.99 us
    concatenate x2, other arithmetic, pack(): jnp.concatenate([b_part.reshape(-1, C), a_part.reshape(-1, C)], axis=0)  1.59 us
  transfers between devices with their start and end apart: 4, of which 2 were waited for; matrix products, arithmetic and copies ran while one was open for 8% of the time, Pallas kernels for 0%

profile of v1, /device:TPU:7, one launch (start us, length us, event | category | flops | bytes accessed | tf_op | source)
XLA Modules:
  0.0 76.9 jit_solution(13887545322870988216)
XLA Ops:
  0.0 1.0 %fusion.6 = (bf16[16,12,256]{2,1,0:T(8,128)(2,1)S(1)}, bf16[16,12,256]{2,1,0:T(8,128)(2,1)S(1)}) fusion(bf16[16,32,256]{2,1,0:T(8,128)(2,1)} %param.19), kind=kLoop, calls=%fused_computation.27 | loop fusion | bytes 393216 | tf_op jit(solution)/shard_map/slice | solution.py:307
  1.0 0.9 %fusion.7 = (bf16[16,4,256]{2,1,0:T(4,128)(2,1)S(1)}, bf16[16,4,256]{2,1,0:T(4,128)(2,1)S(1)}) fusion(bf16[16,32,256]{2,1,0:T(8,128)(2,1)} %param.18), kind=kLoop, calls=%fused_computation.28 | loop fusion | bytes 131072 | tf_op jit(solution)/shard_map/slice | solution.py:307
  2.0 12.1 %collective-permute-start.1 = (bf16[16,16,256]{2,1,0:T(8,128)(2,1)S(1)}, bf16[16,16,256]{2,1,0:T(8,128)(2,1)S(1)}, u32[]{:S(2)}, u32[]{:S(2)}) collective-permute-start(bf16[16,16,256]{2,1,0:T(8,128)(2,1)S(1)} %pad_maximum_fusion.5), channel_id=1, source_target_pairs={{0,31},{1,0},{2,1},{3,2},{4,3},{5,4},{6,5},{7,6},{8,7},{9,8},{10,9... | collective-permute-start | bytes 393224 | tf_op jit(solution)/shard_map/ppermute | solution.py:36
  14.2 1.9 %collective-permute-start = (bf16[16,16,256]{2,1,0:T(8,128)(2,1)S(1)}, bf16[16,16,256]{2,1,0:T(8,128)(2,1)S(1)}, u32[]{:S(2)}, u32[]{:S(2)}) collective-permute-start(bf16[16,16,256]{2,1,0:T(8,128)(2,1)S(1)} %pad_maximum_fusion.4), channel_id=1, source_target_pairs={{0,1},{1,2},{2,3},{3,4},{4,5},{5,6},{6,7},{7,8},{8,9},{9,10},{10,1... | collective-permute-start | bytes 393224 | tf_op jit(solution)/shard_map/ppermute | solution.py:36
  16.2 0.1 broadcast_add_fusion
  16.3 2.0 %fusion = f32[24,4096]{1,0:T(8,128)S(1)} fusion(bf16[225,4096]{1,0:T(8,128)(2,1)} %constant.54.clone, bf16[8,225]{1,0:T(8,128)(2,1)S(1)} %get-tuple-element.16, bf16[8,225]{1,0:T(8,128)(2,1)S(1)} %get-tuple-element.17, bf16[8,225]{1,0:T(8,128)(2,1)S(1)} %get-tuple-element.15), kind=kOutput, calls=%fused_computation.12 | convolution fusion | flops 44269200 | bytes 2247216 | tf_op jit(solution)/shard_map/dot_general | solution.py:40
  18.3 3.7 %collective-permute-done = bf16[16,16,256]{2,1,0:T(8,128)(2,1)S(1)} collective-permute-done((bf16[16,16,256]{2,1,0:T(8,128)(2,1)S(1)}, bf16[16,16,256]{2,1,0:T(8,128)(2,1)S(1)}, u32[]{:S(2)}, u32[]{:S(2)}) %collective-permute-start) | collective-permute-done | bytes 131104 | tf_op jit(solution)/shard_map/ppermute | solution.py:36
  22.0 0.1 copy_bitcast_fusion
  22.2 0.7 copy-done.10
  22.9 0.1 copy_bitcast_fusion.1
  23.1 0.8 %pad_maximum_fusion.2 = bf16[832,256]{1,0:T(8,128)(2,1)} fusion(bf16[160,256]{1,0:T(8,128)(2,1)S(1)} %bitcast.50, bf16[672,256]{1,0:T(8,128)(2,1)S(1)} %bitcast.47), kind=kLoop, calls=%fused_computation.5 | loop fusion | flops 851968 | bytes 851968 | tf_op jit(solution)/shard_map/concatenate | solution.py:316
  23.9 6.4 %collective-permute-start.2 = (bf16[832,256]{1,0:T(8,128)(2,1)}, bf16[832,256]{1,0:T(8,128)(2,1)S(1)}, u32[]{:S(2)}, u32[]{:S(2)}) collective-permute-start(bf16[832,256]{1,0:T(8,128)(2,1)} %pad_maximum_fusion.2), channel_id=1, source_target_pairs={{0,32},{32,64},{64,96},{96,128},{128,160},{160,192},{192,224},{224... | collective-permute-start | bytes 1277960 | tf_op jit(solution)/shard_map/ppermute | solution.py:36
  30.3 0.8 %pad_maximum_fusion.3 = bf16[832,256]{1,0:T(8,128)(2,1)} fusion(bf16[160,256]{1,0:T(8,128)(2,1)S(1)} %bitcast.49, bf16[672,256]{1,0:T(8,128)(2,1)S(1)} %bitcast.46), kind=kLoop, calls=%fused_computation.6 | loop fusion | flops 851968 | bytes 851968 | tf_op jit(solution)/shard_map/concatenate | solution.py:316
  31.1 1.9 %collective-permute-start.3 = (bf16[832,256]{1,0:T(8,128)(2,1)}, bf16[832,256]{1,0:T(8,128)(2,1)S(1)}, u32[]{:S(2)}, u32[]{:S(2)}) collective-permute-start(bf16[832,256]{1,0:T(8,128)(2,1)} %pad_maximum_fusion.3), channel_id=1, source_target_pairs={{0,480},{32,0},{64,32},{96,64},{128,96},{160,128},{192,160},{224,1... | collective-permute-start | bytes 1277960 | tf_op jit(solution)/shard_map/ppermute | solution.py:36
  33.0 0.1 add.69
  33.1 0.6 add.65
  33.7 0.3 reshape.142
  34.0 0.1 reduce_sum.9
  34.1 0.2 copy.30
  34.3 0.1 add.70
  34.4 0.5 copy-done.11
  35.0 0.3 add.73
  35.3 1.0 %reshape.143 = bf16[17,17,256]{2,1,0:T(8,128)(2,1)S(1)} reshape(bf16[289,256]{1,0:T(8,128)(2,1)} %param.27) | data formatting | bytes 295936 | tf_op jit(solution)/shard_map/reshape | solution.py:214
  36.3 0.1 copy.31
  36.6 0.1 concatenate.30.marks
  36.7 0.1 fusion.3
  36.9 7.5 %collective-permute-done.3 = bf16[832,256]{1,0:T(8,128)(2,1)S(1)} collective-permute-done((bf16[832,256]{1,0:T(8,128)(2,1)}, bf16[832,256]{1,0:T(8,128)(2,1)S(1)}, u32[]{:S(2)}, u32[]{:S(2)}) %collective-permute-start.3) | collective-permute-done | bytes 426016 | tf_op jit(solution)/shard_map/ppermute | solution.py:36
  44.6 0.1 pad_maximum_fusion
  44.7 0.8 %copy-done = bf16[2,1152,128]{2,1,0:T(8,128)(2,1)S(1)} copy-done((bf16[2,1152,128]{2,1,0:T(8,128)(2,1)S(1)}, bf16[2,1152,128]{2,1,0:T(8,128)(2,1)}, u32[]{:S(2)}) %copy-start) | copy-done | bytes 589848
  45.6 0.1 copy-done.1
  45.7 0.1 copy-done.2
  45.9 31.0 %shard_map.172 = f32[2,16,32]{2,1,0:T(8,128)} custom-call(s32[68]{0:T(128)S(1)} %concatenate.30.marks, bf16[2240,256]{1,0:T(8,128)(2,1)S(1)} %bitcast.36, bf16[960,256]{1,0:T(8,128)(2,1)S(1)} %bitcast.39, f32[1,256]{1,0:T(1,128)S(1)} %bitcast.40, f32[1,256]{1,0:T(1,128)S(1)} %bitcast.41, bf16[256,768]{1,0:T(8,128)(2,1)S(1)} %copy-done.1, ...), custom_call_target="tpu_custom_call" | custom-call | tf_op jit(solution)/shard_map/pallas_call | solution.py:351
  (55 shorter events, 0.8 us)
Async XLA Ops:
  0.0 16.2 %copy-start.12 = (f32[8,225]{1,0:T(8,128)S(1)}, f32[8,225]{1,0:T(8,128)}, u32[]{:S(2)}) copy-start(f32[8,225]{1,0:T(8,128)} %param.24) | copy-start | bytes 21604
  2.0 16.4 %collective-permute-start.1 = (bf16[16,16,256]{2,1,0:T(8,128)(2,1)S(1)}, bf16[16,16,256]{2,1,0:T(8,128)(2,1)S(1)}, u32[]{:S(2)}, u32[]{:S(2)}) collective-permute-start(bf16[16,16,256]{2,1,0:T(8,128)(2,1)S(1)} %pad_maximum_fusion.5), channel_id=1, source_target_pairs={{0,31},{1,0},{2,1},{3,2},{4,3},{5,4},{6,5},{7,6},{8,7},{9,8},{10,9... | collective-permute-start | bytes 393224 | tf_op jit(solution)/shard_map/ppermute | solution.py:36
  14.2 7.8 %collective-permute-start = (bf16[16,16,256]{2,1,0:T(8,128)(2,1)S(1)}, bf16[16,16,256]{2,1,0:T(8,128)(2,1)S(1)}, u32[]{:S(2)}, u32[]{:S(2)}) collective-permute-start(bf16[16,16,256]{2,1,0:T(8,128)(2,1)S(1)} %pad_maximum_fusion.4), channel_id=1, source_target_pairs={{0,1},{1,2},{2,3},{3,4},{4,5},{5,6},{6,7},{7,8},{8,9},{9,10},{10,1... | collective-permute-start | bytes 393224 | tf_op jit(solution)/shard_map/ppermute | solution.py:36
  16.3 5.7 %copy-start.9 = (bf16[16,32,256]{2,1,0:T(8,128)(2,1)S(1)}, bf16[16,32,256]{2,1,0:T(8,128)(2,1)}, u32[]{:S(2)}) copy-start(bf16[16,32,256]{2,1,0:T(8,128)(2,1)} %param.19) | copy-start | bytes 786436
  22.0 1.0 %copy-start.10 = (bf16[16,32,256]{2,1,0:T(8,128)(2,1)S(1)}, bf16[16,32,256]{2,1,0:T(8,128)(2,1)}, u32[]{:S(2)}) copy-start(bf16[16,32,256]{2,1,0:T(8,128)(2,1)} %param.18) | copy-start | bytes 786436
  23.1 10.0 %copy-start.16 = (f32[2]{0:T(128)S(1)}, f32[2]{0:T(128)}, u32[]{:S(2)}) copy-start(f32[2]{0:T(128)} %param.30) | copy-start | bytes 28
  23.9 13.0 %collective-permute-start.2 = (bf16[832,256]{1,0:T(8,128)(2,1)}, bf16[832,256]{1,0:T(8,128)(2,1)S(1)}, u32[]{:S(2)}, u32[]{:S(2)}) collective-permute-start(bf16[832,256]{1,0:T(8,128)(2,1)} %pad_maximum_fusion.2), channel_id=1, source_target_pairs={{0,32},{32,64},{64,96},{96,128},{128,160},{160,192},{192,224},{224... | collective-permute-start | bytes 1277960 | tf_op jit(solution)/shard_map/ppermute | solution.py:36
  31.1 13.3 %collective-permute-start.3 = (bf16[832,256]{1,0:T(8,128)(2,1)}, bf16[832,256]{1,0:T(8,128)(2,1)S(1)}, u32[]{:S(2)}, u32[]{:S(2)}) collective-permute-start(bf16[832,256]{1,0:T(8,128)(2,1)} %pad_maximum_fusion.3), channel_id=1, source_target_pairs={{0,480},{32,0},{64,32},{96,64},{128,96},{160,128},{192,160},{224,1... | collective-permute-start | bytes 1277960 | tf_op jit(solution)/shard_map/ppermute | solution.py:36
  34.0 0.9 %copy-start.11 = (f32[4,64,64]{2,1,0:T(8,128)S(1)}, f32[4,64,64]{2,1,0:T(8,128)}, u32[]{:S(2)}) copy-start(f32[4,64,64]{2,1,0:T(8,128)} %constant.55.clone) | copy-start | bytes 196612
  35.0 1.3 %copy-start.15 = (bf16[256,2]{0,1:T(2,128)(2,1)S(1)}, bf16[256,2]{0,1:T(2,128)(2,1)}, u32[]{:S(2)}) copy-start(bf16[256,2]{0,1:T(2,128)(2,1)} %param.29) | copy-start | bytes 3076
  35.0 1.5 %copy-start.13 = (f32[768]{0:T(1024)S(1)}, f32[768]{0:T(1024)}, u32[]{:S(2)}) copy-start(f32[768]{0:T(1024)} %param.23) | copy-start | bytes 9220
  35.0 1.5 %copy-start.14 = (s32[35]{0:T(128)S(1)}, s32[35]{0:T(128)}, u32[]{:S(2)}) copy-start(s32[35]{0:T(128)} %add.65) | copy-start | bytes 424
  44.5 1.1 %copy-start = (bf16[2,1152,128]{2,1,0:T(8,128)(2,1)S(1)}, bf16[2,1152,128]{2,1,0:T(8,128)(2,1)}, u32[]{:S(2)}) copy-start(bf16[2,1152,128]{2,1,0:T(8,128)(2,1)} %constant.56.clone.w_off) | copy-start | bytes 1769476
  44.5 1.2 %copy-start.1 = (bf16[256,768]{1,0:T(8,128)(2,1)S(1)}, bf16[256,768]{1,0:T(8,128)(2,1)}, u32[]{:S(2)}) copy-start(bf16[256,768]{1,0:T(8,128)(2,1)} %w_qkv.1) | copy-start | bytes 1179652
  44.5 1.2 %copy-start.2 = (f32[256,256]{1,0:T(8,128)S(1)}, f32[256,256]{1,0:T(8,128)}, u32[]{:S(2)}) copy-start(f32[256,256]{1,0:T(8,128)} %constant.58.clone.unmirror) | copy-start | bytes 786436
  44.5 1.3 %copy-start.3 = (bf16[256,320]{1,0:T(8,128)(2,1)S(1)}, bf16[256,320]{1,0:T(8,128)(2,1)}, u32[]{:S(2)}) copy-start(bf16[256,320]{1,0:T(8,128)(2,1)} %constant.57.clone.mirror) | copy-start | bytes 491524
  44.6 1.3 %copy-start.4 = (bf16[256,256]{1,0:T(8,128)(2,1)S(1)}, bf16[256,256]{1,0:T(8,128)(2,1)}, u32[]{:S(2)}) copy-start(bf16[256,256]{1,0:T(8,128)(2,1)} %w_out.1) | copy-start | bytes 393220
  44.6 1.3 %copy-start.5 = (f32[256]{0:T(256)S(1)}, f32[256]{0:T(256)}, u32[]{:S(2)}) copy-start(f32[256]{0:T(256)} %param.20) | copy-start | bytes 3076
  44.6 1.3 %copy-start.6 = (f32[256]{0:T(256)S(1)}, f32[256]{0:T(256)}, u32[]{:S(2)}) copy-start(f32[256]{0:T(256)} %param.21) | copy-start | bytes 3076
  44.6 1.3 %copy-start.7 = (f32[256]{0:T(256)S(1)}, f32[256]{0:T(256)}, u32[]{:S(2)}) copy-start(f32[256]{0:T(256)} %param.26) | copy-start | bytes 3076
  44.6 1.3 %copy-start.8 = (f32[256]{0:T(256)S(1)}, f32[256]{0:T(256)}, u32[]{:S(2)}) copy-start(f32[256]{0:T(256)} %param.28) | copy-start | bytes 3076

commit v2 on v1

v2 whole, which is shorter than its diff:
```python
import jax
import jax.numpy as jnp
import numpy as np
from jax import lax
from jax.experimental import pallas as pl
from jax.experimental.pallas import tpu as pltpu
from jax.sharding import PartitionSpec as P

C = 256
HEADS = 8
HEAD = 32
WIN = 8
SHIFT = 4
RADIUS = 8
SPAN = 2 * RADIUS + 1
OFFS = SPAN * SPAN
ROWS = 16
COLS = 32
HALO_A = 4
HALO_B = 12
HIGH_A, WIDE_A = 3, 5
HIGH_B, WIDE_B = 5, 7
CELLS = WIN * WIN
COUNT_A = HIGH_A * WIDE_A
COUNT_B = HIGH_B * WIDE_B
BLOCK = 640
TOTAL = (COUNT_A + COUNT_B) * CELLS
START_A = COUNT_B * CELLS
HALF = C // 2
GROUP = 25
PACKED = 5 * 128
KEYS = 64
GRAM = (ROWS + 2 * RADIUS) * KEYS
LOG2E = 1.4426950408889634
NT = (((1,), (1,)), ((), ()))


def swap(array, axis, step):
    peers = lax.axis_size(axis)
    pairs = [(i, (i ^ 1) if step == 0 else (i - 1 if i % 2 == 0 else i + 1) % peers) for i in range(peers)]
    return lax.ppermute(array, axis, pairs)


def dot(left, right):
    return jnp.dot(left, right, preferred_element_type=jnp.float32)


MID_A = WIDE_B * ROWS * WIN
MID = (WIDE_B + WIDE_A) * ROWS * WIN
SENT_B = HALO_B * WIN
SENT_A = HALO_A * WIN
SENT = WIDE_B * SENT_B + WIDE_A * SENT_A


def pack_cols(ids, a_ref, b_ref, near_ref, far_ref):
    even = ids[1] % 2 == 0
    for r in range(ROWS):
        a, b = a_ref[r].astype(jnp.float32), b_ref[r].astype(jnp.float32)
        first = jnp.concatenate([b[:HALO_B], a[:HALO_A]], axis=0)
        last = jnp.concatenate([b[-HALO_B:], a[-HALO_A:]], axis=0)
        near_ref[r] = jnp.where(even, last, first).astype(jnp.bfloat16)
        far_ref[r] = jnp.where(even, first, last).astype(jnp.bfloat16)


def pack_rows(ids, a_ref, b_ref, near_ref, far_ref, mid, up_ref, down_ref):
    even = ids[1] % 2 == 0
    for r in range(0, ROWS, 2):
        rows = []
        for k in range(2):
            near = near_ref[r + k].astype(jnp.float32)
            far = far_ref[r + k].astype(jnp.float32)
            before, after = jnp.where(even, far, near), jnp.where(even, near, far)
            a = a_ref[r + k].astype(jnp.float32)
            b = b_ref[r + k].astype(jnp.float32)
            b = jnp.concatenate([before[:HALO_B], b, after[:HALO_B]], axis=0)
            a = jnp.concatenate([before[HALO_B:], a, after[HALO_B:]], axis=0)
            rows.append(jnp.concatenate([b, a], axis=0))
        for j in range(WIDE_B + WIDE_A):
            part = slice(WIN * j, WIN * (j + 1))
            mid[(j * ROWS + r) * WIN : (j * ROWS + r + 2) * WIN] = jnp.concatenate(
                [rows[0][part], rows[1][part]], axis=0
            ).astype(jnp.bfloat16)

    def send(out, last):
        for j in range(WIDE_B):
            start = pl.multiple_of(j * ROWS * WIN + last * (ROWS * WIN - SENT_B), 16)
            out[j * SENT_B : (j + 1) * SENT_B] = mid[pl.ds(start, SENT_B)]
        for j in range(WIDE_A):
            start = pl.multiple_of(MID_A + j * ROWS * WIN + last * (ROWS * WIN - SENT_A), 16)
            at = WIDE_B * SENT_B + j * SENT_A
            out[at : at + SENT_A] = mid[pl.ds(start, SENT_A)]

    odd = ids[0] % 2
    send(up_ref, 1 - odd)
    send(down_ref, odd)


def body(
    ids,
    mid,
    near,
    far,
    gain,
    shift,
    w_k,
    b_k,
    w_qv,
    b_qv,
    bias,
    w_out,
    b_out,
    w_hid,
    w_off,
    b_hid,
    w_flow,
    b_flow,
    mirror,
    unmirror,
    out,
    x_all,
    q_s,
    k_s,
    v_s,
    mix_s,
    fb,
    fa,
    g_s,
    e_s,
):
    def place_rows(above, below):
        for j in range(WIDE_B + WIDE_A):
            if j < WIDE_B:
                at, sent, got = j * HIGH_B * CELLS, SENT_B, j * SENT_B
            else:
                at = START_A + (j - WIDE_B) * HIGH_A * CELLS
                sent, got = SENT_A, WIDE_B * SENT_B + (j - WIDE_B) * SENT_A
            own = ROWS * WIN
            x_all[at : at + sent] = above[got : got + sent]
            x_all[at + sent : at + sent + own] = mid[j * own : (j + 1) * own]
            x_all[at + sent + own : at + 2 * sent + own] = below[got : got + sent]

    even = ids[0] % 2 == 0

    @pl.when(even)
    def _():
        place_rows(far, near)

    @pl.when(jnp.logical_not(even))
    def _():
        place_rows(near, far)

    @pl.loop(0, TOTAL // BLOCK)
    def _(j):
        rows = pl.ds(pl.multiple_of(j * BLOCK, BLOCK), BLOCK)
        x = x_all[rows].astype(jnp.float32)
        centred = x - jnp.mean(x, axis=-1, keepdims=True)
        variance = jnp.mean(centred * centred, axis=-1, keepdims=True)
        normed = centred * lax.rsqrt(variance + 1e-05) * gain[...] + shift[...]
        normed = normed.astype(jnp.bfloat16)
        k_s[rows] = (dot(normed, w_k[...]) + b_k[...]).astype(jnp.bfloat16)
        qv = lax.dot_general(w_qv[...], normed, NT, preferred_element_type=jnp.float32)
        qv = qv + b_qv[...]
        q_s[:, rows] = (qv[:C] * (HEAD**-0.5 * LOG2E)).astype(jnp.bfloat16)
        v_s[:, rows] = qv[C:].astype(jnp.bfloat16)

    place = lax.broadcasted_iota(jnp.int32, (HALF, C), 0) // HEAD
    which = lax.broadcasted_iota(jnp.int32, (HALF, C), 1) // CELLS
    diagonal = (place == which).astype(jnp.float32).astype(jnp.bfloat16)
    low = lax.broadcasted_iota(jnp.int32, (HEAD, 128), 1) < CELLS


    def table_of(window):
        high, wide, inset = HIGH_B, WIDE_B, 1
        if window >= COUNT_B:
            window, high, wide, inset = window - COUNT_B, HIGH_A, WIDE_A, 0
        i, j = window % high, window // high
        index = 0
        for n, at, end in ((0, i, high - 1), (1, j, wide - 1)):
            if at == inset:
                index += (ids[n] == 0).astype(jnp.int32) * (n + 1)
            elif at == end - inset:
                index += (ids[n] == ids[n + 2] - 1).astype(jnp.int32) * (n + 1)
        return bias.at[index]

    def group(first):
        qs, vs, ks = [], [], []
        for u in range(GROUP):
            both = slice((first + u) * 128, (first + u + 1) * 128)
            queries, values = q_s[:, both], v_s[:, both]
            qs += [queries[:, :CELLS], queries[:, CELLS:]]
            vs += [values[:, :CELLS], values[:, CELLS:]]
            keys = k_s[both]
            ks += [keys[:CELLS], keys[CELLS:]]
        scores = []
        for w in range(2 * GROUP):
            for side in range(2):
                part = slice(HALF * side, HALF * (side + 1))
                spread = jnp.concatenate([qs[w][part]] * 4, axis=1) * diagonal
                scores.append(dot(ks[w][:, part], spread))
        weights, scales = [], []
        for w in range(2 * GROUP):
            table = table_of(2 * first + w)
            for side in range(2):
                s = scores[2 * w + side] + table[:, C * side : C * (side + 1)]
                p = jnp.exp2(s - jnp.max(s, axis=0, keepdims=True))
                scales.append(1.0 / jnp.sum(p, axis=0, keepdims=True))
                weights.append(p.astype(jnp.bfloat16))
        results = []
        for w in range(2 * GROUP):
            for side in range(2):
                part = slice(HALF * side, HALF * (side + 1))
                results.append(dot(vs[w][part], weights[2 * w + side]))
        for u in range(GROUP):
            mixed = []
            for head in range(HEADS):
                side, at = head // 4, head % 4
                rows = slice(HEAD * at, HEAD * (at + 1))
                cols = slice(128 * (at // 2), 128 * (at // 2 + 1))
                n = 4 * u + side
                a = results[n][rows, cols] * scales[n][:, cols]
                b = results[n + 2][rows, cols] * scales[n + 2][:, cols]
                if at % 2 == 0:
                    mixed.append(jnp.where(low, a, pltpu.roll(b, CELLS, 1)))
                else:
                    mixed.append(jnp.where(low, pltpu.roll(a, CELLS, 1), b))
            both = slice((first + u) * 128, (first + u + 1) * 128)
            mix_s[both] = jnp.concatenate(mixed, axis=0).T.astype(jnp.bfloat16)

    group(0)

    row_start = ids[0] * ROWS
    col_start = ids[1] * COLS
    total_rows = ids[2] * ROWS
    total_cols = ids[3] * COLS

    def features(x, mixed):
        attended = (dot(mixed, w_out[...]) + b_out[...]).astype(jnp.bfloat16)
        return x.astype(jnp.float32) + attended.astype(jnp.float32)

    col_places = col_start - HALO_B + lax.broadcasted_iota(jnp.int32, (KEYS, 1), 0)
    col_inside = (col_places >= 0) & (col_places < total_cols)
    blank = jnp.zeros((KEYS - WIDE_B * WIN, C), jnp.float32)

    def gather(ref, start, high, wide, i):
        return jnp.concatenate(
            [ref[pl.ds(start + (j * high + i) * CELLS, CELLS)] for j in range(wide)], axis=0
        )

    strips = [(0, HIGH_B, WIDE_B, i) for i in range(HIGH_B)]
    strips += [(START_A, HIGH_A, WIDE_A, i) for i in range(HIGH_A)]
    sums = [dot(gather(mix_s, *strip), w_out[...]) for strip in strips]
    for strip, total in zip(strips, sums):
        i = strip[-1]
        attended = (total + b_out[...]).astype(jnp.bfloat16)
        f = gather(x_all, *strip).astype(jnp.float32) + attended.astype(jnp.float32)
        if strip[0] == START_A:
            f = dot(mirror[...], f.astype(jnp.bfloat16)).astype(jnp.bfloat16)
            fa[i * WIN * COLS : (i + 1) * WIN * COLS] = f
            continue
        for r in range(WIN):
            row = jnp.concatenate(
                [f[CELLS * j + WIN * r : CELLS * j + WIN * (r + 1)] for j in range(WIDE_B)]
                + [blank],
                axis=0,
            )
            at = i * WIN + r
            place = row_start - HALO_B + at
            inside = col_inside & (place >= 0) & (place < total_rows)
            fb[at * KEYS : (at + 1) * KEYS] = jnp.where(inside, row, 0.0).astype(jnp.bfloat16)

    lane = lax.broadcasted_iota(jnp.int32, (COLS, 128), 1)
    near = lane % 32 < SPAN
    early = lane % KEYS < 32
    first = near & (lane < 32)
    second = near & (lane >= 32)

    for n in range(4):
        top, end = max(0, 8 * n - 16), min(ROWS, 8 * n + 8)
        queries = fa[(HALO_A + top) * COLS : (HALO_A + end) * COLS]
        start = (HALO_B - RADIUS + 8 * n) * KEYS
        keys = fb[start : start + 8 * KEYS]
        g_s[top * COLS : end * COLS, 8 * KEYS * n : 8 * KEYS * (n + 1)] = lax.dot_general(
            queries, keys, NT, preferred_element_type=jnp.float32
        )

    def align(r, n):
        at = 128 * (n + r // 2)
        tile = g_s[COLS * r : COLS * (r + 1), at : at + 128]
        turn = 128 - HALO_A - COLS + 1 - 32 * (n % 2)
        return pltpu.roll(tile, turn, 1, stride=1, stride_axis=0)

    for r in range(ROWS):
        tiles = []
        for n in range(5):
            tile = align(r, 2 * n)
            if n < 4:
                tile = jnp.where(early, tile, align(r, 2 * n + 1))
            keep = near
            if r % 2 == 0 and n == 4:
                keep = first
            if r % 2 == 1 and n == 0:
                keep = second
            if n == 4 and r % 2 == 1:
                keep = near & early
            tiles.append(jnp.where(keep, tile * (C**-0.5 * LOG2E), -1e30))
        most = tiles[0]
        for tile in tiles[1:]:
            most = jnp.maximum(most, tile)
        most = jnp.max(most, axis=-1, keepdims=True)
        rows = slice((r // 2) * COLS, (r // 2 + 1) * COLS)
        for n in range(5):
            e_s[r % 2, rows, 128 * n : 128 * (n + 1)] = jnp.exp2(tiles[n] - most).astype(
                jnp.bfloat16
            )

    sums = [dot(e_s[par], w_off[par]) for par in range(2)]
    hidden = [dot(e_s[par], w_hid[par]) for par in range(2)]
    flows = []
    for par in range(2):
        scale = 1.0 / sums[par][:, 2:3]
        act = jax.nn.gelu(hidden[par] * (scale * OFFS) + b_hid[...]).astype(jnp.bfloat16)
        flow = sums[par] * scale + dot(act, w_flow[...]) + b_flow[...]
        flows.append(flow.T[:WIN])
    flow = jnp.concatenate(flows, axis=0)
    high = flow.astype(jnp.bfloat16)
    rest = flow - high.astype(jnp.float32)
    mid = rest.astype(jnp.bfloat16)
    tail = (rest - mid.astype(jnp.float32)).astype(jnp.bfloat16)
    flow = dot(high, unmirror[...]) + dot(mid, unmirror[...]) + dot(tail, unmirror[...])
    for r in range(ROWS):
        at = WIN * (r % 2)
        out[:, r, :] = flow[at : at + 2, COLS * (r // 2) : COLS * (r // 2 + 1)]


def places():
    lanes = np.zeros((2, SPAN, SPAN), np.int64)
    for par in range(2):
        for dr in range(SPAN):
            row = dr + par
            tile, half = row // 2, row % 2
            slot = 2 * half if tile % 2 == 0 else 3 - 2 * half
            lanes[par, dr] = 128 * (tile // 2) + 32 * slot + np.arange(SPAN)
    return lanes.reshape(2, OFFS)


def skewed(w_hid):
    pick = np.zeros((2, PACKED, OFFS), np.float32)
    for par, lanes in enumerate(places()):
        pick[par, lanes, np.arange(OFFS)] = 1.0
    pick = jnp.asarray(pick.reshape(2 * PACKED, OFFS), jnp.bfloat16)
    return dot(pick, w_hid).astype(jnp.bfloat16).reshape(2, PACKED, C)


def offsets():
    table = np.zeros((2, PACKED, 128), np.float32)
    offs = np.arange(OFFS)
    for par, lanes in enumerate(places()):
        table[par, lanes, 0] = offs // SPAN - RADIUS
        table[par, lanes, 1] = offs % SPAN - RADIUS
        table[par, lanes, 2] = 1.0
    return jnp.asarray(table, jnp.bfloat16)


def mirrors():
    turn = np.zeros((WIN, COLS, WIDE_A, WIN, WIN), np.float32)
    for r in range(WIN):
        for c in range(COLS):
            place = HALO_A + COLS - 1 - c
            turn[r, c, place // WIN, r, place % WIN] = 1.0
    turn = jnp.asarray(turn.reshape(WIN * COLS, WIDE_A * CELLS), jnp.bfloat16)
    back = np.kron(np.eye(ROWS // 2, dtype=np.float32), np.eye(COLS, dtype=np.float32)[::-1])
    return turn, jnp.asarray(back, jnp.bfloat16)


def position_bias(rel_table):
    places = np.arange(CELLS)
    rows, cols = places // WIN, places % WIN
    index = (rows[:, None] - rows[None, :] + WIN - 1) * (2 * WIN - 1) + (
        cols[:, None] - cols[None, :] + WIN - 1
    )
    pick = np.zeros(((2 * WIN - 1) ** 2, CELLS * CELLS), np.float32)
    pick[index.reshape(-1), np.arange(CELLS * CELLS)] = 1.0
    pick = jnp.asarray(pick, jnp.bfloat16)
    high = rel_table.astype(jnp.bfloat16)
    rest = rel_table - high.astype(jnp.float32)
    mid = rest.astype(jnp.bfloat16)
    low = (rest - mid.astype(jnp.float32)).astype(jnp.bfloat16)
    table = jnp.sum(
        dot(jnp.concatenate([high, mid, low], axis=0), pick).reshape(3, HEADS, CELLS, CELLS),
        axis=0,
    )
    split_r = (rows[:, None] < SHIFT) != (rows[None, :] < SHIFT)
    split_c = (cols[:, None] < SHIFT) != (cols[None, :] < SHIFT)
    masks = np.stack([split_r & False, split_r, split_c, split_r | split_c])
    masks = jnp.asarray(np.where(masks, -100.0, 0.0), jnp.float32)
    full = (table.transpose(2, 0, 1)[None] + masks[:, :, None, :]) * LOG2E
    return full.reshape(4, CELLS, HEADS * CELLS)


def shards(
    section_a,
    section_b,
    ln_gain,
    ln_shift,
    w_qkv,
    b_qkv,
    rel_table,
    w_out,
    b_out,
    w_hid,
    b_hid,
    w_flow,
    b_flow,
):
    ids = jnp.stack(
        [
            lax.axis_index("row"),
            lax.axis_index("col"),
            jnp.int32(lax.axis_size("row")),
            jnp.int32(lax.axis_size("col")),
        ]
    )
    scalars = pl.BlockSpec(memory_space=pltpu.SMEM)
    whole = pl.BlockSpec(memory_space=pltpu.VMEM)
    strip = jax.ShapeDtypeStruct((ROWS, HALO_A + HALO_B, C), jnp.bfloat16)
    near, far = pl.pallas_call(
        pack_cols,
        out_shape=(strip, strip),
        in_specs=[scalars, whole, whole],
        out_specs=(whole, whole),
    )(ids, section_a, section_b)
    near, far = swap(near, "col", 0), swap(far, "col", 1)
    sent = jax.ShapeDtypeStruct((SENT, C), jnp.bfloat16)
    mid, near, far = pl.pallas_call(
        pack_rows,
        out_shape=(jax.ShapeDtypeStruct((MID, C), jnp.bfloat16), sent, sent),
        in_specs=[scalars] + [whole] * 4,
        out_specs=(whole,) * 3,
    )(ids, section_a, section_b, near, far)
    near, far = swap(near, "row", 0), swap(far, "row", 1)

    w_qv = jnp.concatenate([w_qkv[:, :C], w_qkv[:, 2 * C :]], axis=1).T
    b_qv = jnp.concatenate([b_qkv[:C], b_qkv[2 * C :]])[:, None]

    flow_pad = jnp.pad(w_flow, ((0, 0), (0, 126)))
    b_flow_pad = jnp.pad(b_flow, (0, 126))
    call = pl.pallas_call(
        body,
        out_shape=jax.ShapeDtypeStruct((2, ROWS, COLS), jnp.float32),
        in_specs=[scalars] + [whole] * 19,
        out_specs=whole,
        scratch_shapes=[
            pltpu.VMEM((TOTAL, C), jnp.bfloat16),
            pltpu.VMEM((C, TOTAL), jnp.bfloat16),
            pltpu.VMEM((TOTAL, C), jnp.bfloat16),
            pltpu.VMEM((C, TOTAL), jnp.bfloat16),
            pltpu.VMEM((TOTAL, C), jnp.bfloat16),
            pltpu.VMEM((HIGH_B * WIN * KEYS, C), jnp.bfloat16),
            pltpu.VMEM((HIGH_A * WIN * COLS, C), jnp.bfloat16),
            pltpu.VMEM((ROWS * COLS, GRAM), jnp.float32),
            pltpu.VMEM((2, ROWS // 2 * COLS, PACKED), jnp.bfloat16),
        ],
        compiler_params=pltpu.CompilerParams(vmem_limit_bytes=40 * 1024 * 1024),
    )
    return call(
        ids,
        mid,
        near,
        far,
        ln_gain[None],
        ln_shift[None],
        w_qkv[:, C : 2 * C],
        b_qkv[None, C : 2 * C],
        w_qv,
        b_qv,
        position_bias(rel_table),
        w_out,
        b_out[None],
        skewed(w_hid),
        offsets(),
        b_hid[None],
        flow_pad,
        b_flow_pad[None],
        *mirrors(),
    )


def solution(mesh):
    placed = (P("row", "col", None),) * 2 + (P(),) * 11
    return jax.shard_map(
        shards, mesh=mesh, in_specs=placed, out_specs=P(None, "row", "col"), check_vma=False
    )
```

time: 77.3 us -> 54.6 us (0.71)
  Pallas kernels: 31 us -> 17.1 us
  waiting for transfers between devices: 11.1 us -> 2.61 us
  matrix products: 1.99 us -> 3.68 us
  local copies, waits for them, and re-layouts: 7.52 us -> 5.86 us
    pallas_call x1 -> x3, Pallas kernels: 31 us -> 17.1 us  [the longest x1 12.7 us: shards(): call(ids, mid, near, far, ln_gain[None], ln_shift[None], w_qkv[:, C:2 * C...]
    ppermute x4, waiting for transfers between devices: 11.1 us -> 2.61 us  [swap(): return lax.ppermute(array, axis, pairs)]
    slice x10 -> x2, local copies, waits for them, and re-layouts: 2.1 us -> 0.03 us  [the longest x1 0.03 us: shards(): w_qv = jnp.concatenate([w_qkv[:, :C], w_qkv[:, 2 * C:]], axis=1).T]
    concatenate x6 -> x1, other arithmetic: 1.85 us -> 0.01 us  [shards(): b_qv = jnp.concatenate([b_qkv[:C], b_qkv[2 * C:]])[:, None]]
    dot_general x1 -> x2, matrix products: 1.99 us -> 3.68 us  [dot(): return jnp.dot(left, right, preferred_element_type=jnp.float32)]
    unnamed x35 -> x39, local copies, waits for them, and re-layouts: 2.56 us -> 4.06 us
    reshape x1 -> x0, local copies, waits for them, and re-layouts: 0.97 us -> none  [skewed(): w = w_hid.reshape(SPAN, SPAN, C)]
    pad x1, local copies, waits for them, and re-layouts: 0.02 us -> 0.86 us  [shards(): flow_pad = jnp.pad(w_flow, ((0, 0), (0, 126)))]
  transfers between devices with their start and end apart: 4 -> 4, of which waited for: 2 -> 1; matrix products, arithmetic and copies ran while one was open for 8% -> 18% of each run, Pallas kernels for 0% -> 0%
where the time goes in v2:
time: 54.6 us; the launch traced here: 54.2 us
  starting transfers between devices  22.1 us (40%)
  Pallas kernels  17.1 us (31%)
  local copies, waits for them, and re-layouts  5.86 us (11%)
  matrix products  3.68 us (7%)
  waiting for transfers between devices  2.61 us (5%)
  other arithmetic  2.51 us (5%)
    ppermute x4, starting transfers between devices, swap(): return lax.ppermute(array, axis, pairs)  22.1 us
    pallas_call x1, Pallas kernels, shards(): call(ids, mid, near, far, ln_gain[None], ln_shift[None], w_qkv[:, C:2 * C...  12.7 us
    unnamed x39, local copies, waits for them, and re-layouts  4.06 us
    dot_general x2, matrix products, dot(): return jnp.dot(left, right, preferred_element_type=jnp.float32)  3.68 us
    ppermute x4, waiting for transfers between devices, swap(): return lax.ppermute(array, axis, pairs)  2.61 us
    pallas_call x1, Pallas kernels, shards(): pl.pallas_call(pack_rows, out_shape=(jax.ShapeDtypeStruct((MID, C), jnp.b...  2.53 us
    pallas_call x1, Pallas kernels, shards(): pl.pallas_call(pack_cols, out_shape=(strip, strip), in_specs=[scalars, wh...  1.82 us
  transfers between devices with their start and end apart: 4, of which 1 were waited for; matrix products, arithmetic and copies ran while one was open for 18% of the time, Pallas kernels for 0%

profile of v2, /device:TPU:7, one launch (start us, length us, event | category | flops | bytes accessed | tf_op | source)
XLA Modules:
  0.0 54.2 jit_solution(11437323884887658668)
XLA Ops:
  0.0 0.6 %pad_add_fusion.ids = s32[4]{0:T(128)} fusion(s32[1]{0:T(128)} %constant.29.clone.1, s32[1]{0:T(128)} %constant.28.clone.1, s32[1]{0:T(128)} %bitcast.1, s32[1]{0:T(128)} %bitcast), kind=kLoop, calls=%fused_computation.9 | loop fusion | flops 12 | bytes 32 | tf_op jit(solution)/shard_map/stack | solution.py:415
  0.6 1.8 %shard_map.181 = (bf16[16,16,256]{2,1,0:T(8,128)(2,1)}, bf16[16,16,256]{2,1,0:T(8,128)(2,1)}) custom-call(s32[4]{0:T(128)} %pad_add_fusion.ids, bf16[16,32,256]{2,1,0:T(8,128)(2,1)} %a_ref.3, bf16[16,32,256]{2,1,0:T(8,128)(2,1)} %b_ref.3), custom_call_target="tpu_custom_call" | custom-call | tf_op jit(solution)/shard_map/pallas_call | solution.py:426
  2.4 3.2 %collective-permute-start = (bf16[16,16,256]{2,1,0:T(8,128)(2,1)}, bf16[16,16,256]{2,1,0:T(8,128)(2,1)S(1)}, u32[]{:S(2)}, u32[]{:S(2)}) collective-permute-start(bf16[16,16,256]{2,1,0:T(8,128)(2,1)} %get-tuple-element.10), channel_id=1, source_target_pairs={{0,1},{1,0},{2,3},{3,2},{4,5},{5,4},{6,7},{7,6},{8,9},{9,8},{10,11... | collective-permute-start | bytes 393224 | tf_op jit(solution)/shard_map/ppermute | solution.py:41
  5.6 11.0 %collective-permute-start.1 = (bf16[16,16,256]{2,1,0:T(8,128)(2,1)}, bf16[16,16,256]{2,1,0:T(8,128)(2,1)S(1)}, u32[]{:S(2)}, u32[]{:S(2)}) collective-permute-start(bf16[16,16,256]{2,1,0:T(8,128)(2,1)} %get-tuple-element.11), channel_id=1, source_target_pairs={{0,31},{1,2},{2,1},{3,4},{4,3},{5,6},{6,5},{7,8},{8,7},{9,10},{10,... | collective-permute-start | bytes 393224 | tf_op jit(solution)/shard_map/ppermute | solution.py:41
  16.6 0.8 %fusion.4 = (bf16[8,225]{1,0:T(8,128)(2,1)S(1)}, bf16[8,225]{1,0:T(8,128)(2,1)S(1)}, bf16[8,225]{1,0:T(8,128)(2,1)S(1)}) fusion(f32[8,225]{1,0:T(8,128)} %param.25), kind=kLoop, calls=%fused_computation.13 | loop fusion | flops 12600 | bytes 18000 | tf_op jit(solution)/shard_map/convert_element_type | solution.py:384
  17.4 2.0 %fusion = f32[24,4096]{1,0:T(8,128)S(1)} fusion(bf16[225,4096]{1,0:T(8,128)(2,1)} %constant.33.clone, bf16[8,225]{1,0:T(8,128)(2,1)S(1)} %get-tuple-element.19, bf16[8,225]{1,0:T(8,128)(2,1)S(1)} %get-tuple-element.20, bf16[8,225]{1,0:T(8,128)(2,1)S(1)} %get-tuple-element.18), kind=kOutput, calls=%fused_computation.4 | convolution fusion | flops 44269200 | bytes 2247216 | tf_op jit(solution)/shard_map/dot_general | solution.py:45
  19.4 0.3 reshape.12
  19.7 0.1 reduce_sum.9
  19.8 0.1 copy.29
  20.0 0.1 add.24
  20.0 0.0 copy-start.17
  20.1 0.3 add.25
  20.3 0.4 copy-done.11
  20.8 0.1 add_multiply_fusion.bias
  20.9 0.0 copy-start.2
  20.9 0.0 copy-start.3
  20.9 0.0 copy-start.5
  20.9 0.0 copy-start.7
  21.0 0.6 %copy-done.13 = bf16[16,16,256]{2,1,0:T(8,128)(2,1)} copy-done((bf16[16,16,256]{2,1,0:T(8,128)(2,1)}, bf16[16,16,256]{2,1,0:T(8,128)(2,1)S(1)}, u32[]{:S(2)}) %copy-start.13) | copy-done | bytes 131096
  21.7 0.7 %copy-done.14 = bf16[16,16,256]{2,1,0:T(8,128)(2,1)} copy-done((bf16[16,16,256]{2,1,0:T(8,128)(2,1)}, bf16[16,16,256]{2,1,0:T(8,128)(2,1)S(1)}, u32[]{:S(2)}) %copy-start.14) | copy-done | bytes 131096
  22.3 2.5 %shard_map.182 = (bf16[1536,256]{1,0:T(8,128)(2,1)}, bf16[832,256]{1,0:T(8,128)(2,1)}, bf16[832,256]{1,0:T(8,128)(2,1)}) custom-call(s32[4]{0:T(128)} %pad_add_fusion.ids, bf16[16,32,256]{2,1,0:T(8,128)(2,1)} %a_ref.3, bf16[16,32,256]{2,1,0:T(8,128)(2,1)} %b_ref.3, bf16[16,16,256]{2,1,0:T(8,128)(2,1)} %copy-done.13, bf16[16,16,256]{2,1,0:T(8,128)(2,1)} %copy-done.14), custom_call_target="tpu_custom_call" | custom-call | tf_op jit(solution)/shard_map/pallas_call | solution.py:434
  24.8 3.3 %collective-permute-start.2 = (bf16[832,256]{1,0:T(8,128)(2,1)}, bf16[832,256]{1,0:T(8,128)(2,1)S(1)}, u32[]{:S(2)}, u32[]{:S(2)}) collective-permute-start(bf16[832,256]{1,0:T(8,128)(2,1)} %get-tuple-element.13), channel_id=1, source_target_pairs={{0,32},{32,0},{64,96},{96,64},{128,160},{160,128},{192,224},{224,1... | collective-permute-start | bytes 1277960 | tf_op jit(solution)/shard_map/ppermute | solution.py:41
  28.1 4.6 %collective-permute-start.3 = (bf16[832,256]{1,0:T(8,128)(2,1)}, bf16[832,256]{1,0:T(8,128)(2,1)S(1)}, u32[]{:S(2)}, u32[]{:S(2)}) collective-permute-start(bf16[832,256]{1,0:T(8,128)(2,1)} %get-tuple-element.14), channel_id=1, source_target_pairs={{0,480},{32,64},{64,32},{96,128},{128,96},{160,192},{192,160},{224... | collective-permute-start | bytes 1277960 | tf_op jit(solution)/shard_map/ppermute | solution.py:41
  32.8 0.8 %copy.32 = bf16[256,256]{0,1:T(8,128)(2,1)} copy(bf16[256,256]{1,0:T(8,128)(2,1)S(1)} %get-tuple-element.15) | data formatting | bytes 262144
  33.5 0.8 %copy.33 = bf16[256,256]{0,1:T(8,128)(2,1)} copy(bf16[256,256]{1,0:T(8,128)(2,1)S(1)} %get-tuple-element.17) | data formatting | bytes 262144
  34.3 0.1 copy.31.b_qv
  34.5 0.8 %copy.30 = bf16[256,2]{1,0:T(8,128)(2,1)} copy(bf16[256,2]{0,1:T(2,128)(2,1)S(1)} %copy-done.16) | data formatting | bytes 2048 | tf_op args[11]
  35.2 0.9 %pad.8.w_flow = bf16[256,128]{1,0:T(8,128)(2,1)S(1)} pad(bf16[256,2]{1,0:T(8,128)(2,1)} %copy.30, bf16[]{:T(256)} %constant.32.clone.1), padding=0_0x0_126 | pad | bytes 66562 | tf_op jit(solution)/shard_map/jit(_pad)/pad | solution.py:445
  36.1 1.0 %maximum_bitcast_fusion.w_qv = bf16[512,256]{1,0:T(8,128)(2,1)S(1)} fusion(bf16[256,256]{0,1:T(8,128)(2,1)} %copy.33, bf16[256,256]{0,1:T(8,128)(2,1)} %copy.32), kind=kLoop, calls=%fused_computation.2 | loop fusion | flops 524288 | bytes 524288 | tf_op jit(solution)/shard_map/transpose | solution.py:442
  37.1 1.7 %convolution_convert_fusion = bf16[1280,256]{1,0:T(8,128)(2,1)S(1)} fusion(bf16[1280,289]{1,0:T(8,128)(2,1)} %constant.35.clone, bf16[289,256]{1,0:T(8,128)(2,1)S(1)} %copy-done), kind=kOutput, calls=%fused_computation | convolution fusion | flops 189726720 | bytes 1543168 | tf_op jit(solution)/shard_map/dot_general | solution.py:45
  38.8 2.6 %collective-permute-done.3.far = bf16[832,256]{1,0:T(8,128)(2,1)S(1)} collective-permute-done((bf16[832,256]{1,0:T(8,128)(2,1)}, bf16[832,256]{1,0:T(8,128)(2,1)S(1)}, u32[]{:S(2)}, u32[]{:S(2)}) %collective-permute-start.3) | collective-permute-done | bytes 426016 | tf_op jit(solution)/shard_map/ppermute | solution.py:41
  41.5 12.7 %shard_map.183 = f32[2,16,32]{2,1,0:T(8,128)} custom-call(s32[4]{0:T(128)S(1)} %copy-done.6, bf16[1536,256]{1,0:T(8,128)(2,1)S(1)} %copy-done.1, bf16[832,256]{1,0:T(8,128)(2,1)S(1)} %collective-permute-done.2.near, bf16[832,256]{1,0:T(8,128)(2,1)S(1)} %collective-permute-done.3.far, f32[1,256]{1,0:T(1,128)S(1)} %bitcast.23, f32[1,256]{1,0:T(1,128)S(1)} %bitcast.24, ...), custom_call_target="tpu_custom_call" | custom-call | tf_op jit(solution)/shard_map/pallas_call | solution.py:465
  (35 shorter events, 0.1 us)
Async XLA Ops:
  0.0 37.1 %copy-start = (bf16[289,256]{1,0:T(8,128)(2,1)S(1)}, bf16[289,256]{1,0:T(8,128)(2,1)}, u32[]{:S(2)}) copy-start(bf16[289,256]{1,0:T(8,128)(2,1)} %param.28) | copy-start | bytes 443908
  2.4 18.6 %collective-permute-start = (bf16[16,16,256]{2,1,0:T(8,128)(2,1)}, bf16[16,16,256]{2,1,0:T(8,128)(2,1)S(1)}, u32[]{:S(2)}, u32[]{:S(2)}) collective-permute-start(bf16[16,16,256]{2,1,0:T(8,128)(2,1)} %get-tuple-element.10), channel_id=1, source_target_pairs={{0,1},{1,0},{2,3},{3,2},{4,5},{5,4},{6,7},{7,6},{8,9},{9,8},{10,11... | collective-permute-start | bytes 393224 | tf_op jit(solution)/shard_map/ppermute | solution.py:41
  5.6 15.4 %collective-permute-start.1 = (bf16[16,16,256]{2,1,0:T(8,128)(2,1)}, bf16[16,16,256]{2,1,0:T(8,128)(2,1)S(1)}, u32[]{:S(2)}, u32[]{:S(2)}) collective-permute-start(bf16[16,16,256]{2,1,0:T(8,128)(2,1)} %get-tuple-element.11), channel_id=1, source_target_pairs={{0,31},{1,2},{2,1},{3,4},{4,3},{5,6},{6,5},{7,8},{8,7},{9,10},{10,... | collective-permute-start | bytes 393224 | tf_op jit(solution)/shard_map/ppermute | solution.py:41
  17.4 2.5 %copy-start.12 = (f32[4,64,64]{2,1,0:T(8,128)S(1)}, f32[4,64,64]{2,1,0:T(8,128)}, u32[]{:S(2)}) copy-start(f32[4,64,64]{2,1,0:T(8,128)} %constant.34.clone) | copy-start | bytes 196612
  19.7 1.0 %copy-start.11 = (bf16[256,768]{1,0:T(8,128)(2,1)S(1)}, bf16[256,768]{1,0:T(8,128)(2,1)}, u32[]{:S(2)}) copy-start(bf16[256,768]{1,0:T(8,128)(2,1)} %param.23) | copy-start | bytes 1179652
  20.0 0.8 %copy-start.15 = (f32[768]{0:T(1024)S(1)}, f32[768]{0:T(1024)}, u32[]{:S(2)}) copy-start(f32[768]{0:T(1024)} %param.24) | copy-start | bytes 9220
  20.0 12.7 %copy-start.17 = (f32[2]{0:T(128)S(1)}, f32[2]{0:T(128)}, u32[]{:S(2)}) copy-start(f32[2]{0:T(128)} %param.31) | copy-start | bytes 28
  20.7 13.7 %copy-start.16 = (bf16[256,2]{0,1:T(2,128)(2,1)S(1)}, bf16[256,2]{0,1:T(2,128)(2,1)}, u32[]{:S(2)}) copy-start(bf16[256,2]{0,1:T(2,128)(2,1)} %param.30) | copy-start | bytes 3076
  20.9 20.5 %copy-start.2 = (bf16[2,640,128]{2,1,0:T(8,128)(2,1)S(1)}, bf16[2,640,128]{2,1,0:T(8,128)(2,1)}, u32[]{:S(2)}) copy-start(bf16[2,640,128]{2,1,0:T(8,128)(2,1)} %constant.36.clone.w_off) | copy-start | bytes 983044
  20.9 20.5 %copy-start.3 = (bf16[256,320]{1,0:T(8,128)(2,1)S(1)}, bf16[256,320]{1,0:T(8,128)(2,1)}, u32[]{:S(2)}) copy-start(bf16[256,320]{1,0:T(8,128)(2,1)} %constant.37.clone.mirror) | copy-start | bytes 491524
  20.9 20.5 %copy-start.4 = (bf16[256,256]{1,0:T(8,128)(2,1)S(1)}, bf16[256,256]{1,0:T(8,128)(2,1)}, u32[]{:S(2)}) copy-start(bf16[256,256]{1,0:T(8,128)(2,1)} %w_out.1) | copy-start | bytes 393220
  20.9 20.5 %copy-start.5 = (bf16[256,256]{1,0:T(8,128)(2,1)S(1)}, bf16[256,256]{1,0:T(8,128)(2,1)}, u32[]{:S(2)}) copy-start(bf16[256,256]{1,0:T(8,128)(2,1)} %constant.38.clone.unmirror) | copy-start | bytes 393220
  20.9 20.5 %copy-start.6 = (s32[4]{0:T(128)S(1)}, s32[4]{0:T(128)}, u32[]{:S(2)}) copy-start(s32[4]{0:T(128)} %pad_add_fusion.ids) | copy-start | bytes 52
  20.9 20.5 %copy-start.7 = (f32[256]{0:T(256)S(1)}, f32[256]{0:T(256)}, u32[]{:S(2)}) copy-start(f32[256]{0:T(256)} %param.21) | copy-start | bytes 3076
  20.9 20.5 %copy-start.8 = (f32[256]{0:T(256)S(1)}, f32[256]{0:T(256)}, u32[]{:S(2)}) copy-start(f32[256]{0:T(256)} %param.22) | copy-start | bytes 3076
  21.0 20.5 %copy-start.9 = (f32[256]{0:T(256)S(1)}, f32[256]{0:T(256)}, u32[]{:S(2)}) copy-start(f32[256]{0:T(256)} %param.27) | copy-start | bytes 3076
  21.0 20.5 %copy-start.10 = (f32[256]{0:T(256)S(1)}, f32[256]{0:T(256)}, u32[]{:S(2)}) copy-start(f32[256]{0:T(256)} %param.29) | copy-start | bytes 3076
  21.0 0.7 %copy-start.13 = (bf16[16,16,256]{2,1,0:T(8,128)(2,1)}, bf16[16,16,256]{2,1,0:T(8,128)(2,1)S(1)}, u32[]{:S(2)}) copy-start(bf16[16,16,256]{2,1,0:T(8,128)(2,1)S(1)} %collective-permute-done.near_ref) | copy-start | bytes 393220
  21.7 0.7 %copy-start.14 = (bf16[16,16,256]{2,1,0:T(8,128)(2,1)}, bf16[16,16,256]{2,1,0:T(8,128)(2,1)S(1)}, u32[]{:S(2)}) copy-start(bf16[16,16,256]{2,1,0:T(8,128)(2,1)S(1)} %collective-permute-done.1.far_ref) | copy-start | bytes 393220
  24.8 16.6 %copy-start.1 = (bf16[1536,256]{1,0:T(8,128)(2,1)S(1)}, bf16[1536,256]{1,0:T(8,128)(2,1)}, u32[]{:S(2)}) copy-start(bf16[1536,256]{1,0:T(8,128)(2,1)} %get-tuple-element.12.mid) | copy-start | bytes 2359300
  24.8 13.9 %collective-permute-start.2 = (bf16[832,256]{1,0:T(8,128)(2,1)}, bf16[832,256]{1,0:T(8,128)(2,1)S(1)}, u32[]{:S(2)}, u32[]{:S(2)}) collective-permute-start(bf16[832,256]{1,0:T(8,128)(2,1)} %get-tuple-element.13), channel_id=1, source_target_pairs={{0,32},{32,0},{64,96},{96,64},{128,160},{160,128},{192,224},{224,1... | collective-permute-start | bytes 1277960 | tf_op jit(solution)/shard_map/ppermute | solution.py:41
  28.1 13.3 %collective-permute-start.3 = (bf16[832,256]{1,0:T(8,128)(2,1)}, bf16[832,256]{1,0:T(8,128)(2,1)S(1)}, u32[]{:S(2)}, u32[]{:S(2)}) collective-permute-start(bf16[832,256]{1,0:T(8,128)(2,1)} %get-tuple-element.14), channel_id=1, source_target_pairs={{0,480},{32,64},{64,32},{96,128},{128,96},{160,192},{192,160},{224... | collective-permute-start | bytes 1277960 | tf_op jit(solution)/shard_map/ppermute | solution.py:41

commit v3 on v2

v3 whole, which is shorter than its diff:
```python
import jax
import jax.numpy as jnp
from jax import lax
from jax.experimental import pallas as pl
from jax.experimental.pallas import tpu as pltpu
from jax.sharding import PartitionSpec as P

C = 256
HEADS = 8
HEAD = 32
WIN = 8
SHIFT = 4
RADIUS = 8
SPAN = 2 * RADIUS + 1
OFFS = SPAN * SPAN
ROWS = 16
COLS = 32
HALO_A = 4
HALO_B = 12
HIGH_A, WIDE_A = 3, 5
HIGH_B, WIDE_B = 5, 7
CELLS = WIN * WIN
STRIPS_A, STRIPS_B = (0, 2), (0, 1, 3, 4)
LEFT_A, LEFT_B = len(STRIPS_A), len(STRIPS_B)
START_A = LEFT_B * WIDE_B * CELLS
TOTAL = START_A + LEFT_A * WIDE_A * CELLS
HALF = C // 2
PACKED = 5 * 128
KEYS = 64
GRAM = (ROWS + 2 * RADIUS) * KEYS
LOG2E = 1.4426950408889634
NT = (((1,), (1,)), ((), ()))


def swap(array, axis, step):
    peers = lax.axis_size(axis)
    pairs = [(i, (i ^ 1) if step == 0 else (i - 1 if i % 2 == 0 else i + 1) % peers) for i in range(peers)]
    return lax.ppermute(array, axis, pairs)


def dot(left, right):
    return jnp.dot(left, right, preferred_element_type=jnp.float32)


MID_A = WIDE_B * ROWS * WIN
MID = (WIDE_B + WIDE_A) * ROWS * WIN
SENT_B = HALO_B * WIN
SENT_A = HALO_A * WIN
SENT = WIDE_B * SENT_B + WIDE_A * SENT_A


def pack_cols(ids, a_ref, b_ref, far_ref, near_ref):
    even = ids[1] % 2 == 0
    for r in range(ROWS):
        a, b = a_ref[r].astype(jnp.float32), b_ref[r].astype(jnp.float32)
        first = jnp.concatenate([b[:HALO_B], a[:HALO_A]], axis=0)
        last = jnp.concatenate([b[-HALO_B:], a[-HALO_A:]], axis=0)
        near_ref[r] = jnp.where(even, last, first).astype(jnp.bfloat16)
        far_ref[r] = jnp.where(even, first, last).astype(jnp.bfloat16)


def pack_rows(ids, a_ref, b_ref, far_ref, near_ref, mid, down_ref, up_ref):
    even = ids[1] % 2 == 0
    for r in range(0, ROWS, 2):
        rows = []
        for k in range(2):
            near = near_ref[r + k].astype(jnp.float32)
            far = far_ref[r + k].astype(jnp.float32)
            before, after = jnp.where(even, far, near), jnp.where(even, near, far)
            a = a_ref[r + k].astype(jnp.float32)
            b = b_ref[r + k].astype(jnp.float32)
            b = jnp.concatenate([before[:HALO_B], b, after[:HALO_B]], axis=0)
            a = jnp.concatenate([before[HALO_B:], a, after[HALO_B:]], axis=0)
            rows.append(jnp.concatenate([b, a], axis=0))
        for j in range(WIDE_B + WIDE_A):
            part = slice(WIN * j, WIN * (j + 1))
            mid[(j * ROWS + r) * WIN : (j * ROWS + r + 2) * WIN] = jnp.concatenate(
                [rows[0][part], rows[1][part]], axis=0
            ).astype(jnp.bfloat16)

    def send(out, last):
        for j in range(WIDE_B):
            start = pl.multiple_of(j * ROWS * WIN + last * (ROWS * WIN - SENT_B), 16)
            out[j * SENT_B : (j + 1) * SENT_B] = mid[pl.ds(start, SENT_B)]
        for j in range(WIDE_A):
            start = pl.multiple_of(MID_A + j * ROWS * WIN + last * (ROWS * WIN - SENT_A), 16)
            at = WIDE_B * SENT_B + j * SENT_A
            out[at : at + SENT_A] = mid[pl.ds(start, SENT_A)]

    odd = ids[0] % 2
    send(up_ref, 1 - odd)
    send(down_ref, odd)


def normalise(x, gain, shift):
    x = x.astype(jnp.float32)
    centred = x - jnp.mean(x, axis=-1, keepdims=True)
    variance = jnp.mean(centred * centred, axis=-1, keepdims=True)
    normed = centred * lax.rsqrt(variance + 1e-05) * gain[...] + shift[...]
    return normed.astype(jnp.bfloat16)


def project(normed, rows, w_qkv, b_qkv, w_qv, b_qv, q_s, k_s, v_s):
    k_s[rows] = (dot(normed, w_qkv[:, C : 2 * C]) + b_qkv[:, C : 2 * C]).astype(jnp.bfloat16)
    qv = lax.dot_general(w_qv[...], normed, NT, preferred_element_type=jnp.float32)
    qv = qv + b_qv[:, :1]
    q_s[:, rows] = (qv[:C] * (HEAD**-0.5 * LOG2E)).astype(jnp.bfloat16)
    v_s[:, rows] = qv[C:].astype(jnp.bfloat16)


def table_of(ids, bias, i, j, high, wide, inset):
    index = 0
    for n, at, end in ((0, i, high - 1), (1, j, wide - 1)):
        if at == inset:
            index += (ids[n] == 0).astype(jnp.int32) * (n + 1)
        elif at == end - inset:
            index += (ids[n] == ids[n + 2] - 1).astype(jnp.int32) * (n + 1)
    return bias.at[index]


def attend(tables, q_s, k_s, v_s, mix_s):
    place = lax.broadcasted_iota(jnp.int32, (HALF, C), 0) // HEAD
    which = lax.broadcasted_iota(jnp.int32, (HALF, C), 1) // CELLS
    diagonal = (place == which).astype(jnp.float32).astype(jnp.bfloat16)
    low = lax.broadcasted_iota(jnp.int32, (HEAD, 128), 1) < CELLS
    pairs = [slice(128 * u, 128 * (u + 1)) for u in range(len(tables) // 2)]
    sides = [slice(HALF * side, HALF * (side + 1)) for side in range(2)]
    qs, ks, vs = [], [], []
    for both in pairs:
        queries, values, keys = q_s[:, both], v_s[:, both], k_s[both]
        qs += [queries[:, :CELLS], queries[:, CELLS:]]
        vs += [values[:, :CELLS], values[:, CELLS:]]
        ks += [keys[:CELLS], keys[CELLS:]]
    scores = []
    for q, k in zip(qs, ks):
        for part in sides:
            spread = jnp.concatenate([q[part]] * 4, axis=1) * diagonal
            scores.append(dot(k[:, part], spread))
    weights, scales = [], []
    for w, table in enumerate(tables):
        for side in range(2):
            s = scores[2 * w + side] + table[:, C * side : C * (side + 1)]
            p = jnp.exp2(s - jnp.max(s, axis=0, keepdims=True))
            scales.append(1.0 / jnp.sum(p, axis=0, keepdims=True))
            weights.append(p.astype(jnp.bfloat16))
    results = []
    for w, v in enumerate(vs):
        for side, part in enumerate(sides):
            results.append(dot(v[part], weights[2 * w + side]))
    for u, both in enumerate(pairs):
        mixed = []
        for head in range(HEADS):
            side, at = head // 4, head % 4
            rows = slice(HEAD * at, HEAD * (at + 1))
            cols = slice(128 * (at // 2), 128 * (at // 2 + 1))
            n = 4 * u + side
            a = results[n][rows, cols] * scales[n][:, cols]
            b = results[n + 2][rows, cols] * scales[n + 2][:, cols]
            if at % 2 == 0:
                mixed.append(jnp.where(low, a, pltpu.roll(b, CELLS, 1)))
            else:
                mixed.append(jnp.where(low, pltpu.roll(a, CELLS, 1), b))
        mix_s[both] = jnp.concatenate(mixed, axis=0).T.astype(jnp.bfloat16)


def column(ref, start, high, wide, t):
    return jnp.concatenate(
        [ref[start + (j * high + t) * CELLS : start + (j * high + t + 1) * CELLS] for j in range(wide)],
        axis=0,
    )


def finish(ids, x, total, b_out, mirror, strip, out, at):
    f = x.astype(jnp.float32) + (total + b_out[...]).astype(jnp.bfloat16).astype(jnp.float32)
    if strip is None:
        out[at : at + WIN * COLS] = dot(mirror[...], f.astype(jnp.bfloat16)).astype(jnp.bfloat16)
        return
    row_start, col_start = ids[0] * ROWS - HALO_B, ids[1] * COLS - HALO_B
    col_places = col_start + lax.broadcasted_iota(jnp.int32, (KEYS, 1), 0)
    col_inside = (col_places >= 0) & (col_places < ids[3] * COLS)
    blank = jnp.zeros((KEYS - WIDE_B * WIN, C), jnp.float32)
    for r in range(WIN):
        row = jnp.concatenate(
            [f[CELLS * j + WIN * r : CELLS * j + WIN * (r + 1)] for j in range(WIDE_B)] + [blank],
            axis=0,
        )
        place = row_start + strip * WIN + r
        inside = col_inside & (place >= 0) & (place < ids[2] * ROWS)
        out[at + r * KEYS : at + (r + 1) * KEYS] = jnp.where(inside, row, 0.0).astype(jnp.bfloat16)


def centre(
    ids, mid, gain, shift, w_qkv, b_qkv, w_qv, b_qv, bias, w_out, b_out, mirror,
    outer, fb, fa, q_s, k_s, v_s, mix_s,
):
    x_s = []
    for j in range(0, WIDE_B + WIDE_A, 4):
        inner = []
        for n in range(j, j + 4):
            at = n * ROWS * WIN
            normed = normalise(mid[at : at + ROWS * WIN], gain, shift)
            outer[n * CELLS : n * CELLS + SENT_A] = normed[:SENT_A]
            outer[n * CELLS + SENT_A : (n + 1) * CELLS] = normed[-SENT_A:]
            inner.append(normed[SENT_A:-SENT_A])
            x_s.append(mid[at + SENT_A : at + SENT_A + CELLS])
        rows = slice(j * CELLS, (j + 4) * CELLS)
        project(jnp.concatenate(inner, axis=0), rows, w_qkv, b_qkv, w_qv, b_qv, q_s, k_s, v_s)
    tables = [table_of(ids, bias, 2, j, HIGH_B, WIDE_B, 1) for j in range(WIDE_B)]
    tables += [table_of(ids, bias, 1, j, HIGH_A, WIDE_A, 0) for j in range(WIDE_A)]
    attend(tables, q_s, k_s, v_s, mix_s)
    cut = WIDE_B * CELLS
    sum_b, sum_a = dot(mix_s[:cut], w_out[...]), dot(mix_s[cut:], w_out[...])
    finish(ids, jnp.concatenate(x_s[:WIDE_B], axis=0), sum_b, b_out, mirror, 2, fb, 0)
    finish(ids, jnp.concatenate(x_s[WIDE_B:], axis=0), sum_a, b_out, mirror, None, fa, 0)


def body(
    ids,
    mid,
    far,
    near,
    outer,
    centre_b,
    centre_a,
    gain,
    shift,
    w_qkv,
    b_qkv,
    w_qv,
    b_qv,
    bias,
    w_out,
    b_out,
    w_hid,
    w_off,
    b_hid,
    w_flow,
    b_flow,
    mirror,
    unmirror,
    out,
    x_s,
    q_s,
    k_s,
    v_s,
    mix_s,
    fb,
    fa,
    g_s,
    e_s,
):
    def spans():
        for j in range(WIDE_B + WIDE_A):
            if j < WIDE_B:
                yield j, j * LEFT_B * CELLS, SENT_B, j * SENT_B
            else:
                n = j - WIDE_B
                yield j, START_A + n * LEFT_A * CELLS, SENT_A, WIDE_B * SENT_B + n * SENT_A

    def place_rows(above, below):
        for j, at, sent, got in spans():
            own = j * ROWS * WIN
            x_s[at : at + sent] = above[got : got + sent]
            x_s[at + sent : at + sent + SENT_A] = mid[own : own + SENT_A]
            x_s[at + sent + SENT_A : at + sent + CELLS] = mid[
                own + ROWS * WIN - SENT_A : own + ROWS * WIN
            ]
            x_s[at + sent + CELLS : at + 2 * sent + CELLS] = below[got : got + sent]

    even = ids[0] % 2 == 0

    @pl.when(even)
    def _():
        place_rows(far, near)

    @pl.when(jnp.logical_not(even))
    def _():
        place_rows(near, far)

    normed, start = [], 0
    for j, at, sent, _ in spans():
        top = normalise(x_s[at : at + sent], gain, shift)
        low = normalise(x_s[at + sent + CELLS : at + 2 * sent + CELLS], gain, shift)
        normed += [top, outer[j * CELLS : (j + 1) * CELLS], low]
        end = at + 2 * sent + CELLS
        if j % 2 == 1 or j == WIDE_B + WIDE_A - 1:
            rows = slice(start, end)
            project(jnp.concatenate(normed, axis=0), rows, w_qkv, b_qkv, w_qv, b_qv, q_s, k_s, v_s)
            normed, start = [], end

    tables = [
        table_of(ids, bias, i, j, HIGH_B, WIDE_B, 1) for j in range(WIDE_B) for i in STRIPS_B
    ] + [table_of(ids, bias, i, j, HIGH_A, WIDE_A, 0) for j in range(WIDE_A) for i in STRIPS_A]
    attend(tables, q_s, k_s, v_s, mix_s)

    strips = [(0, LEFT_B, WIDE_B, t) for t in range(LEFT_B)]
    strips += [(START_A, LEFT_A, WIDE_A, t) for t in range(LEFT_A)]
    sums = [dot(column(mix_s, *strip), w_out[...]) for strip in strips]
    for strip, total in zip(strips, sums):
        x, t = column(x_s, *strip), strip[-1]
        if strip[0] == START_A:
            finish(ids, x, total, b_out, mirror, None, fa, STRIPS_A[t] * WIN * COLS)
        else:
            i = STRIPS_B[t]
            finish(ids, x, total, b_out, mirror, i, fb, i * WIN * KEYS)
    fb[2 * WIN * KEYS : 3 * WIN * KEYS] = centre_b[...]
    fa[WIN * COLS : 2 * WIN * COLS] = centre_a[...]

    lane = lax.broadcasted_iota(jnp.int32, (COLS, 128), 1)
    valid = lane % 32 < SPAN
    early = lane % KEYS < 32
    first = valid & (lane < 32)
    second = valid & (lane >= 32)

    for n in range(4):
        top, end = max(0, 8 * n - 16), min(ROWS, 8 * n + 8)
        queries = fa[(HALO_A + top) * COLS : (HALO_A + end) * COLS]
        start = (HALO_B - RADIUS + 8 * n) * KEYS
        keys = fb[start : start + 8 * KEYS]
        g_s[top * COLS : end * COLS, 8 * KEYS * n : 8 * KEYS * (n + 1)] = lax.dot_general(
            queries, keys, NT, preferred_element_type=jnp.float32
        )

    def align(r, n):
        at = 128 * (n + r // 2)
        tile = g_s[COLS * r : COLS * (r + 1), at : at + 128]
        turn = 128 - HALO_A - COLS + 1 - 32 * (n % 2)
        return pltpu.roll(tile, turn, 1, stride=1, stride_axis=0)

    for r in range(ROWS):
        tiles = []
        for n in range(5):
            tile = align(r, 2 * n)
            if n < 4:
                tile = jnp.where(early, tile, align(r, 2 * n + 1))
            keep = valid
            if r % 2 == 0 and n == 4:
                keep = first
            if r % 2 == 1 and n == 0:
                keep = second
            if n == 4 and r % 2 == 1:
                keep = valid & early
            tiles.append(jnp.where(keep, tile * (C**-0.5 * LOG2E), -1e30))
        most = tiles[0]
        for tile in tiles[1:]:
            most = jnp.maximum(most, tile)
        most = jnp.max(most, axis=-1, keepdims=True)
        rows = slice((r // 2) * COLS, (r // 2 + 1) * COLS)
        for n in range(5):
            e_s[r % 2, rows, 128 * n : 128 * (n + 1)] = jnp.exp2(tiles[n] - most).astype(
                jnp.bfloat16
            )

    sums = [dot(e_s[par], w_off[par * PACKED : (par + 1) * PACKED]) for par in range(2)]
    hidden = [dot(e_s[par], w_hid[par * PACKED : (par + 1) * PACKED]) for par in range(2)]
    flows = []
    for par in range(2):
        scale = 1.0 / sums[par][:, 2:3]
        act = jax.nn.gelu(hidden[par] * (scale * OFFS) + b_hid[...]).astype(jnp.bfloat16)
        flow = sums[par] * scale + dot(act, w_flow[...]) + b_flow[...]
        flows.append(flow.T[:WIN])
    flow = jnp.concatenate(flows, axis=0)
    high = flow.astype(jnp.bfloat16)
    rest = flow - high.astype(jnp.float32)
    mid = rest.astype(jnp.bfloat16)
    tail = (rest - mid.astype(jnp.float32)).astype(jnp.bfloat16)
    flow = dot(high, unmirror[...]) + dot(mid, unmirror[...]) + dot(tail, unmirror[...])
    for r in range(ROWS):
        at = WIN * (r % 2)
        out[:, r, :] = flow[at : at + 2, COLS * (r // 2) : COLS * (r // 2 + 1)]


def prepare(
    w_qkv, b_qkv, w_hid, w_flow, b_flow, rel,
    w_qv, b_qv, packed, flow_w, flow_b, bias, w_off, turn, back,
):
    def iota(shape, dim):
        return lax.broadcasted_iota(jnp.int32, shape, dim)

    def onehot(hit):
        return hit.astype(jnp.float32).astype(jnp.bfloat16)

    lane = iota((2 * PACKED, 1), 0)
    par = (lane >= PACKED).astype(jnp.int32)
    lane = lane - par * PACKED
    slot, dc = lane % 128 // 32, lane % 32
    dr = lane // 128 * 4 + jnp.where(slot == 1, 3, jnp.where(slot == 3, 2, slot // 2)) - par
    inside = (dr >= 0) & (dr < SPAN) & (dc < SPAN)
    place = jnp.where(inside, dr * SPAN + dc, -1)
    pick = onehot(iota((2 * PACKED, OFFS), 1) == place)
    which = iota((2 * PACKED, 128), 1)
    offs = jnp.where(which == 0, dr - RADIUS, jnp.where(which == 1, dc - RADIUS, 1))
    offs = jnp.where(inside & (which < 3), offs, 0)
    w_off[...] = offs.astype(jnp.float32).astype(jnp.bfloat16)
    at = iota(turn.shape, 0)
    col = HALO_A + COLS - 1 - at % COLS
    source = col // WIN * CELLS + at // COLS * WIN + col % WIN
    turn[...] = onehot(iota(turn.shape, 1) == source)
    at = iota(back.shape, 0)
    back[...] = onehot(iota(back.shape, 1) == at // COLS * COLS + COLS - 1 - at % COLS)
    side = 2 * WIN - 1
    at = iota((side * side, C), 0)
    spread = onehot(iota(at.shape, 1) == 16 * (at // side + 1) + at % side)
    at = iota((C, 128), 0)
    cell = at % 128 // 16 * WIN + at % 16
    squeeze = onehot((at % 16 < WIN) & (iota(at.shape, 1) == at // 128 * CELLS + cell))

    w_qv[:C] = w_qkv[:, :C].T
    w_qv[C:] = w_qkv[:, 2 * C :].T
    b = b_qkv[...]
    b = jnp.concatenate([b[:, :C], b[:, 2 * C :]], axis=1)
    b_qv[...] = jnp.broadcast_to(b, (128, 2 * C)).T
    packed[...] = dot(pick, w_hid[...]).astype(jnp.bfloat16)
    flow_w[...] = jnp.concatenate(
        [w_flow[...].astype(jnp.float32), jnp.zeros((C, 126), jnp.float32)], axis=1
    ).astype(jnp.bfloat16)
    flow_b[...] = jnp.concatenate([b_flow[...], jnp.zeros((1, 126), jnp.float32)], axis=1)

    def exactly(x, onehot):
        high = x.astype(jnp.bfloat16)
        rest = x - high.astype(jnp.float32)
        mid = rest.astype(jnp.bfloat16)
        low = (rest - mid.astype(jnp.float32)).astype(jnp.bfloat16)
        return dot(high, onehot) + dot(mid, onehot) + dot(low, onehot)

    table = exactly(rel[...], spread) * LOG2E
    parts = []
    for head in range(HEADS):
        line = jnp.broadcast_to(table[head : head + 1], (WIN, C))
        rows = []
        for r in range(WIN):
            start = 16 * (WIN - r) - 1
            rows.append(pltpu.roll(line[:, start : start + 128], 120, 1, stride=1, stride_axis=0))
        parts.append(jnp.concatenate(rows, axis=0))
    pairs = [
        exactly(jnp.concatenate(parts[2 * p : 2 * p + 2], axis=1), squeeze)
        for p in range(HEADS // 2)
    ]
    base = jnp.concatenate(pairs, axis=1)
    key = lax.broadcasted_iota(jnp.int32, base.shape, 0)
    query = lax.broadcasted_iota(jnp.int32, base.shape, 1) % CELLS
    rows = (key // WIN < SHIFT) != (query // WIN < SHIFT)
    cols = (key % WIN < SHIFT) != (query % WIN < SHIFT)
    far = base - 100.0 * LOG2E
    bias[0] = base
    bias[1] = jnp.where(rows, far, base)
    bias[2] = jnp.where(cols, far, base)
    bias[3] = jnp.where(rows | cols, far, base)


def shards(
    section_a,
    section_b,
    ln_gain,
    ln_shift,
    w_qkv,
    b_qkv,
    rel_table,
    w_out,
    b_out,
    w_hid,
    b_hid,
    w_flow,
    b_flow,
):
    ids = jnp.stack(
        [
            lax.axis_index("row"),
            lax.axis_index("col"),
            jnp.int32(lax.axis_size("row")),
            jnp.int32(lax.axis_size("col")),
        ]
    )
    scalars = pl.BlockSpec(memory_space=pltpu.SMEM)
    whole = pl.BlockSpec(memory_space=pltpu.VMEM)
    params = pltpu.CompilerParams(vmem_limit_bytes=40 * 1024 * 1024)
    def made(*shape):
        return jax.ShapeDtypeStruct(shape, jnp.bfloat16)

    def made_f32(*shape):
        return jax.ShapeDtypeStruct(shape, jnp.float32)

    made_ready = pl.pallas_call(
        prepare,
        out_shape=(
            made(2 * C, C),
            made_f32(2 * C, 128),
            made(2 * PACKED, C),
            made(C, 128),
            made_f32(1, 128),
            made_f32(4, CELLS, HEADS * CELLS),
            made(2 * PACKED, 128),
            made(WIN * COLS, WIDE_A * CELLS),
            made(C, C),
        ),
        in_specs=[whole] * 6,
        out_specs=(whole,) * 9,
        compiler_params=params,
        cost_estimate=pl.CostEstimate(flops=10**9, bytes_accessed=4 * 10**6, transcendentals=0),
    )(w_qkv, b_qkv[None], w_hid, w_flow, b_flow[None], rel_table)
    strip = jax.ShapeDtypeStruct((ROWS, HALO_A + HALO_B, C), jnp.bfloat16)
    far, near = pl.pallas_call(
        pack_cols,
        out_shape=(strip, strip),
        in_specs=[scalars, whole, whole],
        out_specs=(whole, whole),
        compiler_params=params,
    )(ids, section_a, section_b)
    far = swap(far, "col", 1)
    near = swap(near, "col", 0)
    far, near, made_ready = lax.optimization_barrier((far, near, made_ready))
    w_qv, b_qv, packed, flow_pad, b_flow_pad, bias, w_off, turn, back = made_ready
    sent = jax.ShapeDtypeStruct((SENT, C), jnp.bfloat16)
    mid, far, near = pl.pallas_call(
        pack_rows,
        out_shape=(jax.ShapeDtypeStruct((MID, C), jnp.bfloat16), sent, sent),
        in_specs=[scalars] + [whole] * 4,
        out_specs=(whole,) * 3,
        compiler_params=params,
    )(ids, section_a, section_b, far, near)
    far = swap(far, "row", 1)
    near = swap(near, "row", 0)

    side = (WIDE_B + WIDE_A) * CELLS
    tables = (ln_gain[None], ln_shift[None], w_qkv, b_qkv[None], w_qv, b_qv, bias, w_out, b_out[None])
    outer, centre_b, centre_a = pl.pallas_call(
        centre,
        out_shape=(made(side, C), made(WIN * KEYS, C), made(WIN * COLS, C)),
        in_specs=[scalars] + [whole] * 11,
        out_specs=(whole,) * 3,
        scratch_shapes=[
            pltpu.VMEM((C, side), jnp.bfloat16),
            pltpu.VMEM((side, C), jnp.bfloat16),
            pltpu.VMEM((C, side), jnp.bfloat16),
            pltpu.VMEM((side, C), jnp.bfloat16),
        ],
        compiler_params=params,
        cost_estimate=pl.CostEstimate(flops=2 * 10**9, bytes_accessed=4 * 10**6, transcendentals=0),
    )(ids, mid, *tables, turn)

    call = pl.pallas_call(
        body,
        out_shape=jax.ShapeDtypeStruct((2, ROWS, COLS), jnp.float32),
        in_specs=[scalars] + [whole] * 22,
        out_specs=whole,
        scratch_shapes=[
            pltpu.VMEM((TOTAL, C), jnp.bfloat16),
            pltpu.VMEM((C, TOTAL), jnp.bfloat16),
            pltpu.VMEM((TOTAL, C), jnp.bfloat16),
            pltpu.VMEM((C, TOTAL), jnp.bfloat16),
            pltpu.VMEM((TOTAL, C), jnp.bfloat16),
            pltpu.VMEM((HIGH_B * WIN * KEYS, C), jnp.bfloat16),
            pltpu.VMEM((HIGH_A * WIN * COLS, C), jnp.bfloat16),
            pltpu.VMEM((ROWS * COLS, GRAM), jnp.float32),
            pltpu.VMEM((2, ROWS // 2 * COLS, PACKED), jnp.bfloat16),
        ],
        compiler_params=params,
    )
    return call(
        ids,
        mid,
        far,
        near,
        outer,
        centre_b,
        centre_a,
        *tables,
        packed,
        w_off,
        b_hid[None],
        flow_pad,
        b_flow_pad,
        turn,
        back,
    )


def solution(mesh):
    placed = (P("row", "col", None),) * 2 + (P(),) * 11
    return jax.shard_map(
        shards, mesh=mesh, in_specs=placed, out_specs=P(None, "row", "col"), check_vma=False
    )
```

time: 54.6 us -> 45.9 us (0.84)
  the two profiles are of different devices: /device:TPU:7 before, /device:TPU:16 now
where the time goes in v3:
time: 45.9 us; the launch traced here: 45.6 us
  starting transfers between devices  19.5 us (42%)
  Pallas kernels  15.7 us (34%)
  waiting for transfers between devices  6.05 us (13%)
  local copies, waits for them, and re-layouts  4.05 us (9%)
    ppermute x4, starting transfers between devices, swap(): return lax.ppermute(array, axis, pairs)  19.5 us
    pallas_call x1, Pallas kernels, shards(): call(ids, mid, far, near, outer, centre_b, centre_a, *tables, packed, w_o...  9.4 us
    ppermute x4, waiting for transfers between devices, swap(): return lax.ppermute(array, axis, pairs)  6.05 us
    unnamed x31, local copies, waits for them, and re-layouts  4.04 us
    pallas_call x1, Pallas kernels, shards(): pl.pallas_call(centre, out_shape=(made(side, C), made(WIN * KEYS, C), mad...  3.29 us
    pallas_call x1, Pallas kernels, shards(): pl.pallas_call(prepare, out_shape=(made(2 * C, C), made_f32(2 * C, 128),...  1.66 us
  transfers between devices with their start and end apart: 4, of which 2 were waited for; matrix products, arithmetic and copies ran while one was open for 0% of the time, Pallas kernels for 11%

profile of v3, /device:TPU:16, one launch (start us, length us, event | category | flops | bytes accessed | tf_op | source)
XLA Modules:
  0.0 45.6 jit_solution(2864411342448941449)
XLA Ops:
  0.0 0.1 pad_add_fusion.ids
  0.1 0.9 %copy-done = bf16[16,32,256]{2,1,0:T(8,128)(2,1)S(1)} copy-done((bf16[16,32,256]{2,1,0:T(8,128)(2,1)S(1)}, bf16[16,32,256]{2,1,0:T(8,128)(2,1)}, u32[]{:S(2)}) %copy-start) | copy-done | bytes 262168
  1.0 0.9 %copy-done.2 = bf16[16,32,256]{2,1,0:T(8,128)(2,1)S(1)} copy-done((bf16[16,32,256]{2,1,0:T(8,128)(2,1)S(1)}, bf16[16,32,256]{2,1,0:T(8,128)(2,1)}, u32[]{:S(2)}) %copy-start.2) | copy-done | bytes 262168
  2.0 0.6 %shard_map.127 = (bf16[16,16,256]{2,1,0:T(8,128)(2,1)S(1)}, bf16[16,16,256]{2,1,0:T(8,128)(2,1)S(1)}) custom-call(s32[4]{0:T(128)S(1)} %pad_add_fusion.ids, bf16[16,32,256]{2,1,0:T(8,128)(2,1)S(1)} %copy-done, bf16[16,32,256]{2,1,0:T(8,128)(2,1)S(1)} %copy-done.2), custom_call_target="tpu_custom_call" | custom-call | tf_op jit(solution)/shard_map/pallas_call | solution.py:502
  2.6 12.1 %collective-permute-start = (bf16[16,16,256]{2,1,0:T(8,128)(2,1)S(1)}, bf16[16,16,256]{2,1,0:T(8,128)(2,1)S(1)}, u32[]{:S(2)}, u32[]{:S(2)}) collective-permute-start(bf16[16,16,256]{2,1,0:T(8,128)(2,1)S(1)} %get-tuple-element.33), channel_id=1, source_target_pairs={{0,31},{1,2},{2,1},{3,4},{4,3},{5,6},{6,5},{7,8},{8,7},{9,10},{10,... | collective-permute-start | bytes 393224 | tf_op jit(solution)/shard_map/ppermute | solution.py:38
  14.7 1.9 %collective-permute-start.1 = (bf16[16,16,256]{2,1,0:T(8,128)(2,1)S(1)}, bf16[16,16,256]{2,1,0:T(8,128)(2,1)S(1)}, u32[]{:S(2)}, u32[]{:S(2)}) collective-permute-start(bf16[16,16,256]{2,1,0:T(8,128)(2,1)S(1)} %get-tuple-element.34), channel_id=1, source_target_pairs={{0,1},{1,0},{2,3},{3,2},{4,5},{5,4},{6,7},{7,6},{8,9},{9,8},{10,11... | collective-permute-start | bytes 393224 | tf_op jit(solution)/shard_map/ppermute | solution.py:38
  16.7 0.0 copy-done.13
  16.7 0.0 copy-done.14
  16.7 0.0 copy-start.11
  16.7 0.1 copy.14.w_flow
  16.9 0.0 copy-done.4
  16.9 0.0 copy-done.10
  16.9 0.5 %copy-done.11 = f32[8,225]{1,0:T(8,128)S(1)} copy-done((f32[8,225]{1,0:T(8,128)S(1)}, f32[8,225]{1,0:T(8,128)}, u32[]{:S(2)}) %copy-start.11) | copy-done | bytes 7224
  17.4 0.1 copy-done.12
  17.5 1.7 %shard_map.128 = (bf16[512,256]{1,0:T(8,128)(2,1)S(1)}, f32[512,128]{1,0:T(8,128)S(1)}, bf16[1280,256]{1,0:T(8,128)(2,1)S(1)}, bf16[256,128]{1,0:T(8,128)(2,1)S(...) custom-call(bf16[256,768]{1,0:T(8,128)(2,1)S(1)} %copy-done.4, ...), custom_call_target="tpu_custom_call" | custom-call | flops 1000000000 | bytes 4000000 | tf_op jit(solution)/shard_map/pallas_call | solution.py:483
  19.2 0.0 collective-permute-done.far_ref
  19.2 2.4 %collective-permute-done.1.near_ref = bf16[16,16,256]{2,1,0:T(8,128)(2,1)S(1)} collective-permute-done((bf16[16,16,256]{2,1,0:T(8,128)(2,1)S(1)}, bf16[16,16,256]{2,1,0:T(8,128)(2,1)S(1)}, u32[]{:S(2)}, u32[]{:S(2)}) %collective-permute-start.1) | collective-permute-done | bytes 131104 | tf_op jit(solution)/shard_map/ppermute | solution.py:38
  21.6 0.0 copy-done.1
  21.6 0.0 copy-done.3
  21.6 0.0 copy-start.8
  21.6 0.8 %shard_map.129 = (bf16[1536,256]{1,0:T(8,128)(2,1)S(1)}, bf16[832,256]{1,0:T(8,128)(2,1)S(1)}, bf16[832,256]{1,0:T(8,128)(2,1)S(1)}) custom-call(s32[4]{0:T(128)S(1)} %pad_add_fusion.ids, bf16[16,32,256]{2,1,0:T(8,128)(2,1)S(1)} %copy-done.1, bf16[16,32,256]{2,1,0:T(8,128)(2,1)S(1)} %copy-done.3, bf16[16,16,256]{2,1,0:T(8,128)(2,1)S(1)} %collective-permute-done.far_ref, ...), custom_call_target="tpu_custom_call" | custom-call | tf_op jit(solution)/shard_map/pallas_call | solution.py:514
  22.4 2.7 %collective-permute-start.2 = (bf16[832,256]{1,0:T(8,128)(2,1)S(1)}, bf16[832,256]{1,0:T(8,128)(2,1)S(1)}, u32[]{:S(2)}, u32[]{:S(2)}) collective-permute-start(bf16[832,256]{1,0:T(8,128)(2,1)S(1)} %get-tuple-element.47), channel_id=1, source_target_pairs={{0,480},{32,64},{64,32},{96,128},{128,96},{160,192},{192,160},{224... | collective-permute-start | bytes 1277960 | tf_op jit(solution)/shard_map/ppermute | solution.py:38
  25.2 2.7 %collective-permute-start.3 = (bf16[832,256]{1,0:T(8,128)(2,1)S(1)}, bf16[832,256]{1,0:T(8,128)(2,1)S(1)}, u32[]{:S(2)}, u32[]{:S(2)}) collective-permute-start(bf16[832,256]{1,0:T(8,128)(2,1)S(1)} %get-tuple-element.48), channel_id=1, source_target_pairs={{0,32},{32,0},{64,96},{96,64},{128,160},{160,128},{192,224},{224,1... | collective-permute-start | bytes 1277960 | tf_op jit(solution)/shard_map/ppermute | solution.py:38
  27.9 0.0 copy-start.6
  27.9 0.0 copy-done.5
  27.9 0.0 copy-done.7
  27.9 0.6 %copy-done.6 = f32[256]{0:T(256)S(1)} copy-done((f32[256]{0:T(256)S(1)}, f32[256]{0:T(256)}, u32[]{:S(2)}) %copy-start.6) | copy-done | bytes 1048
  28.5 3.3 %shard_map.130 = (bf16[768,256]{1,0:T(8,128)(2,1)S(1)}, bf16[512,256]{1,0:T(8,128)(2,1)S(1)}, bf16[256,256]{1,0:T(8,128)(2,1)S(1)}) custom-call(s32[4]{0:T(128)S(1)} %pad_add_fusion.ids, bf16[1536,256]{1,0:T(8,128)(2,1)S(1)} %get-tuple-element.46.mid, f32[1,256]{1,0:T(1,128)S(1)} %bitcast.7, f32[1,256]{1,0:T(1,128)S(1)} %bitcast.9, ...), custom_call_target="tpu_custom_call" | custom-call | flops 2000000000 | bytes 4000000 | tf_op jit(solution)/shard_map/pallas_call | solution.py:526
  31.8 3.6 %collective-permute-done.2.far = bf16[832,256]{1,0:T(8,128)(2,1)S(1)} collective-permute-done((bf16[832,256]{1,0:T(8,128)(2,1)S(1)}, bf16[832,256]{1,0:T(8,128)(2,1)S(1)}, u32[]{:S(2)}, u32[]{:S(2)}) %collective-permute-start.2) | collective-permute-done | bytes 426016 | tf_op jit(solution)/shard_map/ppermute | solution.py:38
  35.5 0.0 collective-permute-done.3.near
  35.5 0.7 %copy-done.9 = f32[256]{0:T(256)S(1)} copy-done((f32[256]{0:T(256)S(1)}, f32[256]{0:T(256)}, u32[]{:S(2)}) %copy-start.9) | copy-done | bytes 1048
  36.2 9.4 %shard_map.131 = f32[2,16,32]{2,1,0:T(8,128)} custom-call(s32[4]{0:T(128)S(1)} %pad_add_fusion.ids, bf16[1536,256]{1,0:T(8,128)(2,1)S(1)} %get-tuple-element.46.mid, bf16[832,256]{1,0:T(8,128)(2,1)S(1)} %collective-permute-done.2.far, bf16[832,256]{1,0:T(8,128)(2,1)S(1)} %collective-permute-done.3.near, bf16[768,256]{1,0:T(8,128)(2,1)S(1)} %get-tuple-element.53.outer, ...), custom_call_target="tpu_custom_call" | custom-call | tf_op jit(solution)/shard_map/pallas_call | solution.py:559
  (14 shorter events, 0.0 us)
Async XLA Ops:
  0.0 16.7 %copy-start.13 = (f32[768]{0:T(1024)S(1)}, f32[768]{0:T(1024)}, u32[]{:S(2)}) copy-start(f32[768]{0:T(1024)} %param.18) | copy-start | bytes 9220
  0.0 16.7 %copy-start.14 = (bf16[256,2]{0,1:T(2,128)(2,1)S(1)}, bf16[256,2]{0,1:T(2,128)(2,1)}, u32[]{:S(2)}) copy-start(bf16[256,2]{0,1:T(2,128)(2,1)} %param.24) | copy-start | bytes 3076
  0.1 1.0 %copy-start = (bf16[16,32,256]{2,1,0:T(8,128)(2,1)S(1)}, bf16[16,32,256]{2,1,0:T(8,128)(2,1)}, u32[]{:S(2)}) copy-start(bf16[16,32,256]{2,1,0:T(8,128)(2,1)} %a_ref.3) | copy-start | bytes 786436
  1.0 0.9 %copy-start.2 = (bf16[16,32,256]{2,1,0:T(8,128)(2,1)S(1)}, bf16[16,32,256]{2,1,0:T(8,128)(2,1)}, u32[]{:S(2)}) copy-start(bf16[16,32,256]{2,1,0:T(8,128)(2,1)} %b_ref.3) | copy-start | bytes 786436
  2.0 14.9 %copy-start.4 = (bf16[256,768]{1,0:T(8,128)(2,1)S(1)}, bf16[256,768]{1,0:T(8,128)(2,1)}, u32[]{:S(2)}) copy-start(bf16[256,768]{1,0:T(8,128)(2,1)} %w_qkv.5) | copy-start | bytes 1179652
  2.0 14.9 %copy-start.10 = (bf16[289,256]{1,0:T(8,128)(2,1)S(1)}, bf16[289,256]{1,0:T(8,128)(2,1)}, u32[]{:S(2)}) copy-start(bf16[289,256]{1,0:T(8,128)(2,1)} %w_hid.1) | copy-start | bytes 443908
  2.6 16.6 %collective-permute-start = (bf16[16,16,256]{2,1,0:T(8,128)(2,1)S(1)}, bf16[16,16,256]{2,1,0:T(8,128)(2,1)S(1)}, u32[]{:S(2)}, u32[]{:S(2)}) collective-permute-start(bf16[16,16,256]{2,1,0:T(8,128)(2,1)S(1)} %get-tuple-element.33), channel_id=1, source_target_pairs={{0,31},{1,2},{2,1},{3,4},{4,3},{5,6},{6,5},{7,8},{8,7},{9,10},{10,... | collective-permute-start | bytes 393224 | tf_op jit(solution)/shard_map/ppermute | solution.py:38
  14.7 6.9 %collective-permute-start.1 = (bf16[16,16,256]{2,1,0:T(8,128)(2,1)S(1)}, bf16[16,16,256]{2,1,0:T(8,128)(2,1)S(1)}, u32[]{:S(2)}, u32[]{:S(2)}) collective-permute-start(bf16[16,16,256]{2,1,0:T(8,128)(2,1)S(1)} %get-tuple-element.34), channel_id=1, source_target_pairs={{0,1},{1,0},{2,3},{3,2},{4,5},{5,4},{6,7},{7,6},{8,9},{9,8},{10,11... | collective-permute-start | bytes 393224 | tf_op jit(solution)/shard_map/ppermute | solution.py:38
  16.7 0.7 %copy-start.11 = (f32[8,225]{1,0:T(8,128)S(1)}, f32[8,225]{1,0:T(8,128)}, u32[]{:S(2)}) copy-start(f32[8,225]{1,0:T(8,128)} %rel.1) | copy-start | bytes 21604
  16.9 0.7 %copy-start.12 = (f32[2]{0:T(128)S(1)}, f32[2]{0:T(128)}, u32[]{:S(2)}) copy-start(f32[2]{0:T(128)} %param.25) | copy-start | bytes 28
  17.5 4.1 %copy-start.1 = (bf16[16,32,256]{2,1,0:T(8,128)(2,1)S(1)}, bf16[16,32,256]{2,1,0:T(8,128)(2,1)}, u32[]{:S(2)}) copy-start(bf16[16,32,256]{2,1,0:T(8,128)(2,1)} %a_ref.3) | copy-start | bytes 786436
  17.5 4.1 %copy-start.3 = (bf16[16,32,256]{2,1,0:T(8,128)(2,1)S(1)}, bf16[16,32,256]{2,1,0:T(8,128)(2,1)}, u32[]{:S(2)}) copy-start(bf16[16,32,256]{2,1,0:T(8,128)(2,1)} %b_ref.3) | copy-start | bytes 786436
  21.6 6.3 %copy-start.5 = (bf16[256,256]{1,0:T(8,128)(2,1)S(1)}, bf16[256,256]{1,0:T(8,128)(2,1)}, u32[]{:S(2)}) copy-start(bf16[256,256]{1,0:T(8,128)(2,1)} %w_out.3) | copy-start | bytes 393220
  21.6 6.3 %copy-start.7 = (f32[256]{0:T(256)S(1)}, f32[256]{0:T(256)}, u32[]{:S(2)}) copy-start(f32[256]{0:T(256)} %param.16) | copy-start | bytes 3076
  21.6 6.3 %copy-start.8 = (f32[256]{0:T(256)S(1)}, f32[256]{0:T(256)}, u32[]{:S(2)}) copy-start(f32[256]{0:T(256)} %param.21) | copy-start | bytes 3076
  22.4 13.1 %collective-permute-start.2 = (bf16[832,256]{1,0:T(8,128)(2,1)S(1)}, bf16[832,256]{1,0:T(8,128)(2,1)S(1)}, u32[]{:S(2)}, u32[]{:S(2)}) collective-permute-start(bf16[832,256]{1,0:T(8,128)(2,1)S(1)} %get-tuple-element.47), channel_id=1, source_target_pairs={{0,480},{32,64},{64,32},{96,128},{128,96},{160,192},{192,160},{224... | collective-permute-start | bytes 1277960 | tf_op jit(solution)/shard_map/ppermute | solution.py:38
  25.2 10.3 %collective-permute-start.3 = (bf16[832,256]{1,0:T(8,128)(2,1)S(1)}, bf16[832,256]{1,0:T(8,128)(2,1)S(1)}, u32[]{:S(2)}, u32[]{:S(2)}) collective-permute-start(bf16[832,256]{1,0:T(8,128)(2,1)S(1)} %get-tuple-element.48), channel_id=1, source_target_pairs={{0,32},{32,0},{64,96},{96,64},{128,160},{160,128},{192,224},{224,1... | collective-permute-start | bytes 1277960 | tf_op jit(solution)/shard_map/ppermute | solution.py:38
  27.9 0.7 %copy-start.6 = (f32[256]{0:T(256)S(1)}, f32[256]{0:T(256)}, u32[]{:S(2)}) copy-start(f32[256]{0:T(256)} %param.15) | copy-start | bytes 3076
  35.5 0.7 %copy-start.9 = (f32[256]{0:T(256)S(1)}, f32[256]{0:T(256)}, u32[]{:S(2)}) copy-start(f32[256]{0:T(256)} %param.23) | copy-start | bytes 3076

commit v4 on v3

--- a/solution.py
+++ b/solution.py
@@ -20,14 +20,16 @@
 HIGH_A, WIDE_A = 3, 5
 HIGH_B, WIDE_B = 5, 7
 CELLS = WIN * WIN
-STRIPS_A, STRIPS_B = (0, 2), (0, 1, 3, 4)
-LEFT_A, LEFT_B = len(STRIPS_A), len(STRIPS_B)
-START_A = LEFT_B * WIDE_B * CELLS
-TOTAL = START_A + LEFT_A * WIDE_A * CELLS
+SIDE_B = 2 * CELLS
+START_A = WIDE_B * SIDE_B
+TOTAL = START_A + (WIDE_A + 1) * CELLS
+CENTRE = (WIDE_B + WIDE_A) * CELLS
+
 HALF = C // 2
 PACKED = 5 * 128
 KEYS = 64
 GRAM = (ROWS + 2 * RADIUS) * KEYS
+FLANK = 2 * WIN * KEYS
 LOG2E = 1.4426950408889634
 NT = (((1,), (1,)), ((), ()))
 
@@ -49,7 +51,7 @@
 SENT = WIDE_B * SENT_B + WIDE_A * SENT_A
 
 
-def pack_cols(ids, a_ref, b_ref, far_ref, near_ref):
+def pack_cols(ids, a_ref, b_ref, near_ref, far_ref):
     even = ids[1] % 2 == 0
     for r in range(ROWS):
         a, b = a_ref[r].astype(jnp.float32), b_ref[r].astype(jnp.float32)
@@ -59,7 +61,7 @@
         far_ref[r] = jnp.where(even, first, last).astype(jnp.bfloat16)
 
 
-def pack_rows(ids, a_ref, b_ref, far_ref, near_ref, mid, down_ref, up_ref):
+def pack_rows(ids, a_ref, b_ref, near_ref, far_ref, mid, up_ref, down_ref):
     even = ids[1] % 2 == 0
     for r in range(0, ROWS, 2):
         rows = []
@@ -92,30 +94,20 @@
     send(down_ref, odd)
 
 
-def normalise(x, gain, shift):
+def normalise(x, vectors):
     x = x.astype(jnp.float32)
     centred = x - jnp.mean(x, axis=-1, keepdims=True)
     variance = jnp.mean(centred * centred, axis=-1, keepdims=True)
-    normed = centred * lax.rsqrt(variance + 1e-05) * gain[...] + shift[...]
+    normed = centred * lax.rsqrt(variance + 1e-05) * vectors[0:1] + vectors[1:2]
     return normed.astype(jnp.bfloat16)
 
 
-def project(normed, rows, w_qkv, b_qkv, w_qv, b_qv, q_s, k_s, v_s):
-    k_s[rows] = (dot(normed, w_qkv[:, C : 2 * C]) + b_qkv[:, C : 2 * C]).astype(jnp.bfloat16)
+def project(normed, rows, vectors, w_k, w_qv, b_qv, q_s, k_s, v_s):
+    k_s[rows] = (dot(normed, w_k[...]) + vectors[4:5]).astype(jnp.bfloat16)
     qv = lax.dot_general(w_qv[...], normed, NT, preferred_element_type=jnp.float32)
     qv = qv + b_qv[:, :1]
     q_s[:, rows] = (qv[:C] * (HEAD**-0.5 * LOG2E)).astype(jnp.bfloat16)
     v_s[:, rows] = qv[C:].astype(jnp.bfloat16)
-
-
-def table_of(ids, bias, i, j, high, wide, inset):
-    index = 0
-    for n, at, end in ((0, i, high - 1), (1, j, wide - 1)):
-        if at == inset:
-            index += (ids[n] == 0).astype(jnp.int32) * (n + 1)
-        elif at == end - inset:
-            index += (ids[n] == ids[n + 2] - 1).astype(jnp.int32) * (n + 1)
-    return bias.at[index]
 
 
 def attend(tables, q_s, k_s, v_s, mix_s):
@@ -170,8 +162,8 @@
     )
 
 
-def finish(ids, x, total, b_out, mirror, strip, out, at):
-    f = x.astype(jnp.float32) + (total + b_out[...]).astype(jnp.bfloat16).astype(jnp.float32)
+def finish(ids, x, total, vectors, mirror, strip, out, at):
+    f = x.astype(jnp.float32) + (total + vectors[2:3]).astype(jnp.bfloat16).astype(jnp.float32)
     if strip is None:
         out[at : at + WIN * COLS] = dot(mirror[...], f.astype(jnp.bfloat16)).astype(jnp.bfloat16)
         return
@@ -189,54 +181,125 @@
         out[at + r * KEYS : at + (r + 1) * KEYS] = jnp.where(inside, row, 0.0).astype(jnp.bfloat16)
 
 
-def centre(
-    ids, mid, gain, shift, w_qkv, b_qkv, w_qv, b_qv, bias, w_out, b_out, mirror,
-    outer, fb, fa, q_s, k_s, v_s, mix_s,
-):
-    x_s = []
+def centre_windows(ids, mid, vectors, w_k, w_qv, b_qv, bias, outer, q_s, k_s, v_s):
+    cells = []
     for j in range(0, WIDE_B + WIDE_A, 4):
         inner = []
         for n in range(j, j + 4):
             at = n * ROWS * WIN
-            normed = normalise(mid[at : at + ROWS * WIN], gain, shift)
+            normed = normalise(mid[at : at + ROWS * WIN], vectors)
             outer[n * CELLS : n * CELLS + SENT_A] = normed[:SENT_A]
             outer[n * CELLS + SENT_A : (n + 1) * CELLS] = normed[-SENT_A:]
             inner.append(normed[SENT_A:-SENT_A])
-            x_s.append(mid[at + SENT_A : at + SENT_A + CELLS])
+            cells.append(mid[at + SENT_A : at + SENT_A + CELLS])
         rows = slice(j * CELLS, (j + 4) * CELLS)
-        project(jnp.concatenate(inner, axis=0), rows, w_qkv, b_qkv, w_qv, b_qv, q_s, k_s, v_s)
-    tables = [table_of(ids, bias, 2, j, HIGH_B, WIDE_B, 1) for j in range(WIDE_B)]
-    tables += [table_of(ids, bias, 1, j, HIGH_A, WIDE_A, 0) for j in range(WIDE_A)]
+        project(jnp.concatenate(inner, axis=0), rows, vectors, w_k, w_qv, b_qv, q_s, k_s, v_s)
+    tables = [table_of(ids, bias, j, WIDE_B, 1) for j in range(WIDE_B)]
+    tables += [table_of(ids, bias, j, WIDE_A, 0) for j in range(WIDE_A)]
+    return cells, tables
+
+
+def table_of(ids, bias, j, wide, inset, on_row=None):
+    index = 0 if on_row is None else on_row.astype(jnp.int32)
+    if j == inset:
+        index += 2 * (ids[1] == 0).astype(jnp.int32)
+    elif j == wide - 1 - inset:
+        index += 2 * (ids[1] == ids[3] - 1).astype(jnp.int32)
+    return bias.at[index]
+
+
+def flank_windows(
+    ids, top, got, mid, outer, vectors, w_k, w_qv, b_qv, bias, x_s, q_s, k_s, v_s, base
+):
+    def order(theirs, ours):
+        return jnp.where(
+            top,
+            jnp.concatenate([theirs, ours], axis=0),
+            jnp.concatenate([ours, theirs], axis=0),
+        )
+
+    def ours(ref, start, size):
+        last = start + size - SENT_A
+        return jnp.where(top, ref[start : start + SENT_A], ref[last : last + SENT_A])
+
+    normed, start = [], 0
+    for j in range(WIDE_B + WIDE_A):
+        if j < WIDE_B:
+            sent, at, end = j * SENT_B, j * SIDE_B, (j + 1) * SIDE_B
+            x = got[sent : sent + SENT_B]
+        else:
+            n = j - WIDE_B
+            sent, at = WIDE_B * SENT_B + n * SENT_A, START_A + n * CELLS
+            x, end = got[sent : sent + SENT_A], at + CELLS
+        x_s[at:end] = order(x, ours(mid, j * ROWS * WIN, ROWS * WIN))
+        normed.append(order(normalise(x, vectors), ours(outer, j * CELLS, CELLS)))
+        last = j == WIDE_B + WIDE_A - 1
+        if last:
+            normed.append(normed[-1])
+            end += CELLS
+        if last or j in (1, 3, 6):
+            part = jnp.concatenate(normed, axis=0)
+            rows = slice(base + start, base + end)
+            project(part, rows, vectors, w_k, w_qv, b_qv, q_s, k_s, v_s)
+            normed, start = [], end
+
+    above = top & (ids[0] == 0)
+    below = jnp.logical_not(top) & (ids[0] == ids[2] - 1)
+    tables = [
+        table_of(ids, bias, j, WIDE_B, 1, edge) for j in range(WIDE_B) for edge in (below, above)
+    ]
+    tables += [table_of(ids, bias, j, WIDE_A, 0, below | above) for j in range(WIDE_A)]
+    return tables + tables[-1:]
+
+
+def flank_features(ids, top, vectors, w_out, mirror, fb, fa, x_s, mix_s, base):
+    strips = [(0, 2, WIDE_B, 0), (0, 2, WIDE_B, 1), (START_A, 1, WIDE_A, 0)]
+    sums = [dot(column(mix_s, base + strip[0], *strip[1:]), w_out[...]) for strip in strips]
+    for t in range(2):
+        strip = jnp.where(top, t, t + 3)
+        x = column(x_s, *strips[t])
+        finish(ids, x, sums[t], vectors, mirror, strip, fb, t * WIN * KEYS)
+    finish(ids, column(x_s, *strips[2]), sums[2], vectors, mirror, None, fa, 0)
+
+
+def early(
+    ids, got, mid, vectors, w_k, w_qv, b_qv, bias, w_out, mirror,
+    outer, centre_b, centre_a, near_b, near_a, x_s, q_s, k_s, v_s, mix_s,
+):
+    top = ids[0] % 2 == 1
+    cells, tables = centre_windows(
+        ids, mid, vectors, w_k, w_qv, b_qv, bias, outer, q_s, k_s, v_s
+    )
+    tables += flank_windows(
+        ids, top, got, mid, outer, vectors, w_k, w_qv, b_qv, bias, x_s, q_s, k_s, v_s, CENTRE
+    )
     attend(tables, q_s, k_s, v_s, mix_s)
     cut = WIDE_B * CELLS
-    sum_b, sum_a = dot(mix_s[:cut], w_out[...]), dot(mix_s[cut:], w_out[...])
-    finish(ids, jnp.concatenate(x_s[:WIDE_B], axis=0), sum_b, b_out, mirror, 2, fb, 0)
-    finish(ids, jnp.concatenate(x_s[WIDE_B:], axis=0), sum_a, b_out, mirror, None, fa, 0)
+    sum_b, sum_a = dot(mix_s[:cut], w_out[...]), dot(mix_s[cut:CENTRE], w_out[...])
+    finish(ids, jnp.concatenate(cells[:WIDE_B], axis=0), sum_b, vectors, mirror, 2, centre_b, 0)
+    finish(ids, jnp.concatenate(cells[WIDE_B:], axis=0), sum_a, vectors, mirror, None, centre_a, 0)
+    flank_features(ids, top, vectors, w_out, mirror, near_b, near_a, x_s, mix_s, CENTRE)
 
 
 def body(
     ids,
+    got,
     mid,
-    far,
-    near,
     outer,
+    near_b,
+    near_a,
     centre_b,
     centre_a,
-    gain,
-    shift,
-    w_qkv,
-    b_qkv,
+    vectors,
+    w_k,
     w_qv,
     b_qv,
     bias,
     w_out,
-    b_out,
+    mirror,
     w_hid,
-    w_off,
-    b_hid,
     w_flow,
     b_flow,
-    mirror,
     unmirror,
     out,
     x_s,
@@ -248,68 +311,33 @@
     fa,
     g_s,
     e_s,
+    stat_s,
 ):
-    def spans():
-        for j in range(WIDE_B + WIDE_A):
-            if j < WIDE_B:
-                yield j, j * LEFT_B * CELLS, SENT_B, j * SENT_B
-            else:
-                n = j - WIDE_B
-                yield j, START_A + n * LEFT_A * CELLS, SENT_A, WIDE_B * SENT_B + n * SENT_A
-
-    def place_rows(above, below):
-        for j, at, sent, got in spans():
-            own = j * ROWS * WIN
-            x_s[at : at + sent] = above[got : got + sent]
-            x_s[at + sent : at + sent + SENT_A] = mid[own : own + SENT_A]
-            x_s[at + sent + SENT_A : at + sent + CELLS] = mid[
-                own + ROWS * WIN - SENT_A : own + ROWS * WIN
-            ]
-            x_s[at + sent + CELLS : at + 2 * sent + CELLS] = below[got : got + sent]
-
     even = ids[0] % 2 == 0
-
-    @pl.when(even)
-    def _():
-        place_rows(far, near)
-
-    @pl.when(jnp.logical_not(even))
-    def _():
-        place_rows(near, far)
-
-    normed, start = [], 0
-    for j, at, sent, _ in spans():
-        top = normalise(x_s[at : at + sent], gain, shift)
-        low = normalise(x_s[at + sent + CELLS : at + 2 * sent + CELLS], gain, shift)
-        normed += [top, outer[j * CELLS : (j + 1) * CELLS], low]
-        end = at + 2 * sent + CELLS
-        if j % 2 == 1 or j == WIDE_B + WIDE_A - 1:
-            rows = slice(start, end)
-            project(jnp.concatenate(normed, axis=0), rows, w_qkv, b_qkv, w_qv, b_qv, q_s, k_s, v_s)
-            normed, start = [], end
-
-    tables = [
-        table_of(ids, bias, i, j, HIGH_B, WIDE_B, 1) for j in range(WIDE_B) for i in STRIPS_B
-    ] + [table_of(ids, bias, i, j, HIGH_A, WIDE_A, 0) for j in range(WIDE_A) for i in STRIPS_A]
+    low_b, low_a = (HIGH_B * WIN * KEYS - FLANK), (HIGH_A - 1) * WIN * COLS
+    here_b = pl.ds(pl.multiple_of(jnp.where(even, 0, low_b), KEYS), FLANK)
+    there_b = pl.ds(pl.multiple_of(jnp.where(even, low_b, 0), KEYS), FLANK)
+    here_a = pl.ds(pl.multiple_of(jnp.where(even, 0, low_a), COLS), WIN * COLS)
+    there_a = pl.ds(pl.multiple_of(jnp.where(even, low_a, 0), COLS), WIN * COLS)
+    fb[there_b] = near_b[...]
+    fa[there_a] = near_a[...]
+    fb[FLANK : FLANK + WIN * KEYS] = centre_b[...]
+    fa[WIN * COLS : 2 * WIN * COLS] = centre_a[...]
+    tables = flank_windows(
+        ids, even, got, mid, outer, vectors, w_k, w_qv, b_qv, bias, x_s, q_s, k_s, v_s, 0
+    )
     attend(tables, q_s, k_s, v_s, mix_s)
-
-    strips = [(0, LEFT_B, WIDE_B, t) for t in range(LEFT_B)]
-    strips += [(START_A, LEFT_A, WIDE_A, t) for t in range(LEFT_A)]
-    sums = [dot(column(mix_s, *strip), w_out[...]) for strip in strips]
-    for strip, total in zip(strips, sums):
-        x, t = column(x_s, *strip), strip[-1]
-        if strip[0] == START_A:
-            finish(ids, x, total, b_out, mirror, None, fa, STRIPS_A[t] * WIN * COLS)
-        else:
-            i = STRIPS_B[t]
-            finish(ids, x, total, b_out, mirror, i, fb, i * WIN * KEYS)
-    fb[2 * WIN * KEYS : 3 * WIN * KEYS] = centre_b[...]
-    fa[WIN * COLS : 2 * WIN * COLS] = centre_a[...]
+    flank_features(
+        ids, even, vectors, w_out, mirror, fb.at[here_b], fa.at[here_a], x_s, mix_s, 0
+    )
 
     lane = lax.broadcasted_iota(jnp.int32, (COLS, 128), 1)
     valid = lane % 32 < SPAN
-    early = lane % KEYS < 32
+    fore = lane % KEYS < 32
     first = valid & (lane < 32)
+    slot = lane // 32
+    slot_row = jnp.where(slot == 1, 3, jnp.where(slot == 3, 2, slot // 2)).astype(jnp.float32)
+    slot_col = (lane % 32 - RADIUS).astype(jnp.float32)
     second = valid & (lane >= 32)
 
     for n in range(4):
@@ -332,31 +360,39 @@
         for n in range(5):
             tile = align(r, 2 * n)
             if n < 4:
-                tile = jnp.where(early, tile, align(r, 2 * n + 1))
+                tile = jnp.where(fore, tile, align(r, 2 * n + 1))
             keep = valid
             if r % 2 == 0 and n == 4:
                 keep = first
             if r % 2 == 1 and n == 0:
                 keep = second
             if n == 4 and r % 2 == 1:
-                keep = valid & early
+                keep = valid & fore
             tiles.append(jnp.where(keep, tile * (C**-0.5 * LOG2E), -1e30))
         most = tiles[0]
         for tile in tiles[1:]:
             most = jnp.maximum(most, tile)
         most = jnp.max(most, axis=-1, keepdims=True)
         rows = slice((r // 2) * COLS, (r // 2 + 1) * COLS)
-        for n in range(5):
-            e_s[r % 2, rows, 128 * n : 128 * (n + 1)] = jnp.exp2(tiles[n] - most).astype(
-                jnp.bfloat16
-            )
-
-    sums = [dot(e_s[par], w_off[par * PACKED : (par + 1) * PACKED]) for par in range(2)]
+        parts = [jnp.exp2(tile - most) for tile in tiles]
+        for n, part in enumerate(parts):
+            e_s[r % 2, rows, 128 * n : 128 * (n + 1)] = part.astype(jnp.bfloat16)
+        whole = parts[0] + parts[1] + parts[2] + parts[3] + parts[4]
+        steps = parts[1] + 2.0 * parts[2] + 3.0 * parts[3] + 4.0 * parts[4]
+        down = 4.0 * steps + whole * (slot_row - float(r % 2 + RADIUS))
+        stats = [
+            jnp.sum(x, axis=-1, keepdims=True) for x in (down, whole * slot_col, whole)
+        ]
+        stat_s[r % 2, rows] = jnp.where(
+            lane == 0, stats[0], jnp.where(lane == 1, stats[1], jnp.where(lane == 2, stats[2], 0.0))
+        )
+
+    sums = [stat_s[par] for par in range(2)]
     hidden = [dot(e_s[par], w_hid[par * PACKED : (par + 1) * PACKED]) for par in range(2)]
     flows = []
     for par in range(2):
         scale = 1.0 / sums[par][:, 2:3]
-        act = jax.nn.gelu(hidden[par] * (scale * OFFS) + b_hid[...]).astype(jnp.bfloat16)
+        act = jax.nn.gelu(hidden[par] * (scale * OFFS) + vectors[3:4]).astype(jnp.bfloat16)
         flow = sums[par] * scale + dot(act, w_flow[...]) + b_flow[...]
         flows.append(flow.T[:WIN])
     flow = jnp.concatenate(flows, axis=0)
@@ -371,8 +407,8 @@
 
 
 def prepare(
-    w_qkv, b_qkv, w_hid, w_flow, b_flow, rel,
-    w_qv, b_qv, packed, flow_w, flow_b, bias, w_off, turn, back,
+    gain, shift, w_qkv, b_qkv, rel, w_out, b_out, w_hid, b_hid, w_flow, b_flow,
+    vectors, w_k, w_o, w_qv, b_qv, packed, flow_w, flow_b, bias, turn, back,
 ):
     def iota(shape, dim):
         return lax.broadcasted_iota(jnp.int32, shape, dim)
@@ -388,10 +424,6 @@
     inside = (dr >= 0) & (dr < SPAN) & (dc < SPAN)
     place = jnp.where(inside, dr * SPAN + dc, -1)
     pick = onehot(iota((2 * PACKED, OFFS), 1) == place)
-    which = iota((2 * PACKED, 128), 1)
-    offs = jnp.where(which == 0, dr - RADIUS, jnp.where(which == 1, dc - RADIUS, 1))
-    offs = jnp.where(inside & (which < 3), offs, 0)
-    w_off[...] = offs.astype(jnp.float32).astype(jnp.bfloat16)
     at = iota(turn.shape, 0)
     col = HALO_A + COLS - 1 - at % COLS
     source = col // WIN * CELLS + at // COLS * WIN + col % WIN
@@ -405,6 +437,12 @@
     cell = at % 128 // 16 * WIN + at % 16
     squeeze = onehot((at % 16 < WIN) & (iota(at.shape, 1) == at // 128 * CELLS + cell))
 
+    for n, row in enumerate((gain, shift, b_out, b_hid)):
+        vectors[n : n + 1] = row[...]
+    vectors[4:5] = b_qkv[:, C : 2 * C]
+    vectors[5:8] = jnp.zeros((3, C), jnp.float32)
+    w_k[...] = w_qkv[:, C : 2 * C]
+    w_o[...] = w_out[...]
     w_qv[:C] = w_qkv[:, :C].T
     w_qv[C:] = w_qkv[:, 2 * C :].T
     b = b_qkv[...]
@@ -483,94 +521,112 @@
     made_ready = pl.pallas_call(
         prepare,
         out_shape=(
+            made_f32(8, C),
+            made(C, C),
+            made(C, C),
             made(2 * C, C),
             made_f32(2 * C, 128),
             made(2 * PACKED, C),
             made(C, 128),
             made_f32(1, 128),
             made_f32(4, CELLS, HEADS * CELLS),
-            made(2 * PACKED, 128),
             made(WIN * COLS, WIDE_A * CELLS),
             made(C, C),
         ),
-        in_specs=[whole] * 6,
-        out_specs=(whole,) * 9,
+        in_specs=[whole] * 11,
+        out_specs=(whole,) * 11,
         compiler_params=params,
         cost_estimate=pl.CostEstimate(flops=10**9, bytes_accessed=4 * 10**6, transcendentals=0),
-    )(w_qkv, b_qkv[None], w_hid, w_flow, b_flow[None], rel_table)
+    )(
+        ln_gain[None],
+        ln_shift[None],
+        w_qkv,
+        b_qkv[None],
+        rel_table,
+        w_out,
+        b_out[None],
+        w_hid,
+        b_hid[None],
+        w_flow,
+        b_flow[None],
+    )
     strip = jax.ShapeDtypeStruct((ROWS, HALO_A + HALO_B, C), jnp.bfloat16)
-    far, near = pl.pallas_call(
+    near, far = pl.pallas_call(
         pack_cols,
         out_shape=(strip, strip),
         in_specs=[scalars, whole, whole],
-        out_specs=(whole, whole),
+        out_specs=(whole,) * 2,
         compiler_params=params,
     )(ids, section_a, section_b)
     far = swap(far, "col", 1)
     near = swap(near, "col", 0)
-    far, near, made_ready = lax.optimization_barrier((far, near, made_ready))
-    w_qv, b_qv, packed, flow_pad, b_flow_pad, bias, w_off, turn, back = made_ready
+    near, far, made_ready = lax.optimization_barrier((near, far, made_ready))
+    vectors, w_k, w_o, w_qv, b_qv, packed, flow_pad, b_flow_pad, bias, turn, back = made_ready
     sent = jax.ShapeDtypeStruct((SENT, C), jnp.bfloat16)
-    mid, far, near = pl.pallas_call(
+    mid, near, far = pl.pallas_call(
         pack_rows,
         out_shape=(jax.ShapeDtypeStruct((MID, C), jnp.bfloat16), sent, sent),
         in_specs=[scalars] + [whole] * 4,
         out_specs=(whole,) * 3,
         compiler_params=params,
-    )(ids, section_a, section_b, far, near)
+    )(ids, section_a, section_b, near, far)
+    near = swap(near, "row", 0)
     far = swap(far, "row", 1)
-    near = swap(near, "row", 0)
-
-    side = (WIDE_B + WIDE_A) * CELLS
-    tables = (ln_gain[None], ln_shift[None], w_qkv, b_qkv[None], w_qv, b_qv, bias, w_out, b_out[None])
-    outer, centre_b, centre_a = pl.pallas_call(
-        centre,
-        out_shape=(made(side, C), made(WIN * KEYS, C), made(WIN * COLS, C)),
-        in_specs=[scalars] + [whole] * 11,
-        out_specs=(whole,) * 3,
-        scratch_shapes=[
-            pltpu.VMEM((C, side), jnp.bfloat16),
-            pltpu.VMEM((side, C), jnp.bfloat16),
-            pltpu.VMEM((C, side), jnp.bfloat16),
-            pltpu.VMEM((side, C), jnp.bfloat16),
-        ],
+
+    tables = (vectors, w_k, w_qv, b_qv, bias, w_o, turn)
+
+    def rooms(cells):
+        return [
+            pltpu.VMEM((TOTAL, C), jnp.bfloat16),
+            pltpu.VMEM((C, cells), jnp.bfloat16),
+            pltpu.VMEM((cells, C), jnp.bfloat16),
+            pltpu.VMEM((C, cells), jnp.bfloat16),
+            pltpu.VMEM((cells, C), jnp.bfloat16),
+        ]
+
+    outer, centre_b, centre_a, near_b, near_a = pl.pallas_call(
+        early,
+        out_shape=(
+            made(CENTRE, C),
+            made(WIN * KEYS, C),
+            made(WIN * COLS, C),
+            made(FLANK, C),
+            made(WIN * COLS, C),
+        ),
+        in_specs=[scalars] + [whole] * 9,
+        out_specs=(whole,) * 5,
+        scratch_shapes=rooms(CENTRE + TOTAL),
         compiler_params=params,
-        cost_estimate=pl.CostEstimate(flops=2 * 10**9, bytes_accessed=4 * 10**6, transcendentals=0),
-    )(ids, mid, *tables, turn)
-
-    call = pl.pallas_call(
+        cost_estimate=pl.CostEstimate(flops=4 * 10**9, bytes_accessed=4 * 10**6, transcendentals=0),
+    )(ids, near, mid, *tables)
+
+    return pl.pallas_call(
         body,
         out_shape=jax.ShapeDtypeStruct((2, ROWS, COLS), jnp.float32),
-        in_specs=[scalars] + [whole] * 22,
+        in_specs=[scalars] + [whole] * 18,
         out_specs=whole,
-        scratch_shapes=[
-            pltpu.VMEM((TOTAL, C), jnp.bfloat16),
-            pltpu.VMEM((C, TOTAL), jnp.bfloat16),
-            pltpu.VMEM((TOTAL, C), jnp.bfloat16),
-            pltpu.VMEM((C, TOTAL), jnp.bfloat16),
-            pltpu.VMEM((TOTAL, C), jnp.bfloat16),
+        scratch_shapes=rooms(TOTAL)
+        + [
             pltpu.VMEM((HIGH_B * WIN * KEYS, C), jnp.bfloat16),
             pltpu.VMEM((HIGH_A * WIN * COLS, C), jnp.bfloat16),
             pltpu.VMEM((ROWS * COLS, GRAM), jnp.float32),
             pltpu.VMEM((2, ROWS // 2 * COLS, PACKED), jnp.bfloat16),
+            pltpu.VMEM((2, ROWS // 2 * COLS, 128), jnp.float32),
         ],
         compiler_params=params,
-    )
-    return call(
+    )(
         ids,
+        far,
         mid,
-        far,
-        near,
         outer,
+        near_b,
+        near_a,
         centre_b,
         centre_a,
         *tables,
         packed,
-        w_off,
-        b_hid[None],
         flow_pad,
         b_flow_pad,
-        turn,
         back,
     )
 

time: 45.9 us -> 44.7 us (0.974)
  the two profiles are of different devices: /device:TPU:16 before, /device:TPU:7 now
where the time goes in v4:
time: 44.7 us; the launch traced here: 44.4 us
  starting transfers between devices  22.2 us (50%)
  Pallas kernels  16.2 us (36%)
  local copies, waits for them, and re-layouts  3.66 us (8%)
  waiting for transfers between devices  2.12 us (5%)
    ppermute x4, starting transfers between devices, swap(): return lax.ppermute(array, axis, pairs)  22.2 us
    pallas_call x1, Pallas kernels, shards(): pl.pallas_call(body, out_shape=jax.ShapeDtypeStruct((2, ROWS, COLS), jnp....  7.12 us
    pallas_call x1, Pallas kernels, shards(): pl.pallas_call(early, out_shape=(made(CENTRE, C), made(WIN * KEYS, C), ma...  6.11 us
    unnamed x31, local copies, waits for them, and re-layouts  3.66 us
    ppermute x4, waiting for transfers between devices, swap(): return lax.ppermute(array, axis, pairs)  2.12 us
    pallas_call x1, Pallas kernels, shards(): pl.pallas_call(prepare, out_shape=(made_f32(8, C), made(C, C), made(C, C)...  1.54 us
  transfers between devices with their start and end apart: 4, of which 1 were waited for; matrix products, arithmetic and copies ran while one was open for 0% of the time, Pallas kernels for 17%

profile of v4, /device:TPU:7, one launch (start us, length us, event | category | flops | bytes accessed | tf_op | source)
XLA Modules:
  0.0 44.4 jit_solution(8746950431235062712)
XLA Ops:
  0.0 0.1 pad_add_fusion.ids
  0.1 0.9 %copy-done = bf16[16,32,256]{2,1,0:T(8,128)(2,1)S(1)} copy-done((bf16[16,32,256]{2,1,0:T(8,128)(2,1)S(1)}, bf16[16,32,256]{2,1,0:T(8,128)(2,1)}, u32[]{:S(2)}) %copy-start) | copy-done | bytes 262168
  1.0 0.9 %copy-done.2 = bf16[16,32,256]{2,1,0:T(8,128)(2,1)S(1)} copy-done((bf16[16,32,256]{2,1,0:T(8,128)(2,1)S(1)}, bf16[16,32,256]{2,1,0:T(8,128)(2,1)}, u32[]{:S(2)}) %copy-start.2) | copy-done | bytes 262168
  2.0 0.6 %shard_map.127 = (bf16[16,16,256]{2,1,0:T(8,128)(2,1)S(1)}, bf16[16,16,256]{2,1,0:T(8,128)(2,1)S(1)}) custom-call(s32[4]{0:T(128)S(1)} %pad_add_fusion.ids, bf16[16,32,256]{2,1,0:T(8,128)(2,1)S(1)} %copy-done, bf16[16,32,256]{2,1,0:T(8,128)(2,1)S(1)} %copy-done.2), custom_call_target="tpu_custom_call" | custom-call | tf_op jit(solution)/shard_map/pallas_call | solution.py:554
  2.6 3.2 %collective-permute-start = (bf16[16,16,256]{2,1,0:T(8,128)(2,1)S(1)}, bf16[16,16,256]{2,1,0:T(8,128)(2,1)S(1)}, u32[]{:S(2)}, u32[]{:S(2)}) collective-permute-start(bf16[16,16,256]{2,1,0:T(8,128)(2,1)S(1)} %get-tuple-element.39), channel_id=1, source_target_pairs={{0,1},{1,0},{2,3},{3,2},{4,5},{5,4},{6,7},{7,6},{8,9},{9,8},{10,11... | collective-permute-start | bytes 393224 | tf_op jit(solution)/shard_map/ppermute | solution.py:40
  5.8 11.0 %collective-permute-start.1 = (bf16[16,16,256]{2,1,0:T(8,128)(2,1)S(1)}, bf16[16,16,256]{2,1,0:T(8,128)(2,1)S(1)}, u32[]{:S(2)}, u32[]{:S(2)}) collective-permute-start(bf16[16,16,256]{2,1,0:T(8,128)(2,1)S(1)} %get-tuple-element.40), channel_id=1, source_target_pairs={{0,31},{1,2},{2,1},{3,4},{4,3},{5,6},{6,5},{7,8},{8,7},{9,10},{10,... | collective-permute-start | bytes 393224 | tf_op jit(solution)/shard_map/ppermute | solution.py:40
  16.8 0.0 copy-done.13
  16.9 0.0 copy-done.14
  16.9 0.0 copy-start.9
  16.9 0.0 copy-start.10
  16.9 0.0 copy-start.11
  16.9 0.0 copy-start.12
  16.9 0.1 copy.14.w_flow
  17.1 0.0 copy-start.8
  17.1 0.0 copy-done.4
  17.1 0.0 copy-done.5
  17.1 0.4 %copy-done.9 = f32[256]{0:T(256)S(1)} copy-done((f32[256]{0:T(256)S(1)}, f32[256]{0:T(256)}, u32[]{:S(2)}) %copy-start.9) | copy-done | bytes 1048
  17.6 0.0 copy-done.10
  17.6 0.0 copy-done.11
  17.6 0.0 copy-done.12
  17.6 0.2 copy-done.7
  17.8 0.9 %copy-done.6 = bf16[256,256]{1,0:T(8,128)(2,1)S(1)} copy-done((bf16[256,256]{1,0:T(8,128)(2,1)S(1)}, bf16[256,256]{1,0:T(8,128)(2,1)}, u32[]{:S(2)}) %copy-start.6) | copy-done | bytes 131096
  18.7 1.5 %shard_map.128 = (f32[8,256]{1,0:T(8,128)S(1)}, bf16[256,256]{1,0:T(8,128)(2,1)S(1)}, bf16[256,256]{1,0:T(8,128)(2,1)S(1)}, bf16[512,256]{1,0:T(8,128)(2,1)S(1)}...) custom-call(f32[1,256]{1,0:T(1,128)S(1)} %bitcast.7, ...), custom_call_target="tpu_custom_call" | custom-call | flops 1000000000 | bytes 4000000 | tf_op jit(solution)/shard_map/pallas_call | solution.py:521
  20.2 0.0 collective-permute-done.near_ref
  20.2 0.0 collective-permute-done.1.far_ref
  20.3 0.8 %shard_map.129 = (bf16[1536,256]{1,0:T(8,128)(2,1)S(1)}, bf16[832,256]{1,0:T(8,128)(2,1)S(1)}, bf16[832,256]{1,0:T(8,128)(2,1)S(1)}) custom-call(s32[4]{0:T(128)S(1)} %pad_add_fusion.ids, bf16[16,32,256]{2,1,0:T(8,128)(2,1)S(1)} %copy-done.1, bf16[16,32,256]{2,1,0:T(8,128)(2,1)S(1)} %copy-done.3, bf16[16,16,256]{2,1,0:T(8,128)(2,1)S(1)} %collective-permute-done.near_ref, ...), custom_call_target="tpu_custom_call" | custom-call | tf_op jit(solution)/shard_map/pallas_call | solution.py:566
  21.1 3.1 %collective-permute-start.3 = (bf16[832,256]{1,0:T(8,128)(2,1)S(1)}, bf16[832,256]{1,0:T(8,128)(2,1)S(1)}, u32[]{:S(2)}, u32[]{:S(2)}) collective-permute-start(bf16[832,256]{1,0:T(8,128)(2,1)S(1)} %get-tuple-element.56), channel_id=1, source_target_pairs={{0,32},{32,0},{64,96},{96,64},{128,160},{160,128},{192,224},{224,1... | collective-permute-start | bytes 1277960 | tf_op jit(solution)/shard_map/ppermute | solution.py:40
  24.2 4.8 %collective-permute-start.2 = (bf16[832,256]{1,0:T(8,128)(2,1)S(1)}, bf16[832,256]{1,0:T(8,128)(2,1)S(1)}, u32[]{:S(2)}, u32[]{:S(2)}) collective-permute-start(bf16[832,256]{1,0:T(8,128)(2,1)S(1)} %get-tuple-element.54), channel_id=1, source_target_pairs={{0,480},{32,64},{64,32},{96,128},{128,96},{160,192},{192,160},{224... | collective-permute-start | bytes 1277960 | tf_op jit(solution)/shard_map/ppermute | solution.py:40
  29.0 0.0 collective-permute-done.3.got
  29.0 6.1 %shard_map.130 = (bf16[768,256]{1,0:T(8,128)(2,1)S(1)}, bf16[512,256]{1,0:T(8,128)(2,1)S(1)}, bf16[256,256]{1,0:T(8,128)(2,1)S(1)}, bf16[1024,256]{1,0:T(8,128)(2,1)S(1)}, bf16[256,256]{1,0:T(8,128)(2,1)S(1)}) custom-call(s32[4]{0:T(128)S(1)} %pad_add_fusion.ids, bf16[832,256]{1,0:T(8,128)(2,1)S(1)} %collective-permute-done.3.got, ...), custom_call_target="tpu_custom_call" | custom-call | flops 4000000000 | bytes 4000000 | tf_op jit(solution)/shard_map/pallas_call | solution.py:587
  35.2 2.1 %collective-permute-done.2.got = bf16[832,256]{1,0:T(8,128)(2,1)S(1)} collective-permute-done((bf16[832,256]{1,0:T(8,128)(2,1)S(1)}, bf16[832,256]{1,0:T(8,128)(2,1)S(1)}, u32[]{:S(2)}, u32[]{:S(2)}) %collective-permute-start.2) | collective-permute-done | bytes 426016 | tf_op jit(solution)/shard_map/ppermute | solution.py:40
  37.3 7.1 %shard_map.131 = f32[2,16,32]{2,1,0:T(8,128)} custom-call(s32[4]{0:T(128)S(1)} %pad_add_fusion.ids, bf16[832,256]{1,0:T(8,128)(2,1)S(1)} %collective-permute-done.2.got, bf16[1536,256]{1,0:T(8,128)(2,1)S(1)} %get-tuple-element.55.mid, bf16[768,256]{1,0:T(8,128)(2,1)S(1)} %get-tuple-element.64.outer, bf16[1024,256]{1,0:T(8,128)(2,1)S(1)} %get-tuple-element.65.near_b, ...), custom_call_target="tpu_custom_call" | custom-call | tf_op jit(solution)/shard_map/pallas_call | solution.py:603
  (14 shorter events, 0.0 us)
Async XLA Ops:
  0.0 16.8 %copy-start.13 = (f32[768]{0:T(1024)S(1)}, f32[768]{0:T(1024)}, u32[]{:S(2)}) copy-start(f32[768]{0:T(1024)} %param.18) | copy-start | bytes 9220
  0.0 16.9 %copy-start.14 = (bf16[256,2]{0,1:T(2,128)(2,1)S(1)}, bf16[256,2]{0,1:T(2,128)(2,1)}, u32[]{:S(2)}) copy-start(bf16[256,2]{0,1:T(2,128)(2,1)} %param.24) | copy-start | bytes 3076
  0.1 1.0 %copy-start = (bf16[16,32,256]{2,1,0:T(8,128)(2,1)S(1)}, bf16[16,32,256]{2,1,0:T(8,128)(2,1)}, u32[]{:S(2)}) copy-start(bf16[16,32,256]{2,1,0:T(8,128)(2,1)} %a_ref.3) | copy-start | bytes 786436
  1.0 0.9 %copy-start.2 = (bf16[16,32,256]{2,1,0:T(8,128)(2,1)S(1)}, bf16[16,32,256]{2,1,0:T(8,128)(2,1)}, u32[]{:S(2)}) copy-start(bf16[16,32,256]{2,1,0:T(8,128)(2,1)} %b_ref.3) | copy-start | bytes 786436
  2.0 15.1 %copy-start.4 = (bf16[256,768]{1,0:T(8,128)(2,1)S(1)}, bf16[256,768]{1,0:T(8,128)(2,1)}, u32[]{:S(2)}) copy-start(bf16[256,768]{1,0:T(8,128)(2,1)} %w_qkv.1) | copy-start | bytes 1179652
  2.0 15.1 %copy-start.5 = (bf16[289,256]{1,0:T(8,128)(2,1)S(1)}, bf16[289,256]{1,0:T(8,128)(2,1)}, u32[]{:S(2)}) copy-start(bf16[289,256]{1,0:T(8,128)(2,1)} %w_hid.1) | copy-start | bytes 443908
  2.6 17.6 %collective-permute-start = (bf16[16,16,256]{2,1,0:T(8,128)(2,1)S(1)}, bf16[16,16,256]{2,1,0:T(8,128)(2,1)S(1)}, u32[]{:S(2)}, u32[]{:S(2)}) collective-permute-start(bf16[16,16,256]{2,1,0:T(8,128)(2,1)S(1)} %get-tuple-element.39), channel_id=1, source_target_pairs={{0,1},{1,0},{2,3},{3,2},{4,5},{5,4},{6,7},{7,6},{8,9},{9,8},{10,11... | collective-permute-start | bytes 393224 | tf_op jit(solution)/shard_map/ppermute | solution.py:40
  5.8 14.4 %collective-permute-start.1 = (bf16[16,16,256]{2,1,0:T(8,128)(2,1)S(1)}, bf16[16,16,256]{2,1,0:T(8,128)(2,1)S(1)}, u32[]{:S(2)}, u32[]{:S(2)}) collective-permute-start(bf16[16,16,256]{2,1,0:T(8,128)(2,1)S(1)} %get-tuple-element.40), channel_id=1, source_target_pairs={{0,31},{1,2},{2,1},{3,4},{4,3},{5,6},{6,5},{7,8},{8,7},{9,10},{10,... | collective-permute-start | bytes 393224 | tf_op jit(solution)/shard_map/ppermute | solution.py:40
  16.9 0.7 %copy-start.9 = (f32[256]{0:T(256)S(1)}, f32[256]{0:T(256)}, u32[]{:S(2)}) copy-start(f32[256]{0:T(256)} %param.16) | copy-start | bytes 3076
  16.9 0.7 %copy-start.10 = (f32[256]{0:T(256)S(1)}, f32[256]{0:T(256)}, u32[]{:S(2)}) copy-start(f32[256]{0:T(256)} %param.21) | copy-start | bytes 3076
  16.9 0.7 %copy-start.11 = (f32[256]{0:T(256)S(1)}, f32[256]{0:T(256)}, u32[]{:S(2)}) copy-start(f32[256]{0:T(256)} %param.23) | copy-start | bytes 3076
  16.9 0.7 %copy-start.12 = (f32[2]{0:T(128)S(1)}, f32[2]{0:T(128)}, u32[]{:S(2)}) copy-start(f32[2]{0:T(128)} %param.25) | copy-start | bytes 28
  17.1 0.7 %copy-start.7 = (f32[8,225]{1,0:T(8,128)S(1)}, f32[8,225]{1,0:T(8,128)}, u32[]{:S(2)}) copy-start(f32[8,225]{1,0:T(8,128)} %rel.1) | copy-start | bytes 21604
  17.1 0.7 %copy-start.8 = (f32[256]{0:T(256)S(1)}, f32[256]{0:T(256)}, u32[]{:S(2)}) copy-start(f32[256]{0:T(256)} %param.15) | copy-start | bytes 3076
  17.8 0.9 %copy-start.6 = (bf16[256,256]{1,0:T(8,128)(2,1)S(1)}, bf16[256,256]{1,0:T(8,128)(2,1)}, u32[]{:S(2)}) copy-start(bf16[256,256]{1,0:T(8,128)(2,1)} %w_out.1) | copy-start | bytes 393220
  18.7 1.6 %copy-start.1 = (bf16[16,32,256]{2,1,0:T(8,128)(2,1)S(1)}, bf16[16,32,256]{2,1,0:T(8,128)(2,1)}, u32[]{:S(2)}) copy-start(bf16[16,32,256]{2,1,0:T(8,128)(2,1)} %a_ref.3) | copy-start | bytes 786436
  18.7 1.6 %copy-start.3 = (bf16[16,32,256]{2,1,0:T(8,128)(2,1)S(1)}, bf16[16,32,256]{2,1,0:T(8,128)(2,1)}, u32[]{:S(2)}) copy-start(bf16[16,32,256]{2,1,0:T(8,128)(2,1)} %b_ref.3) | copy-start | bytes 786436
  21.1 8.0 %collective-permute-start.3 = (bf16[832,256]{1,0:T(8,128)(2,1)S(1)}, bf16[832,256]{1,0:T(8,128)(2,1)S(1)}, u32[]{:S(2)}, u32[]{:S(2)}) collective-permute-start(bf16[832,256]{1,0:T(8,128)(2,1)S(1)} %get-tuple-element.56), channel_id=1, source_target_pairs={{0,32},{32,0},{64,96},{96,64},{128,160},{160,128},{192,224},{224,1... | collective-permute-start | bytes 1277960 | tf_op jit(solution)/shard_map/ppermute | solution.py:40
  24.2 13.1 %collective-permute-start.2 = (bf16[832,256]{1,0:T(8,128)(2,1)S(1)}, bf16[832,256]{1,0:T(8,128)(2,1)S(1)}, u32[]{:S(2)}, u32[]{:S(2)}) collective-permute-start(bf16[832,256]{1,0:T(8,128)(2,1)S(1)} %get-tuple-element.54), channel_id=1, source_target_pairs={{0,480},{32,64},{64,32},{96,128},{128,96},{160,192},{192,160},{224... | collective-permute-start | bytes 1277960 | tf_op jit(solution)/shard_map/ppermute | solution.py:40

commit v5 on v4

--- a/solution.py
+++ b/solution.py
@@ -28,7 +28,7 @@
 HALF = C // 2
 PACKED = 5 * 128
 KEYS = 64
-GRAM = (ROWS + 2 * RADIUS) * KEYS
+SOON, LATE = 4, 12
 FLANK = 2 * WIN * KEYS
 LOG2E = 1.4426950408889634
 NT = (((1,), (1,)), ((), ()))
@@ -262,9 +262,95 @@
     finish(ids, column(x_s, *strips[2]), sums[2], vectors, mirror, None, fa, 0)
 
 
+def correlate(
+    count, queries, keys, vectors, w_hid, w_flow, b_flow, unmirror, g_s, e_s, stat_s
+):
+    lane = lax.broadcasted_iota(jnp.int32, (COLS, 128), 1)
+    valid = lane % 32 < SPAN
+    fore = lane % KEYS < 32
+    first = valid & (lane < 32)
+    slot = lane // 32
+    slot_row = jnp.where(slot == 1, 3, jnp.where(slot == 3, 2, slot // 2)).astype(jnp.float32)
+    slot_col = (lane % 32 - RADIUS).astype(jnp.float32)
+    second = valid & (lane >= 32)
+
+    for start in range(0, count + 2 * RADIUS, 8):
+        stop = min(count + 2 * RADIUS, start + 8)
+        top, end = max(0, start - 2 * RADIUS), min(count, stop)
+        g_s[top * COLS : end * COLS, start * KEYS : stop * KEYS] = lax.dot_general(
+            queries[top * COLS : end * COLS],
+            keys[start * KEYS : stop * KEYS],
+            NT,
+            preferred_element_type=jnp.float32,
+        )
+
+    def align(r, n):
+        at = 128 * (n + r // 2)
+        tile = g_s[COLS * r : COLS * (r + 1), at : at + 128]
+        turn = 128 - HALO_A - COLS + 1 - 32 * (n % 2)
+        return pltpu.roll(tile, turn, 1, stride=1, stride_axis=0)
+
+    for r in range(count):
+        tiles = []
+        for n in range(5):
+            tile = align(r, 2 * n)
+            if n < 4:
+                tile = jnp.where(fore, tile, align(r, 2 * n + 1))
+            keep = valid
+            if r % 2 == 0 and n == 4:
+                keep = first
+            if r % 2 == 1 and n == 0:
+                keep = second
+            if n == 4 and r % 2 == 1:
+                keep = valid & fore
+            tiles.append(jnp.where(keep, tile * (C**-0.5 * LOG2E), -1e30))
+        most = tiles[0]
+        for tile in tiles[1:]:
+            most = jnp.maximum(most, tile)
+        most = jnp.max(most, axis=-1, keepdims=True)
+        rows = slice((r // 2) * COLS, (r // 2 + 1) * COLS)
+        parts = [jnp.exp2(tile - most) for tile in tiles]
+        for n, part in enumerate(parts):
+            e_s[r % 2, rows, 128 * n : 128 * (n + 1)] = part.astype(jnp.bfloat16)
+        whole = parts[0] + parts[1] + parts[2] + parts[3] + parts[4]
+        steps = parts[1] + 2.0 * parts[2] + 3.0 * parts[3] + 4.0 * parts[4]
+        down = 4.0 * steps + whole * (slot_row - float(r % 2 + RADIUS))
+        stats = [
+            jnp.sum(x, axis=-1, keepdims=True) for x in (down, whole * slot_col, whole)
+        ]
+        stat_s[r % 2, rows] = jnp.where(
+            lane == 0, stats[0], jnp.where(lane == 1, stats[1], jnp.where(lane == 2, stats[2], 0.0))
+        )
+
+    sums = [stat_s[par] for par in range(2)]
+    hidden = [dot(e_s[par], w_hid[par * PACKED : (par + 1) * PACKED]) for par in range(2)]
+    flows = []
+    for par in range(2):
+        scale = 1.0 / sums[par][:, 2:3]
+        act = jax.nn.gelu(hidden[par] * (scale * OFFS) + vectors[3:4]).astype(jnp.bfloat16)
+        flow = sums[par] * scale + dot(act, w_flow[...]) + b_flow[...]
+        size = count // 2 * COLS
+        more = -size % 128
+        if more:
+            flow = jnp.concatenate([flow, jnp.zeros((more, 128), jnp.float32)], axis=0)
+        flows.append(flow.T[:WIN])
+    flow = jnp.concatenate(flows, axis=0)
+    high = flow.astype(jnp.bfloat16)
+    rest = flow - high.astype(jnp.float32)
+    mid = rest.astype(jnp.bfloat16)
+    tail = (rest - mid.astype(jnp.float32)).astype(jnp.bfloat16)
+    turned = unmirror[: flow.shape[1], : flow.shape[1]]
+    flow = dot(high, turned) + dot(mid, turned) + dot(tail, turned)
+    return [
+        flow[WIN * (r % 2) : WIN * (r % 2) + 2, COLS * (r // 2) : COLS * (r // 2 + 1)]
+        for r in range(count)
+    ]
+
+
 def early(
-    ids, got, mid, vectors, w_k, w_qv, b_qv, bias, w_out, mirror,
-    outer, centre_b, centre_a, near_b, near_a, x_s, q_s, k_s, v_s, mix_s,
+    ids, got, mid, vectors, w_k, w_qv, b_qv, bias, w_out, mirror, w_hid, w_flow, b_flow, unmirror,
+    outer, centre_b, centre_a, near_b, near_a, ready,
+    x_s, q_s, k_s, v_s, mix_s, fb, g_s, e_s, stat_s,
 ):
     top = ids[0] % 2 == 1
     cells, tables = centre_windows(
@@ -279,6 +365,18 @@
     finish(ids, jnp.concatenate(cells[:WIDE_B], axis=0), sum_b, vectors, mirror, 2, centre_b, 0)
     finish(ids, jnp.concatenate(cells[WIDE_B:], axis=0), sum_a, vectors, mirror, None, centre_a, 0)
     flank_features(ids, top, vectors, w_out, mirror, near_b, near_a, x_s, mix_s, CENTRE)
+    strip = WIN * KEYS
+    fb[pl.ds(pl.multiple_of(jnp.where(top, FLANK, 0), strip), strip)] = centre_b[...]
+    fb[pl.ds(pl.multiple_of(jnp.where(top, 0, strip), strip), FLANK)] = near_b[...]
+    skip = jnp.where(top, HALO_A, 0)
+    queries = near_a.at[pl.ds(pl.multiple_of(skip * COLS, COLS), SOON * COLS)]
+    reach = (SOON + 2 * RADIUS) * KEYS
+    keys = fb.at[pl.ds(pl.multiple_of(skip * KEYS, KEYS), reach)]
+    flows = correlate(
+        SOON, queries, keys, vectors, w_hid, w_flow, b_flow, unmirror, g_s, e_s, stat_s
+    )
+    for r, flow in enumerate(flows):
+        ready[:, r, :] = flow
 
 
 def body(
@@ -290,6 +388,7 @@
     near_a,
     centre_b,
     centre_a,
+    ready,
     vectors,
     w_k,
     w_qv,
@@ -331,79 +430,18 @@
         ids, even, vectors, w_out, mirror, fb.at[here_b], fa.at[here_a], x_s, mix_s, 0
     )
 
-    lane = lax.broadcasted_iota(jnp.int32, (COLS, 128), 1)
-    valid = lane % 32 < SPAN
-    fore = lane % KEYS < 32
-    first = valid & (lane < 32)
-    slot = lane // 32
-    slot_row = jnp.where(slot == 1, 3, jnp.where(slot == 3, 2, slot // 2)).astype(jnp.float32)
-    slot_col = (lane % 32 - RADIUS).astype(jnp.float32)
-    second = valid & (lane >= 32)
-
-    for n in range(4):
-        top, end = max(0, 8 * n - 16), min(ROWS, 8 * n + 8)
-        queries = fa[(HALO_A + top) * COLS : (HALO_A + end) * COLS]
-        start = (HALO_B - RADIUS + 8 * n) * KEYS
-        keys = fb[start : start + 8 * KEYS]
-        g_s[top * COLS : end * COLS, 8 * KEYS * n : 8 * KEYS * (n + 1)] = lax.dot_general(
-            queries, keys, NT, preferred_element_type=jnp.float32
-        )
-
-    def align(r, n):
-        at = 128 * (n + r // 2)
-        tile = g_s[COLS * r : COLS * (r + 1), at : at + 128]
-        turn = 128 - HALO_A - COLS + 1 - 32 * (n % 2)
-        return pltpu.roll(tile, turn, 1, stride=1, stride_axis=0)
-
-    for r in range(ROWS):
-        tiles = []
-        for n in range(5):
-            tile = align(r, 2 * n)
-            if n < 4:
-                tile = jnp.where(fore, tile, align(r, 2 * n + 1))
-            keep = valid
-            if r % 2 == 0 and n == 4:
-                keep = first
-            if r % 2 == 1 and n == 0:
-                keep = second
-            if n == 4 and r % 2 == 1:
-                keep = valid & fore
-            tiles.append(jnp.where(keep, tile * (C**-0.5 * LOG2E), -1e30))
-        most = tiles[0]
-        for tile in tiles[1:]:
-            most = jnp.maximum(most, tile)
-        most = jnp.max(most, axis=-1, keepdims=True)
-        rows = slice((r // 2) * COLS, (r // 2 + 1) * COLS)
-        parts = [jnp.exp2(tile - most) for tile in tiles]
-        for n, part in enumerate(parts):
-            e_s[r % 2, rows, 128 * n : 128 * (n + 1)] = part.astype(jnp.bfloat16)
-        whole = parts[0] + parts[1] + parts[2] + parts[3] + parts[4]
-        steps = parts[1] + 2.0 * parts[2] + 3.0 * parts[3] + 4.0 * parts[4]
-        down = 4.0 * steps + whole * (slot_row - float(r % 2 + RADIUS))
-        stats = [
-            jnp.sum(x, axis=-1, keepdims=True) for x in (down, whole * slot_col, whole)
-        ]
-        stat_s[r % 2, rows] = jnp.where(
-            lane == 0, stats[0], jnp.where(lane == 1, stats[1], jnp.where(lane == 2, stats[2], 0.0))
-        )
-
-    sums = [stat_s[par] for par in range(2)]
-    hidden = [dot(e_s[par], w_hid[par * PACKED : (par + 1) * PACKED]) for par in range(2)]
-    flows = []
-    for par in range(2):
-        scale = 1.0 / sums[par][:, 2:3]
-        act = jax.nn.gelu(hidden[par] * (scale * OFFS) + vectors[3:4]).astype(jnp.bfloat16)
-        flow = sums[par] * scale + dot(act, w_flow[...]) + b_flow[...]
-        flows.append(flow.T[:WIN])
-    flow = jnp.concatenate(flows, axis=0)
-    high = flow.astype(jnp.bfloat16)
-    rest = flow - high.astype(jnp.float32)
-    mid = rest.astype(jnp.bfloat16)
-    tail = (rest - mid.astype(jnp.float32)).astype(jnp.bfloat16)
-    flow = dot(high, unmirror[...]) + dot(mid, unmirror[...]) + dot(tail, unmirror[...])
-    for r in range(ROWS):
-        at = WIN * (r % 2)
-        out[:, r, :] = flow[at : at + 2, COLS * (r // 2) : COLS * (r // 2 + 1)]
+    base = jnp.where(even, 0, SOON)
+    rest = jnp.where(even, LATE, 0)
+    queries = fa.at[pl.ds(pl.multiple_of((HALO_A + base) * COLS, COLS), LATE * COLS)]
+    reach = (LATE + 2 * RADIUS) * KEYS
+    keys = fb.at[pl.ds(pl.multiple_of((HALO_B - RADIUS + base) * KEYS, KEYS), reach)]
+    flows = correlate(
+        LATE, queries, keys, vectors, w_hid, w_flow, b_flow, unmirror, g_s, e_s, stat_s
+    )
+    for r, flow in enumerate(flows):
+        out[:, pl.ds(base + r, 1), :] = flow[:, None, :]
+    for r in range(SOON):
+        out[:, pl.ds(rest + r, 1), :] = ready[:, r : r + 1, :]
 
 
 def prepare(
@@ -584,7 +622,14 @@
             pltpu.VMEM((cells, C), jnp.bfloat16),
         ]
 
-    outer, centre_b, centre_a, near_b, near_a = pl.pallas_call(
+    def tiles(count):
+        return [
+            pltpu.VMEM((count * COLS, (count + 2 * RADIUS) * KEYS), jnp.float32),
+            pltpu.VMEM((2, count // 2 * COLS, PACKED), jnp.bfloat16),
+            pltpu.VMEM((2, count // 2 * COLS, 128), jnp.float32),
+        ]
+
+    outer, centre_b, centre_a, near_b, near_a, ready = pl.pallas_call(
         early,
         out_shape=(
             made(CENTRE, C),
@@ -592,27 +637,28 @@
             made(WIN * COLS, C),
             made(FLANK, C),
             made(WIN * COLS, C),
+            made_f32(2, SOON, COLS),
         ),
-        in_specs=[scalars] + [whole] * 9,
-        out_specs=(whole,) * 5,
-        scratch_shapes=rooms(CENTRE + TOTAL),
+        in_specs=[scalars] + [whole] * 13,
+        out_specs=(whole,) * 6,
+        scratch_shapes=rooms(CENTRE + TOTAL)
+        + [pltpu.VMEM((3 * WIN * KEYS, C), jnp.bfloat16)]
+        + tiles(SOON),
         compiler_params=params,
         cost_estimate=pl.CostEstimate(flops=4 * 10**9, bytes_accessed=4 * 10**6, transcendentals=0),
-    )(ids, near, mid, *tables)
+    )(ids, near, mid, *tables, packed, flow_pad, b_flow_pad, back)
 
     return pl.pallas_call(
         body,
         out_shape=jax.ShapeDtypeStruct((2, ROWS, COLS), jnp.float32),
-        in_specs=[scalars] + [whole] * 18,
+        in_specs=[scalars] + [whole] * 19,
         out_specs=whole,
         scratch_shapes=rooms(TOTAL)
         + [
             pltpu.VMEM((HIGH_B * WIN * KEYS, C), jnp.bfloat16),
             pltpu.VMEM((HIGH_A * WIN * COLS, C), jnp.bfloat16),
-            pltpu.VMEM((ROWS * COLS, GRAM), jnp.float32),
-            pltpu.VMEM((2, ROWS // 2 * COLS, PACKED), jnp.bfloat16),
-            pltpu.VMEM((2, ROWS // 2 * COLS, 128), jnp.float32),
-        ],
+        ]
+        + tiles(LATE),
         compiler_params=params,
     )(
         ids,
@@ -623,6 +669,7 @@
         near_a,
         centre_b,
         centre_a,
+        ready,
         *tables,
         packed,
         flow_pad,

time: 44.7 us -> 44.3 us (level)
  waiting for transfers between devices: 2.12 us -> 1.03 us
  Pallas kernels: 16.2 us -> 16.8 us
    pallas_call x1, Pallas kernels: 6.11 us -> 7.21 us  [shards(): pl.pallas_call(early, out_shape=(made(CENTRE, C), made(WIN * KEYS, C), ma...]
    ppermute x4, waiting for transfers between devices: 2.12 us -> 1.03 us  [swap(): return lax.ppermute(array, axis, pairs)]
  transfers between devices with their start and end apart: 4 -> 4, of which waited for: 1 -> 1; matrix products, arithmetic and copies ran while one was open for 0% -> 0% of each run, Pallas kernels for 17% -> 20%
where the time goes in v5:
time: 44.3 us; the launch traced here: 44 us
  starting transfers between devices  22.2 us (50%)
  Pallas kernels  16.8 us (38%)
  local copies, waits for them, and re-layouts  3.66 us (8%)
  waiting for transfers between devices  1.03 us (2%)
    ppermute x4, starting transfers between devices, swap(): return lax.ppermute(array, axis, pairs)  22.2 us
    pallas_call x1, Pallas kernels, shards(): pl.pallas_call(early, out_shape=(made(CENTRE, C), made(WIN * KEYS, C), ma...  7.21 us
    pallas_call x1, Pallas kernels, shards(): pl.pallas_call(body, out_shape=jax.ShapeDtypeStruct((2, ROWS, COLS), jnp....  6.69 us
    unnamed x31, local copies, waits for them, and re-layouts  3.66 us
    pallas_call x1, Pallas kernels, shards(): pl.pallas_call(prepare, out_shape=(made_f32(8, C), made(C, C), made(C, C)...  1.54 us
    ppermute x4, waiting for transfers between devices, swap(): return lax.ppermute(array, axis, pairs)  1.03 us
  transfers between devices with their start and end apart: 4, of which 1 were waited for; matrix products, arithmetic and copies ran while one was open for 0% of the time, Pallas kernels for 20%

profile of v5, /device:TPU:7, one launch (start us, length us, event | category | flops | bytes accessed | tf_op | source)
XLA Modules:
  0.0 44.0 jit_solution(7919674488219624893)
XLA Ops:
  0.0 0.1 pad_add_fusion.ids
  0.1 0.9 %copy-done = bf16[16,32,256]{2,1,0:T(8,128)(2,1)S(1)} copy-done((bf16[16,32,256]{2,1,0:T(8,128)(2,1)S(1)}, bf16[16,32,256]{2,1,0:T(8,128)(2,1)}, u32[]{:S(2)}) %copy-start) | copy-done | bytes 262168
  1.0 0.9 %copy-done.2 = bf16[16,32,256]{2,1,0:T(8,128)(2,1)S(1)} copy-done((bf16[16,32,256]{2,1,0:T(8,128)(2,1)S(1)}, bf16[16,32,256]{2,1,0:T(8,128)(2,1)}, u32[]{:S(2)}) %copy-start.2) | copy-done | bytes 262168
  2.0 0.6 %shard_map.127 = (bf16[16,16,256]{2,1,0:T(8,128)(2,1)S(1)}, bf16[16,16,256]{2,1,0:T(8,128)(2,1)S(1)}) custom-call(s32[4]{0:T(128)S(1)} %pad_add_fusion.ids, bf16[16,32,256]{2,1,0:T(8,128)(2,1)S(1)} %copy-done, bf16[16,32,256]{2,1,0:T(8,128)(2,1)S(1)} %copy-done.2), custom_call_target="tpu_custom_call" | custom-call | tf_op jit(solution)/shard_map/pallas_call | solution.py:592
  2.6 3.2 %collective-permute-start = (bf16[16,16,256]{2,1,0:T(8,128)(2,1)S(1)}, bf16[16,16,256]{2,1,0:T(8,128)(2,1)S(1)}, u32[]{:S(2)}, u32[]{:S(2)}) collective-permute-start(bf16[16,16,256]{2,1,0:T(8,128)(2,1)S(1)} %get-tuple-element.40), channel_id=1, source_target_pairs={{0,1},{1,0},{2,3},{3,2},{4,5},{5,4},{6,7},{7,6},{8,9},{9,8},{10,11... | collective-permute-start | bytes 393224 | tf_op jit(solution)/shard_map/ppermute | solution.py:40
  5.8 11.0 %collective-permute-start.1 = (bf16[16,16,256]{2,1,0:T(8,128)(2,1)S(1)}, bf16[16,16,256]{2,1,0:T(8,128)(2,1)S(1)}, u32[]{:S(2)}, u32[]{:S(2)}) collective-permute-start(bf16[16,16,256]{2,1,0:T(8,128)(2,1)S(1)} %get-tuple-element.41), channel_id=1, source_target_pairs={{0,31},{1,2},{2,1},{3,4},{4,3},{5,6},{6,5},{7,8},{8,7},{9,10},{10,... | collective-permute-start | bytes 393224 | tf_op jit(solution)/shard_map/ppermute | solution.py:40
  16.8 0.0 copy-done.13
  16.9 0.0 copy-done.14
  16.9 0.0 copy-start.9
  16.9 0.0 copy-start.10
  16.9 0.0 copy-start.11
  16.9 0.0 copy-start.12
  16.9 0.1 copy.14.w_flow
  17.1 0.0 copy-start.8
  17.1 0.0 copy-done.4
  17.1 0.0 copy-done.5
  17.1 0.4 %copy-done.9 = f32[256]{0:T(256)S(1)} copy-done((f32[256]{0:T(256)S(1)}, f32[256]{0:T(256)}, u32[]{:S(2)}) %copy-start.9) | copy-done | bytes 1048
  17.6 0.0 copy-done.10
  17.6 0.0 copy-done.11
  17.6 0.0 copy-done.12
  17.6 0.2 copy-done.7
  17.8 0.9 %copy-done.6 = bf16[256,256]{1,0:T(8,128)(2,1)S(1)} copy-done((bf16[256,256]{1,0:T(8,128)(2,1)S(1)}, bf16[256,256]{1,0:T(8,128)(2,1)}, u32[]{:S(2)}) %copy-start.6) | copy-done | bytes 131096
  18.7 1.5 %shard_map.128 = (f32[8,256]{1,0:T(8,128)S(1)}, bf16[256,256]{1,0:T(8,128)(2,1)S(1)}, bf16[256,256]{1,0:T(8,128)(2,1)S(1)}, bf16[512,256]{1,0:T(8,128)(2,1)S(1)}...) custom-call(f32[1,256]{1,0:T(1,128)S(1)} %bitcast.7, ...), custom_call_target="tpu_custom_call" | custom-call | flops 1000000000 | bytes 4000000 | tf_op jit(solution)/shard_map/pallas_call | solution.py:559
  20.2 0.0 collective-permute-done.near_ref
  20.2 0.0 collective-permute-done.1.far_ref
  20.3 0.8 %shard_map.129 = (bf16[1536,256]{1,0:T(8,128)(2,1)S(1)}, bf16[832,256]{1,0:T(8,128)(2,1)S(1)}, bf16[832,256]{1,0:T(8,128)(2,1)S(1)}) custom-call(s32[4]{0:T(128)S(1)} %pad_add_fusion.ids, bf16[16,32,256]{2,1,0:T(8,128)(2,1)S(1)} %copy-done.1, bf16[16,32,256]{2,1,0:T(8,128)(2,1)S(1)} %copy-done.3, bf16[16,16,256]{2,1,0:T(8,128)(2,1)S(1)} %collective-permute-done.near_ref, ...), custom_call_target="tpu_custom_call" | custom-call | tf_op jit(solution)/shard_map/pallas_call | solution.py:604
  21.1 3.1 %collective-permute-start.3 = (bf16[832,256]{1,0:T(8,128)(2,1)S(1)}, bf16[832,256]{1,0:T(8,128)(2,1)S(1)}, u32[]{:S(2)}, u32[]{:S(2)}) collective-permute-start(bf16[832,256]{1,0:T(8,128)(2,1)S(1)} %get-tuple-element.57), channel_id=1, source_target_pairs={{0,32},{32,0},{64,96},{96,64},{128,160},{160,128},{192,224},{224,1... | collective-permute-start | bytes 1277960 | tf_op jit(solution)/shard_map/ppermute | solution.py:40
  24.2 4.8 %collective-permute-start.2 = (bf16[832,256]{1,0:T(8,128)(2,1)S(1)}, bf16[832,256]{1,0:T(8,128)(2,1)S(1)}, u32[]{:S(2)}, u32[]{:S(2)}) collective-permute-start(bf16[832,256]{1,0:T(8,128)(2,1)S(1)} %get-tuple-element.55), channel_id=1, source_target_pairs={{0,480},{32,64},{64,32},{96,128},{128,96},{160,192},{192,160},{224... | collective-permute-start | bytes 1277960 | tf_op jit(solution)/shard_map/ppermute | solution.py:40
  29.0 0.0 collective-permute-done.3.got
  29.0 7.2 %shard_map.130 = (bf16[768,256]{1,0:T(8,128)(2,1)S(1)}, bf16[512,256]{1,0:T(8,128)(2,1)S(1)}, bf16[256,256]{1,0:T(8,128)(2,1)S(1)}, bf16[1024,256]{1,0:T(8,128)(...) custom-call(s32[4]{0:T(128)S(1)} %pad_add_fusion.ids, bf16[832,256]{1,0:T(8,128)(2,1)S(1)} %collective-permute-done.3.got, ...), custom_call_target="tpu_custom_call" | custom-call | flops 4000000000 | bytes 4000000 | tf_op jit(solution)/shard_map/pallas_call | solution.py:632
  36.2 1.0 %collective-permute-done.2.got = bf16[832,256]{1,0:T(8,128)(2,1)S(1)} collective-permute-done((bf16[832,256]{1,0:T(8,128)(2,1)S(1)}, bf16[832,256]{1,0:T(8,128)(2,1)S(1)}, u32[]{:S(2)}, u32[]{:S(2)}) %collective-permute-start.2) | collective-permute-done | bytes 426016 | tf_op jit(solution)/shard_map/ppermute | solution.py:40
  37.3 6.7 %shard_map.131 = f32[2,16,32]{2,1,0:T(8,128)} custom-call(s32[4]{0:T(128)S(1)} %pad_add_fusion.ids, bf16[832,256]{1,0:T(8,128)(2,1)S(1)} %collective-permute-done.2.got, bf16[1536,256]{1,0:T(8,128)(2,1)S(1)} %get-tuple-element.56.mid, bf16[768,256]{1,0:T(8,128)(2,1)S(1)} %get-tuple-element.69.outer, bf16[1024,256]{1,0:T(8,128)(2,1)S(1)} %get-tuple-element.70.near_b, ...), custom_call_target="tpu_custom_call" | custom-call | tf_op jit(solution)/shard_map/pallas_call | solution.py:651
  (14 shorter events, 0.0 us)
Async XLA Ops:
  0.0 16.8 %copy-start.13 = (f32[768]{0:T(1024)S(1)}, f32[768]{0:T(1024)}, u32[]{:S(2)}) copy-start(f32[768]{0:T(1024)} %param.18) | copy-start | bytes 9220
  0.0 16.9 %copy-start.14 = (bf16[256,2]{0,1:T(2,128)(2,1)S(1)}, bf16[256,2]{0,1:T(2,128)(2,1)}, u32[]{:S(2)}) copy-start(bf16[256,2]{0,1:T(2,128)(2,1)} %param.24) | copy-start | bytes 3076
  0.1 1.0 %copy-start = (bf16[16,32,256]{2,1,0:T(8,128)(2,1)S(1)}, bf16[16,32,256]{2,1,0:T(8,128)(2,1)}, u32[]{:S(2)}) copy-start(bf16[16,32,256]{2,1,0:T(8,128)(2,1)} %a_ref.3) | copy-start | bytes 786436
  1.0 0.9 %copy-start.2 = (bf16[16,32,256]{2,1,0:T(8,128)(2,1)S(1)}, bf16[16,32,256]{2,1,0:T(8,128)(2,1)}, u32[]{:S(2)}) copy-start(bf16[16,32,256]{2,1,0:T(8,128)(2,1)} %b_ref.3) | copy-start | bytes 786436
  2.0 15.1 %copy-start.4 = (bf16[256,768]{1,0:T(8,128)(2,1)S(1)}, bf16[256,768]{1,0:T(8,128)(2,1)}, u32[]{:S(2)}) copy-start(bf16[256,768]{1,0:T(8,128)(2,1)} %w_qkv.1) | copy-start | bytes 1179652
  2.0 15.1 %copy-start.5 = (bf16[289,256]{1,0:T(8,128)(2,1)S(1)}, bf16[289,256]{1,0:T(8,128)(2,1)}, u32[]{:S(2)}) copy-start(bf16[289,256]{1,0:T(8,128)(2,1)} %w_hid.1) | copy-start | bytes 443908
  2.6 17.6 %collective-permute-start = (bf16[16,16,256]{2,1,0:T(8,128)(2,1)S(1)}, bf16[16,16,256]{2,1,0:T(8,128)(2,1)S(1)}, u32[]{:S(2)}, u32[]{:S(2)}) collective-permute-start(bf16[16,16,256]{2,1,0:T(8,128)(2,1)S(1)} %get-tuple-element.40), channel_id=1, source_target_pairs={{0,1},{1,0},{2,3},{3,2},{4,5},{5,4},{6,7},{7,6},{8,9},{9,8},{10,11... | collective-permute-start | bytes 393224 | tf_op jit(solution)/shard_map/ppermute | solution.py:40
  5.8 14.4 %collective-permute-start.1 = (bf16[16,16,256]{2,1,0:T(8,128)(2,1)S(1)}, bf16[16,16,256]{2,1,0:T(8,128)(2,1)S(1)}, u32[]{:S(2)}, u32[]{:S(2)}) collective-permute-start(bf16[16,16,256]{2,1,0:T(8,128)(2,1)S(1)} %get-tuple-element.41), channel_id=1, source_target_pairs={{0,31},{1,2},{2,1},{3,4},{4,3},{5,6},{6,5},{7,8},{8,7},{9,10},{10,... | collective-permute-start | bytes 393224 | tf_op jit(solution)/shard_map/ppermute | solution.py:40
  16.9 0.7 %copy-start.9 = (f32[256]{0:T(256)S(1)}, f32[256]{0:T(256)}, u32[]{:S(2)}) copy-start(f32[256]{0:T(256)} %param.16) | copy-start | bytes 3076
  16.9 0.7 %copy-start.10 = (f32[256]{0:T(256)S(1)}, f32[256]{0:T(256)}, u32[]{:S(2)}) copy-start(f32[256]{0:T(256)} %param.21) | copy-start | bytes 3076
  16.9 0.7 %copy-start.11 = (f32[256]{0:T(256)S(1)}, f32[256]{0:T(256)}, u32[]{:S(2)}) copy-start(f32[256]{0:T(256)} %param.23) | copy-start | bytes 3076
  16.9 0.7 %copy-start.12 = (f32[2]{0:T(128)S(1)}, f32[2]{0:T(128)}, u32[]{:S(2)}) copy-start(f32[2]{0:T(128)} %param.25) | copy-start | bytes 28
  17.1 0.7 %copy-start.7 = (f32[8,225]{1,0:T(8,128)S(1)}, f32[8,225]{1,0:T(8,128)}, u32[]{:S(2)}) copy-start(f32[8,225]{1,0:T(8,128)} %rel.1) | copy-start | bytes 21604
  17.1 0.7 %copy-start.8 = (f32[256]{0:T(256)S(1)}, f32[256]{0:T(256)}, u32[]{:S(2)}) copy-start(f32[256]{0:T(256)} %param.15) | copy-start | bytes 3076
  17.8 0.9 %copy-start.6 = (bf16[256,256]{1,0:T(8,128)(2,1)S(1)}, bf16[256,256]{1,0:T(8,128)(2,1)}, u32[]{:S(2)}) copy-start(bf16[256,256]{1,0:T(8,128)(2,1)} %w_out.1) | copy-start | bytes 393220
  18.7 1.6 %copy-start.1 = (bf16[16,32,256]{2,1,0:T(8,128)(2,1)S(1)}, bf16[16,32,256]{2,1,0:T(8,128)(2,1)}, u32[]{:S(2)}) copy-start(bf16[16,32,256]{2,1,0:T(8,128)(2,1)} %a_ref.3) | copy-start | bytes 786436
  18.7 1.6 %copy-start.3 = (bf16[16,32,256]{2,1,0:T(8,128)(2,1)S(1)}, bf16[16,32,256]{2,1,0:T(8,128)(2,1)}, u32[]{:S(2)}) copy-start(bf16[16,32,256]{2,1,0:T(8,128)(2,1)} %b_ref.3) | copy-start | bytes 786436
  21.1 8.0 %collective-permute-start.3 = (bf16[832,256]{1,0:T(8,128)(2,1)S(1)}, bf16[832,256]{1,0:T(8,128)(2,1)S(1)}, u32[]{:S(2)}, u32[]{:S(2)}) collective-permute-start(bf16[832,256]{1,0:T(8,128)(2,1)S(1)} %get-tuple-element.57), channel_id=1, source_target_pairs={{0,32},{32,0},{64,96},{96,64},{128,160},{160,128},{192,224},{224,1... | collective-permute-start | bytes 1277960 | tf_op jit(solution)/shard_map/ppermute | solution.py:40
  24.2 13.1 %collective-permute-start.2 = (bf16[832,256]{1,0:T(8,128)(2,1)S(1)}, bf16[832,256]{1,0:T(8,128)(2,1)S(1)}, u32[]{:S(2)}, u32[]{:S(2)}) collective-permute-start(bf16[832,256]{1,0:T(8,128)(2,1)S(1)} %get-tuple-element.55), channel_id=1, source_target_pairs={{0,480},{32,64},{64,32},{96,128},{128,96},{160,192},{192,160},{224... | collective-permute-start | bytes 1277960 | tf_op jit(solution)/shard_map/ppermute | solution.py:40
